TPU v7x, 32 devices: a whole 2x2x4 slice. The times are simulated.
32 devices in a mesh: batch: 4 (over y, x), expert: 8 (over z, core).
Axes of the slice: x: 2, y: 2, z: 4, core: 2. Of those that a mesh axis runs over, the one named last changes fastest.
Arguments:
- tokens: bfloat16 [32768, 768], P(('batch', 'expert')), may hold values from -6 to 6
- cotangent: bfloat16 [32768, 768], P(('batch', 'expert')), may hold values from -6 to 6
- segment_ids: int32 [32, 1024], P(('batch', 'expert')), may hold values from 0 to 5, never falling along the last dimension, each value on 1 to 384 neighbouring positions
- routes: int32 [32768, 1], P(('batch', 'expert')), may hold values from 0 to 31, as said below
- capacity: int32 [32], replicated, may hold values from 32 to 64, as said below
- ln1_gain: bfloat16 [768], P(('batch', 'expert')), may hold values from 0.5 to 1.5
- ln1_bias: bfloat16 [768], P(('batch', 'expert')), may hold values from -1.25 to 1.25
- w_query: bfloat16 [768, 768], P(('batch', 'expert')), may hold values from -0.21875 to 0.21875
- b_query: bfloat16 [768], P(('batch', 'expert')), may hold values from -1.25 to 1.25
- w_key: bfloat16 [768, 768], P(('batch', 'expert')), may hold values from -0.21875 to 0.21875
- w_value: bfloat16 [768, 768], P(('batch', 'expert')), may hold values from -0.21875 to 0.21875
- b_value: bfloat16 [768], P(('batch', 'expert')), may hold values from -1.25 to 1.25
- w_output: bfloat16 [768, 768], P(('batch', 'expert')), may hold values from -1.25 to 1.25
- b_output: bfloat16 [768], P(('batch', 'expert')), may hold values from -1.25 to 1.25
- ln2_gain: bfloat16 [768], P(('batch', 'expert')), may hold values from 0.5 to 1.5
- ln2_bias: bfloat16 [768], P(('batch', 'expert')), may hold values from -1.25 to 1.25
- w_router: bfloat16 [768, 32], P(('batch', 'expert')), may hold values from -0.15625 to 0.15625
- w_in: bfloat16 [32, 768, 3072], P('expert', None, 'batch'), may hold values from -0.21875 to 0.21875
- b_in: bfloat16 [32, 3072], P('expert', 'batch'), may hold values from -0.625 to 0.625
- w_out: bfloat16 [32, 3072, 768], P('expert', 'batch'), may hold values from -3.5 to 3.5
- b_out: bfloat16 [32, 768], P(None, ('batch', 'expert')), may hold values from -12 to 12
Outputs:
- block_out: bfloat16 [32768, 768], P(('batch', 'expert'))
- balance_loss: float32 [], replicated
- expert_shares: float32 [2, 32], replicated
- input_grad: float32 [32768, 768], P(('batch', 'expert'))
- grad_ln1_gain: float32 [768], P(('batch', 'expert'))
- grad_ln1_bias: float32 [768], P(('batch', 'expert'))
- grad_w_query: float32 [768, 768], P(('batch', 'expert'))
- grad_b_query: float32 [768], P(('batch', 'expert'))
- grad_w_key: float32 [768, 768], P(('batch', 'expert'))
- grad_w_value: float32 [768, 768], P(('batch', 'expert'))
- grad_b_value: float32 [768], P(('batch', 'expert'))
- grad_w_output: float32 [768, 768], P(('batch', 'expert'))
- grad_b_output: float32 [768], P(('batch', 'expert'))
- grad_ln2_gain: float32 [768], P(('batch', 'expert'))
- grad_ln2_bias: float32 [768], P(('batch', 'expert'))
- grad_w_router: float32 [768, 32], P(('batch', 'expert'))
- grad_w_in: float32 [32, 768, 3072], P('expert', None, 'batch')
- grad_b_in: float32 [32, 3072], P('expert', 'batch')
- grad_w_out: float32 [32, 3072, 768], P('expert', 'batch')
- grad_b_out: float32 [32, 768], P(None, ('batch', 'expert'))
Inputs may be any that keep to these rules, and one draw needn't show every extreme that they name: `routes`: the rows of one device name each expert at most 64 times, and on every device some expert exactly 64 times; every expert is named by the rows of some device. Some expert has capacity 64. `segment_ids`: segment ids never fall along a packed row.
All inputs are finite; a program needn't handle non-finite values.
Results may differ from a plain program's by a relative error of at most 0.014.
Values may be sent and summed in bfloat16 or wider, within the bound.
No kernel may reach another device: no remote copies, remote signals or barrier semaphores. Data moves between devices by JAX's collectives and lax.ppermute only.
A program may use at most 384 MiB of HBM per device.

v0:
```python
import jax
import jax.numpy as jnp
from jax import lax
from jax.sharding import PartitionSpec as P

D = 768
HEADS = 12
HEAD = 64


epsilon = 1e-05
balance_weight = 0.01


def layer_norm(inputs, gain_vec, shift_vec):
    average = jnp.mean(inputs, axis=-1, keepdims=True)
    centred = inputs - average
    variance = jnp.mean(centred * centred, axis=-1, keepdims=True)
    return centred * lax.rsqrt(variance + epsilon) * gain_vec + shift_vec


def exact_gelu(inputs):
    return jax.nn.gelu(inputs, approximate=False)


def router_softmax(logits):
    return jax.nn.softmax(logits, axis=-1)


def contract_rows(left, right):
    return lax.dot_general(
        left, right, (((0,), (0,)), ((), ())), preferred_element_type=jnp.float32
    )


def times_transpose(left, right):
    return lax.dot_general(
        left, right, (((1,), (1,)), ((), ())), preferred_element_type=jnp.float32
    )


def masked_scores(queries, key_rows, segments):
    scores = jnp.einsum(
        "qhd,khd->hqk", queries, key_rows, preferred_element_type=jnp.float32
    ) * HEAD ** (-0.5)
    position = jnp.arange(segments.shape[0])
    visible = (position[None, :] <= position[:, None]) & (segments[None, :] == segments[:, None])
    return jnp.where(visible[None], scores, -1e30)


def attend_forward(items):
    queries, key_rows, values, segments = items
    scores = masked_scores(queries, key_rows, segments)
    largest = jnp.max(scores, axis=-1, keepdims=True)
    exponent = jnp.exp(scores - largest)
    totals = jnp.sum(exponent, axis=-1, keepdims=True)
    attn_probs = (exponent / totals).astype(jnp.bfloat16)
    attended = jnp.einsum("hqk,khd->qhd", attn_probs, values, preferred_element_type=jnp.float32)
    return (attended.astype(jnp.bfloat16), largest + jnp.log(totals))


def attend_backward(items):
    queries, key_rows, values, segments, log_total, grad_att = items
    scores = masked_scores(queries, key_rows, segments)
    attn_probs = jnp.exp(scores - log_total)
    low_probs = attn_probs.astype(jnp.bfloat16)
    grad_values = jnp.einsum(
        "hqk,qhd->khd", low_probs, grad_att, preferred_element_type=jnp.float32
    )
    grad_probs = jnp.einsum("qhd,khd->hqk", grad_att, values, preferred_element_type=jnp.float32)
    centre = jnp.sum(grad_probs * attn_probs, axis=-1, keepdims=True)
    grad_scores = (attn_probs * (grad_probs - centre)).astype(jnp.bfloat16)
    grad_queries = jnp.einsum(
        "hqk,khd->qhd", grad_scores, key_rows, preferred_element_type=jnp.float32
    ) * HEAD ** (-0.5)
    grad_keys = jnp.einsum(
        "hqk,qhd->khd", grad_scores, queries, preferred_element_type=jnp.float32
    ) * HEAD ** (-0.5)
    return (grad_queries, grad_keys, grad_values)


def local(
    tokens,
    cotangent,
    segment_ids,
    routes,
    capacity,
    ln1_gain,
    ln1_bias,
    w_query,
    b_query,
    w_key,
    w_value,
    b_value,
    w_output,
    b_output,
    ln2_gain,
    ln2_bias,
    w_router,
    w_in,
    b_in,
    w_out,
    b_out,
):
    row_count = tokens.shape[0]
    seq_count, length = segment_ids.shape
    experts = capacity.shape[0]
    slots = 2 * row_count // experts
    local_groups = w_in.shape[0]
    owner_count = lax.axis_size("expert")
    split_count = local_groups * owner_count // experts
    group_total = experts * split_count
    (
        gain_one,
        shift_one,
        full_query,
        bias_query,
        full_key,
        full_value,
        bias_value,
        full_output,
        bias_output,
        gain_two,
        shift_two,
        full_router,
        bias_expert,
    ) = (
        lax.all_gather(ln1_gain, ("batch", "expert"), axis=0, tiled=True),
        lax.all_gather(ln1_bias, ("batch", "expert"), axis=0, tiled=True),
        lax.all_gather(w_query, ("batch", "expert"), axis=0, tiled=True),
        lax.all_gather(b_query, ("batch", "expert"), axis=0, tiled=True),
        lax.all_gather(w_key, ("batch", "expert"), axis=0, tiled=True),
        lax.all_gather(w_value, ("batch", "expert"), axis=0, tiled=True),
        lax.all_gather(b_value, ("batch", "expert"), axis=0, tiled=True),
        lax.all_gather(w_output, ("batch", "expert"), axis=0, tiled=True),
        lax.all_gather(b_output, ("batch", "expert"), axis=0, tiled=True),
        lax.all_gather(ln2_gain, ("batch", "expert"), axis=0, tiled=True),
        lax.all_gather(ln2_bias, ("batch", "expert"), axis=0, tiled=True),
        lax.all_gather(w_router, ("batch", "expert"), axis=0, tiled=True),
        lax.all_gather(b_out, ("batch", "expert"), axis=1, tiled=True),
    )
    inputs = tokens.astype(jnp.float32)
    normed_one, norm_one_pull = jax.vjp(
        layer_norm, inputs, gain_one.astype(jnp.float32), shift_one.astype(jnp.float32)
    )
    h_one = normed_one.astype(jnp.bfloat16)
    queries = (
        jnp.dot(h_one, full_query, preferred_element_type=jnp.float32)
        + bias_query.astype(jnp.float32)
    ).astype(jnp.bfloat16)
    key_rows = jnp.dot(h_one, full_key, preferred_element_type=jnp.float32).astype(jnp.bfloat16)
    values = (
        jnp.dot(h_one, full_value, preferred_element_type=jnp.float32)
        + bias_value.astype(jnp.float32)
    ).astype(jnp.bfloat16)
    head_shape = (seq_count, length, HEADS, HEAD)
    query_heads = queries.reshape(head_shape)
    key_heads = key_rows.reshape(head_shape)
    value_heads = values.reshape(head_shape)
    attended, log_total = lax.map(
        attend_forward, (query_heads, key_heads, value_heads, segment_ids)
    )
    attended = attended.reshape(row_count, D)
    resid = (
        inputs
        + jnp.dot(attended, full_output, preferred_element_type=jnp.float32)
        + bias_output.astype(jnp.float32)
    )
    normed_two, norm_two_pull = jax.vjp(
        layer_norm, resid, gain_two.astype(jnp.float32), shift_two.astype(jnp.float32)
    )
    h_two = normed_two.astype(jnp.bfloat16)
    logits = jnp.dot(h_two, full_router, preferred_element_type=jnp.float32)
    router_probs, softmax_pull = jax.vjp(router_softmax, logits)
    chosen = routes[:, 0]
    picked = chosen[:, None] == jnp.arange(experts, dtype=jnp.int32)[None, :]
    picked_float = picked.astype(jnp.float32)
    picked_int = picked.astype(jnp.int32)
    gate_prob = jnp.sum(router_probs * picked_float, axis=1)
    rank = jnp.cumsum(picked_int, axis=0) - picked_int
    slot_index = jnp.sum(rank * picked_int, axis=1)
    limit = jnp.sum(capacity[None, :] * picked_int, axis=1)
    kept_mask = slot_index < limit
    kept_float = kept_mask.astype(jnp.float32)
    target = jnp.where(kept_mask, slot_index, slots)
    lookup = jnp.minimum(slot_index, slots - 1)
    group_of = chosen[:, None] * split_count + jnp.arange(split_count, dtype=jnp.int32)[None, :]
    counts, prob_sums = lax.psum(
        (jnp.sum(picked_float, axis=0), jnp.sum(router_probs, axis=0)), ("batch", "expert")
    )
    token_total = float(row_count * lax.axis_size("batch") * lax.axis_size("expert"))
    fraction = counts / token_total
    mean_probs = prob_sums / token_total
    balance_loss = experts * jnp.sum(fraction * mean_probs)
    expert_shares = jnp.stack([experts * fraction, experts * mean_probs])
    copies = jnp.broadcast_to(h_two[:, None, :], (row_count, split_count, D))
    send_rows = (
        jnp.zeros((group_total, slots, D), jnp.bfloat16)
        .at[group_of, target[:, None]]
        .set(copies, mode="drop")
    )
    received = lax.all_to_all(send_rows, "expert", split_axis=0, concat_axis=0, tiled=True).reshape(
        owner_count, local_groups, slots, D
    )
    whole_in, whole_out, whole_bin = (
        lax.all_gather(w_in, "batch", axis=2, tiled=True),
        lax.all_gather(w_out, "batch", axis=1, tiled=True),
        lax.all_gather(b_in, "batch", axis=1, tiled=True),
    )
    preact = (
        jnp.einsum("slcd,ldf->slcf", received, whole_in, preferred_element_type=jnp.float32)
        + whole_bin.astype(jnp.float32)[None, :, None, :]
    )
    hidden, gelu_pull = jax.vjp(exact_gelu, preact)
    hidden_low = hidden.astype(jnp.bfloat16)
    piece_out = jnp.einsum(
        "slcf,lfd->slcd", hidden_low, whole_out, preferred_element_type=jnp.float32
    ).astype(jnp.bfloat16)
    returned = lax.all_to_all(
        piece_out.reshape(group_total, slots, D), "expert", split_axis=0, concat_axis=0, tiled=True
    )
    fetched = jnp.sum(returned[group_of, lookup[:, None]].astype(jnp.float32), axis=1)
    expert_bias = jnp.dot(
        picked.astype(jnp.bfloat16), bias_expert, preferred_element_type=jnp.float32
    )
    expert_out = fetched + expert_bias
    mixing = kept_float * gate_prob
    block_out = resid + mixing[:, None] * expert_out
    grad_out = cotangent.astype(jnp.float32)
    grad_gate = kept_float * jnp.sum(grad_out * expert_out, axis=1)
    grad_bias_expert = lax.dot_general(
        picked_float * mixing[:, None],
        grad_out,
        (((0,), (0,)), ((), ())),
        precision=lax.Precision.HIGHEST,
        preferred_element_type=jnp.float32,
    )
    grad_made = (mixing[:, None] * grad_out).astype(jnp.bfloat16)
    grad_copies = jnp.broadcast_to(grad_made[:, None, :], (row_count, split_count, D))
    grad_send = (
        jnp.zeros((group_total, slots, D), jnp.bfloat16)
        .at[group_of, target[:, None]]
        .set(grad_copies, mode="drop")
    )
    grad_expert = lax.all_to_all(
        grad_send, "expert", split_axis=0, concat_axis=0, tiled=True
    ).reshape(owner_count, local_groups, slots, D)
    grad_wout_term = jnp.einsum(
        "slcf,slcd->lfd", hidden_low, grad_expert, preferred_element_type=jnp.float32
    )
    grad_hidden = jnp.einsum(
        "slcd,lfd->slcf", grad_expert, whole_out, preferred_element_type=jnp.float32
    )
    grad_pre = gelu_pull(grad_hidden)[0].astype(jnp.bfloat16)
    grad_bin_term = jnp.sum(grad_pre.astype(jnp.float32), axis=(0, 2))
    grad_win_term = jnp.einsum(
        "slcd,slcf->ldf", received, grad_pre, preferred_element_type=jnp.float32
    )
    grad_received = jnp.einsum(
        "slcf,ldf->slcd", grad_pre, whole_in, preferred_element_type=jnp.float32
    ).astype(jnp.bfloat16)
    grad_w_in, grad_w_out, grad_b_in = (
        lax.psum_scatter(
            grad_win_term.astype(jnp.bfloat16), "batch", scatter_dimension=2, tiled=True
        ).astype(jnp.float32),
        lax.psum_scatter(
            grad_wout_term.astype(jnp.bfloat16), "batch", scatter_dimension=1, tiled=True
        ).astype(jnp.float32),
        lax.psum_scatter(
            grad_bin_term.astype(jnp.bfloat16), "batch", scatter_dimension=1, tiled=True
        ).astype(jnp.float32),
    )
    grad_back = lax.all_to_all(
        grad_received.reshape(group_total, slots, D),
        "expert",
        split_axis=0,
        concat_axis=0,
        tiled=True,
    )
    grad_h_expert = (
        jnp.sum(grad_back[group_of, lookup[:, None]].astype(jnp.float32), axis=1)
        * kept_float[:, None]
    )
    grad_probs = (
        picked_float * grad_gate[:, None]
        + balance_weight * experts * fraction[None, :] / token_total
    )
    grad_logits = softmax_pull(grad_probs)[0].astype(jnp.bfloat16)
    grad_router = contract_rows(h_two, grad_logits)
    grad_h_two = times_transpose(grad_logits, full_router) + grad_h_expert
    grad_resid_norm, grad_gain_two, grad_shift_two = norm_two_pull(grad_h_two)
    grad_resid = grad_out + grad_resid_norm
    grad_branch = grad_resid.astype(jnp.bfloat16)
    grad_bias_output = jnp.sum(grad_branch.astype(jnp.float32), axis=0)
    grad_output = contract_rows(attended, grad_branch)
    grad_att = times_transpose(grad_branch, full_output).astype(jnp.bfloat16)
    grad_q, grad_k, grad_v = lax.map(
        attend_backward,
        (query_heads, key_heads, value_heads, segment_ids, log_total, grad_att.reshape(head_shape)),
    )
    grad_q = grad_q.reshape(row_count, D).astype(jnp.bfloat16)
    grad_k = grad_k.reshape(row_count, D).astype(jnp.bfloat16)
    grad_v = grad_v.reshape(row_count, D).astype(jnp.bfloat16)
    grad_query = contract_rows(h_one, grad_q)
    grad_bias_query = jnp.sum(grad_q.astype(jnp.float32), axis=0)
    grad_key = contract_rows(h_one, grad_k)
    grad_value = contract_rows(h_one, grad_v)
    grad_bias_value = jnp.sum(grad_v.astype(jnp.float32), axis=0)
    grad_h_one = (
        times_transpose(grad_q, full_query)
        + times_transpose(grad_k, full_key)
        + times_transpose(grad_v, full_value)
    )
    grad_input_norm, grad_gain_one, grad_shift_one = norm_one_pull(grad_h_one)
    input_grad = grad_resid + grad_input_norm
    summed_grads = (
        lax.psum_scatter(grad_gain_one, ("batch", "expert"), scatter_dimension=0, tiled=True),
        lax.psum_scatter(grad_shift_one, ("batch", "expert"), scatter_dimension=0, tiled=True),
        lax.psum_scatter(grad_query, ("batch", "expert"), scatter_dimension=0, tiled=True),
        lax.psum_scatter(grad_bias_query, ("batch", "expert"), scatter_dimension=0, tiled=True),
        lax.psum_scatter(grad_key, ("batch", "expert"), scatter_dimension=0, tiled=True),
        lax.psum_scatter(grad_value, ("batch", "expert"), scatter_dimension=0, tiled=True),
        lax.psum_scatter(grad_bias_value, ("batch", "expert"), scatter_dimension=0, tiled=True),
        lax.psum_scatter(grad_output, ("batch", "expert"), scatter_dimension=0, tiled=True),
        lax.psum_scatter(grad_bias_output, ("batch", "expert"), scatter_dimension=0, tiled=True),
        lax.psum_scatter(grad_gain_two, ("batch", "expert"), scatter_dimension=0, tiled=True),
        lax.psum_scatter(grad_shift_two, ("batch", "expert"), scatter_dimension=0, tiled=True),
        lax.psum_scatter(grad_router, ("batch", "expert"), scatter_dimension=0, tiled=True),
        lax.psum_scatter(grad_bias_expert, ("batch", "expert"), scatter_dimension=1, tiled=True),
    )
    return (
        block_out.astype(jnp.bfloat16),
        balance_loss,
        expert_shares,
        input_grad,
        summed_grads[0],
        summed_grads[1],
        summed_grads[2],
        summed_grads[3],
        summed_grads[4],
        summed_grads[5],
        summed_grads[6],
        summed_grads[7],
        summed_grads[8],
        summed_grads[9],
        summed_grads[10],
        summed_grads[11],
        grad_w_in,
        grad_b_in,
        grad_w_out,
        summed_grads[12],
    )


def solution(mesh):
    placed = (
        P(("batch", "expert"), None),
        P(("batch", "expert"), None),
        P(("batch", "expert"), None),
        P(("batch", "expert"), None),
        P(),
        P(("batch", "expert")),
        P(("batch", "expert")),
        P(("batch", "expert"), None),
        P(("batch", "expert")),
        P(("batch", "expert"), None),
        P(("batch", "expert"), None),
        P(("batch", "expert")),
        P(("batch", "expert"), None),
        P(("batch", "expert")),
        P(("batch", "expert")),
        P(("batch", "expert")),
        P(("batch", "expert"), None),
        P("expert", None, "batch"),
        P("expert", "batch"),
        P("expert", "batch", None),
        P(None, ("batch", "expert")),
    )
    return jax.shard_map(
        local,
        mesh=mesh,
        in_specs=placed,
        out_specs=(
            P(("batch", "expert"), None),
            P(),
            P(),
            P(("batch", "expert"), None),
            P(("batch", "expert")),
            P(("batch", "expert")),
            P(("batch", "expert"), None),
            P(("batch", "expert")),
            P(("batch", "expert"), None),
            P(("batch", "expert"), None),
            P(("batch", "expert")),
            P(("batch", "expert"), None),
            P(("batch", "expert")),
            P(("batch", "expert")),
            P(("batch", "expert")),
            P(("batch", "expert"), None),
            P("expert", None, "batch"),
            P("expert", "batch"),
            P("expert", "batch", None),
            P(None, ("batch", "expert")),
        ),
        check_vma=False,
    )
```

profile of v0, /device:TPU:0, one launch (start us, length us, event | category | flops | bytes accessed | tf_op | source)
XLA Modules:
  0.0 1926.0 jit_solution(233971645545646418)
XLA Ops:
  12.9 42.5 %all-reduce.17 = (bf16[768]{0:T(1024)(128)(2,1)S(1)}, bf16[768]{0:T(1024)(128)(2,1)S(1)}, bf16[768]{0:T(1024)(128)(2,1)S(1)}, bf16[768]{0:T(1024)(128)(2,1)S(1)}...) all-reduce(bf16[768]{0:T(1024)(128)(2,1)S(1)} %dynamic-update-slice, ...), channel_id=1, replica_groups=mesh['batch'=4,'expert'=8] {'batch','expert'}, use_global_device_ids=true, to_apply=%add.2 | all-reduce | flops 5376 | bytes 21504
  73.9 50.3 %all-gather.9.cloned.1.call-done = bf16[768,768]{1,0:T(8,128)(2,1)} async-done(((bf16[24,768]{1,0:T(8,128)(2,1)}), bf16[768,768]{1,0:T(8,128)(2,1)}) %all-gather.9.cloned.1.call-update) | async-done | bytes 1179664 | tf_op jit(solution)/shard_map/all_gather | solution.py:130
  128.2 21.5 %fusion.36 = (f32[12,1024]{1,0:T(8,128)S(1)}, f32[12,1024,1024]{1,2,0:T(8,128)}) fusion(pred[1024,1024]{0,1:T(8,128)(4,1)S(1)} %fusion.44, bf16[1024,12,64]{0,2,1:T(8,128)(2,1)} %bitcast.215, bf16[1024,12,64]{0,2,1:T(8,128)(2,1)} %bitcast.217), kind=kOutput, calls=%fused_computation.56 | convolution fusion | flops 1648349184 | bytes 54575104 | tf_op jit(solution)/shard_map/while/body/eval_jaxpr/qhd,khd->hqk/dot_general | solution.py:43
  205.9 30.6 %all-gather.13.cloned.1.call-done = bf16[768,768]{1,0:T(8,128)(2,1)} async-done(((bf16[24,768]{1,0:T(8,128)(2,1)}), bf16[768,768]{1,0:T(8,128)(2,1)}) %all-gather.13.cloned.1.call-update) | async-done | bytes 1179664 | tf_op jit(solution)/shard_map/all_gather | solution.py:135
  263.3 63.1 %all-to-all-done = bf16[32,64,768]{2,1,0:T(8,128)(2,1)S(1)} async-done(((bf16[32,64,768]{2,1,0:T(8,128)(2,1)}), bf16[32,64,768]{2,1,0:T(8,128)(2,1)S(1)}, u32[]{:S(2)}, u32[]{:S(2)}) %all-to-all-start) | async-done | bytes 3145760 | tf_op jit(solution)/shard_map/all_to_all | solution.py:202
  326.5 86.8 %all-gather.15.cloned.1.call-done = bf16[4,768,3072]{2,1,0:T(8,128)(2,1)} async-done(((bf16[4,768,768]{2,1,0:T(8,128)(2,1)}), bf16[4,768,3072]{2,1,0:T(8,128)(2,1)}) %all-gather.15.cloned.1.call-update) | async-done | bytes 18874384 | tf_op jit(solution)/shard_map/all_gather | solution.py:206
  413.3 66.0 %fusion.13 = (bf16[8,4,64,3072]{3,2,0,1:T(8,128)(2,1)}, f32[8,4,64,3072]{3,2,0,1:T(8,128)}, f32[4,8,64,3072]{3,2,1,0:T(8,128)}) fusion(f32[4,3072]{1,0:T(4,128)S(1)} %convert_element_type.212, bf16[4,768,3072]{2,1,0:T(8,128)(2,1)} %all-gather.15.cloned.1.call-done, bf16[8,4,64,768]{3,2,1,0:T(8,128)(2,1)S(1)} %bitcast.219), kind=kOutput, calls=%fused_computation.32 | convolution fusion | flops 10078912512 | bytes 84983808 | tf_op jit(solution)/shard_map/slcd,ldf->slcf/dot_general | solution.py:211
  479.2 111.3 %all-gather.17.cloned.1.call-done = bf16[4,3072,768]{2,1,0:T(8,128)(2,1)} async-done(((bf16[4,768,768]{2,1,0:T(8,128)(2,1)}), bf16[4,3072,768]{2,1,0:T(8,128)(2,1)}) %all-gather.17.cloned.1.call-update) | async-done | bytes 18874384 | tf_op jit(solution)/shard_map/all_gather | solution.py:207
  615.8 90.7 %psum.14 = f32[32]{0:T(128)S(1)} all-reduce(f32[32]{0:T(128)S(1)} %convert_reduce_fusion.4), channel_id=1, replica_groups=mesh['batch'=4,'expert'=8] {'batch','expert'}, use_global_device_ids=true, to_apply=%region_15.16 | all-reduce | flops 32 | bytes 256 | tf_op jit(solution)/shard_map/psum | solution.py:188
  709.0 42.1 %all_gather.59 = bf16[768,32]{1,0:T(8,128)(2,1)S(1)} all-gather(bf16[24,32]{1,0:T(8,128)(2,1)S(1)} %copy-done.64), channel_id=1, replica_groups=mesh['batch'=4,'expert'=8] {'batch','expert'}, dimensions={0}, use_global_device_ids=true | all-gather | bytes 50688 | tf_op jit(solution)/shard_map/all_gather | solution.py:139
  751.1 37.6 %all_gather.63 = bf16[32,768]{0,1:T(8,128)(2,1)S(1)} all-gather(bf16[32,24]{0,1:T(8,128)(2,1)S(1)} %copy-done.65), channel_id=1, replica_groups=mesh['batch'=4,'expert'=8] {'batch','expert'}, dimensions={1}, use_global_device_ids=true | all-gather | bytes 50688 | tf_op jit(solution)/shard_map/all_gather | solution.py:140
  820.3 74.7 %all_to_all.20 = bf16[32,64,768]{2,1,0:T(8,128)(2,1)} all-to-all(bf16[32,64,768]{2,1,0:T(8,128)(2,1)S(1)} %bitcast.214), channel_id=1, replica_groups=mesh['batch'=4,'expert'=8] {'expert'}, dimensions={0} | all-to-all | bytes 6291456 | tf_op jit(solution)/shard_map/all_to_all | solution.py:245
  895.0 31.1 %fusion.116 = (bf16[4,3072]{1,0:T(4,128)(2,1)S(1)}, bf16[8,4,64,3072]{3,2,0,1:T(8,128)(2,1)}) fusion(f32[8,4,64,3072]{3,2,0,1:T(8,128)} %get-tuple-element.165, bf16[4,3072,768]{2,1,0:T(8,128)(2,1)} %all-gather.17.cloned.1.call-done, bf16[8,4,64,768]{3,2,1,0:T(8,128)(2,1)} %bitcast.221, f32[4,8,64,3072]{3,2,1,0:T(8,128)} %get-tuple-element.179, ...), kind=kOutput, calls=%fused_computation.188 | convolution fusion | flops 9764327424 | bytes 85008384 | tf_op jit(solution)/shard_map/slcd,lfd->slcf/dot_general | solution.py:251
  998.3 64.2 %all-to-all-done.3 = bf16[32,64,768]{2,1,0:T(8,128)(2,1)S(1)} async-done(((bf16[32,64,768]{2,1,0:T(8,128)(2,1)}), bf16[32,64,768]{2,1,0:T(8,128)(2,1)S(1)}, u32[]{:S(2)}, u32[]{:S(2)}) %all-to-all-start.3) | async-done | bytes 3145760 | tf_op jit(solution)/shard_map/all_to_all | solution.py:273
  1090.0 21.6 %convert_reduce_fusion.2 = (f32[12,64]{1,0:T(8,128)S(1)}, bf16[12,64,1024]{2,1,0:T(8,128)(2,1)S(1)}) fusion(bf16[1024,12,64]{0,2,1:T(8,128)(2,1)S(1)} %bitcast.232, f32[12,1024]{1,0:T(8,128)S(1)} %log_add_fusion, f32[12,1024,1024]{1,2,0:T(8,128)} %get-tuple-element.176, pred[1024,1024]{0,1:T(8,128)(4,1)S(1)} %copy-done.5), kind=kOutput, calls=%fused_computation.88 | convolution fusion | flops 1663302912 | bytes 54578176 | tf_op jit(solution)/shard_map/while/body/eval_jaxpr/hqk,qhd->khd/dot_general | solution.py:67
  1120.9 35.1 %multiply_reduce_fusion = (f32[12,1024]{1,0:T(8,128)S(1)}, f32[12,1024,1024]{1,2,0:T(8,128)}) fusion(f32[12,1024]{1,0:T(8,128)S(1)} %log_add_fusion, f32[12,1024,1024]{1,2,0:T(8,128)} %get-tuple-element.176, pred[1024,1024]{0,1:T(8,128)(4,1)S(1)} %copy-done.5, bf16[1024,12,64]{0,2,1:T(8,128)(2,1)} %bitcast.233, bf16[1024,12,64]{0,2,1:T(8,128)(2,1)} %bitcast.229), kind=kOutput, calls=%fused_computation.5 | convolution fusion | flops 1673515008 | bytes 104955904 | tf_op jit(solution)/shard_map/while/body/eval_jaxpr/qhd,khd->hqk/dot_general | solution.py:70
  1156.1 43.6 %multiply_convert_fusion = bf16[12,1024,1024]{1,2,0:T(8,128)(2,1)} fusion(f32[12,1024,1024]{1,2,0:T(8,128)} %get-tuple-element.186, f32[12,1024]{1,0:T(8,128)S(1)} %get-tuple-element.185, f32[12,1024]{1,0:T(8,128)S(1)} %log_add_fusion, f32[12,1024,1024]{1,2,0:T(8,128)} %get-tuple-element.176, pred[1024,1024]{0,1:T(8,128)(4,1)S(1)} %copy-done.5), kind=kLoop, calls=%fused_computation.4 | loop fusion | flops 75497472 | bytes 126976000 | tf_op jit(solution)/shard_map/while/body/eval_jaxpr/convert_element_type | solution.py:72
  1248.6 38.3 %all-reduce.16 = (f32[32]{0:T(128)S(1)}, f32[768]{0:T(1024)S(1)}, f32[768]{0:T(1024)S(1)}, f32[768]{0:T(1024)S(1)}, f32[768]{0:T(1024)S(1)}, /*index=5*/f32[768]{0:T(1024)S(1)}, f32[768]{0:T(1024)S(1)}, f32[768]{0:T(1024)S(1)}) all-reduce(f32[32]{0:T(128)S(1)} %copy-done.73, ...), channel_id=1, replica_groups=mesh['batch'=4,'expert'=8] {'batch','expert'}, use_global_device_ids=true, to_apply=%region_17.18 | all-reduce | flops 5408 | bytes 43264 | tf_op jit(solution)/shard_map/psum | solution.py:188
  1318.9 81.6 %reduce-scatter.30.cloned.1.call-done = f32[24,32]{1,0:T(8,128)} async-done(((f32[768,32]{1,0:T(8,128)}), f32[24,32]{1,0:T(8,128)}) %reduce-scatter.30.cloned.1.call-update) | async-done | bytes 3088
  1400.5 100.3 %reduce-scatter.32.cloned.1.call-done = f32[32,24]{0,1:T(8,128)} async-done(((f32[32,768]{0,1:T(8,128)}), f32[32,24]{0,1:T(8,128)}) %reduce-scatter.32.cloned.1.call-update) | async-done | bytes 3088
  1500.8 103.9 %reduce-scatter.22.cloned.1.call-done = f32[24,768]{1,0:T(8,128)} async-done(((f32[768,768]{1,0:T(8,128)}), f32[24,768]{1,0:T(8,128)}) %reduce-scatter.22.cloned.1.call-update) | async-done | bytes 73744 | tf_op jit(solution)/shard_map/reduce_scatter | solution.py:324
  1604.7 104.8 %reduce-scatter.20.cloned.1.call-done = f32[24,768]{1,0:T(8,128)} async-done(((f32[768,768]{1,0:T(8,128)}), f32[24,768]{1,0:T(8,128)}) %reduce-scatter.20.cloned.1.call-update) | async-done | bytes 73744 | tf_op jit(solution)/shard_map/reduce_scatter | solution.py:322
  1709.5 103.8 %reduce-scatter.16.cloned.1.call-done = f32[24,768]{1,0:T(8,128)} async-done(((f32[768,768]{1,0:T(8,128)}), f32[24,768]{1,0:T(8,128)}) %reduce-scatter.16.cloned.1.call-update) | async-done | bytes 73744 | tf_op jit(solution)/shard_map/reduce_scatter | solution.py:319
  1813.3 104.6 %reduce-scatter.18.cloned.1.call-done = f32[24,768]{1,0:T(8,128)} async-done(((f32[768,768]{1,0:T(8,128)}), f32[24,768]{1,0:T(8,128)}) %reduce-scatter.18.cloned.1.call-update) | async-done | bytes 73744 | tf_op jit(solution)/shard_map/reduce_scatter | solution.py:321
  (342 shorter events, 358.6 us)
Async XLA Ops:
  7.2 62.7 %all-gather.11.cloned.1.call-start = ((), (), s32[]{:S(2)}) async-start(), calls=%async_computation.15 | async-start | bytes 1216512 | tf_op jit(solution)/shard_map/all_gather | solution.py:132
  7.9 116.3 %all-gather.9.cloned.1.call-start = ((), (), s32[]{:S(2)}) async-start(), calls=%async_computation.14 | async-start | bytes 1216512 | tf_op jit(solution)/shard_map/all_gather | solution.py:130
  8.7 171.7 %all-gather.7.cloned.1.call-start = ((), (), s32[]{:S(2)}) async-start(), calls=%async_computation.13 | async-start | bytes 1216512 | tf_op jit(solution)/shard_map/all_gather | solution.py:133
  9.4 227.0 %all-gather.13.cloned.1.call-start = ((), (), s32[]{:S(2)}) async-start(), calls=%async_computation.16 | async-start | bytes 1216512 | tf_op jit(solution)/shard_map/all_gather | solution.py:135
  10.0 403.3 %all-gather.15.cloned.1.call-start = ((), (), s32[]{:S(2)}) async-start(), calls=%async_computation.17 | async-start | bytes 23592960 | tf_op jit(solution)/shard_map/all_gather | solution.py:206
  10.7 579.8 %all-gather.17.cloned.1.call-start = ((), (), s32[]{:S(2)}) async-start(), calls=%async_computation.18 | async-start | bytes 23592960 | tf_op jit(solution)/shard_map/all_gather | solution.py:207
  55.5 185.7 %copy-start.56 = (f32[768]{0:T(1024)}, f32[768]{0:T(1024)S(1)}, u32[]{:S(2)}) copy-start(f32[768]{0:T(1024)S(1)} %convert_element_type.209) | copy-start | bytes 9220
  251.2 75.3 %all-to-all-start = ((bf16[32,64,768]{2,1,0:T(8,128)(2,1)}), bf16[32,64,768]{2,1,0:T(8,128)(2,1)S(1)}, u32[]{:S(2)}, u32[]{:S(2)}) async-start(bf16[32,64,768]{2,1,0:T(8,128)(2,1)} %bitcast.213), calls=%async_computation | async-start | bytes 6291456 | tf_op jit(solution)/shard_map/all_to_all | solution.py:202
  610.8 181.1 %all-to-all-start.1 = ((bf16[32,64,768]{2,1,0:T(8,128)(2,1)}), bf16[32,64,768]{2,1,0:T(8,128)(2,1)S(1)}, u32[]{:S(2)}, u32[]{:S(2)}) async-start(bf16[32,64,768]{2,1,0:T(8,128)(2,1)} %bitcast.212), calls=%async_computation.1 | async-start | bytes 6291456 | tf_op jit(solution)/shard_map/all_to_all | solution.py:219
  615.6 173.7 %copy-start.53 = (s32[1024]{0:T(1024)S(1)}, s32[1024]{0:T(1024)}, u32[]{:S(2)}) copy-start(s32[1024]{0:T(1024)} %copy-done.52) | copy-start | bytes 12292
  615.6 173.7 %copy-start.55 = (s32[1024]{0:T(1024)S(1)}, s32[1024]{0:T(1024)}, u32[]{:S(2)}) copy-start(s32[1024]{0:T(1024)} %copy-done.54) | copy-start | bytes 12292
  615.6 602.8 %reduce-scatter.28.cloned.1.call-start = ((), (), s32[]{:S(2)}) async-start(), calls=%async_computation.25 | async-start | bytes 983040
  791.8 199.4 %copy-start.46 = (f32[1024]{0:T(1024)}, f32[1024]{0:T(1024)S(1)}, u32[]{:S(2)}) copy-start(f32[1024]{0:T(1024)S(1)} %get-tuple-element.180) | copy-start | bytes 12292
  791.8 199.4 %copy-start.51 = (f32[1024]{0:T(1024)}, f32[1024]{0:T(1024)S(1)}, u32[]{:S(2)}) copy-start(f32[1024]{0:T(1024)S(1)} %fusion.81) | copy-start | bytes 12292
  810.0 181.2 %copy-start.62 = (f32[1024]{0:T(1024)}, f32[1024]{0:T(1024)S(1)}, u32[]{:S(2)}) copy-start(f32[1024]{0:T(1024)S(1)} %broadcast_select_fusion.1) | copy-start | bytes 12292
  927.4 377.7 %reduce-scatter.26.cloned.1.call-start = ((), (), s32[]{:S(2)}) async-start(), calls=%async_computation.24 | async-start | bytes 23592960 | tf_op jit(solution)/shard_map/reduce_scatter | solution.py:266
  948.2 363.8 %reduce-scatter.24.cloned.1.call-start = ((), (), s32[]{:S(2)}) async-start(), calls=%async_computation.23 | async-start | bytes 23592960 | tf_op jit(solution)/shard_map/reduce_scatter | solution.py:263
  987.2 75.3 %all-to-all-start.3 = ((bf16[32,64,768]{2,1,0:T(8,128)(2,1)}), bf16[32,64,768]{2,1,0:T(8,128)(2,1)S(1)}, u32[]{:S(2)}, u32[]{:S(2)}) async-start(bf16[32,64,768]{2,1,0:T(8,128)(2,1)} %bitcast.211), calls=%async_computation.3 | async-start | bytes 6291456 | tf_op jit(solution)/shard_map/all_to_all | solution.py:273
  991.1 409.4 %reduce-scatter.30.cloned.1.call-start = ((), (), s32[]{:S(2)}) async-start(), calls=%async_computation.26 | async-start | bytes 405504
  994.1 506.7 %reduce-scatter.32.cloned.1.call-start = ((), (), s32[]{:S(2)}) async-start(), calls=%async_computation.27 | async-start | bytes 405504
  998.1 606.6 %reduce-scatter.22.cloned.1.call-start = ((), (), s32[]{:S(2)}) async-start(), calls=%async_computation.22 | async-start | bytes 2433024 | tf_op jit(solution)/shard_map/reduce_scatter | solution.py:324
  1120.6 588.9 %reduce-scatter.20.cloned.1.call-start = ((), (), s32[]{:S(2)}) async-start(), calls=%async_computation.21 | async-start | bytes 2433024 | tf_op jit(solution)/shard_map/reduce_scatter | solution.py:322
  1156.0 657.2 %reduce-scatter.16.cloned.1.call-start = ((), (), s32[]{:S(2)}) async-start(), calls=%async_computation.19 | async-start | bytes 2433024 | tf_op jit(solution)/shard_map/reduce_scatter | solution.py:319
  1218.1 699.8 %reduce-scatter.18.cloned.1.call-start = ((), (), s32[]{:S(2)}) async-start(), calls=%async_computation.20 | async-start | bytes 2433024 | tf_op jit(solution)/shard_map/reduce_scatter | solution.py:321
  (85 other events, 2278.2 us)
Sparse Core Ops, SparseCore 0:
  11.0 57.0 all-gather.10
  71.2 53.0 all-gather.8
  127.3 53.1 all-gather.6
  183.3 53.1 all-gather.12
  238.2 175.0 all-gather.14
  415.0 175.4 all-gather.16
  927.6 23.0 reduce-scatter.27
  953.8 170.8 reduce-scatter.25
  1128.1 172.1 reduce-scatter.23
  1305.7 94.7 reduce-scatter.29
  1406.8 93.9 reduce-scatter.31
  1506.5 98.1 reduce-scatter.21
  1611.4 98.0 reduce-scatter.19
  1715.2 98.0 reduce-scatter.15
  1819.8 98.0 reduce-scatter.17
where the time goes:
time: 1930 us
  waiting for transfers between devices  1020 us (53%)
  matrix products  351 us (18%)
  blocking collectives  334 us (17%)
  other arithmetic  107 us (6%)
  local copies, waits for them, and re-layouts  84.6 us (4%)
    unnamed x18, waiting for transfers between devices  186 us
    psum x2, blocking collectives, local(): lax.psum((jnp.sum(picked_float, axis=0), jnp.sum(router_probs, axis=0)),...  129 us
    all_gather x1, waiting for transfers between devices, local(): lax.all_gather(w_out, 'batch', axis=1, tiled=True)  111 us
    reduce_scatter x1, waiting for transfers between devices, local(): lax.psum_scatter(grad_value, ('batch', 'expert'), scatter_dimension=0, ti...  105 us
    reduce_scatter x1, waiting for transfers between devices, local(): lax.psum_scatter(grad_key, ('batch', 'expert'), scatter_dimension=0, tile...  105 us
    reduce_scatter x1, waiting for transfers between devices, local(): lax.psum_scatter(grad_output, ('batch', 'expert'), scatter_dimension=0, t...  104 us
    reduce_scatter x1, waiting for transfers between devices, local(): lax.psum_scatter(grad_query, ('batch', 'expert'), scatter_dimension=0, ti...  104 us
    all_gather x1, waiting for transfers between devices, local(): lax.all_gather(w_in, 'batch', axis=2, tiled=True)  86.8 us
  transfers between devices with their start and end apart: 18, of which 13 were waited for; matrix products, arithmetic and copies ran while one was open for 23% of the time, Pallas kernels for 0%

commit v1 on v0

v1 whole, which is shorter than its diff:
```python
import functools

import jax
import jax.numpy as jnp
from jax import lax
from jax.experimental import pallas as pl
from jax.experimental.pallas import tpu as pltpu
from jax.sharding import PartitionSpec as P

HEAD = 64
LANES = 128
REACH = 384
QROWS = 256
EPSILON = 1e-05
BALANCE = 0.01
ALL = ("batch", "expert")
VMEM = 60 * 1024 * 1024
F32 = jnp.float32
BF16 = jnp.bfloat16


def dot(a, b):
    return jnp.dot(a, b, preferred_element_type=F32)


def dot_nt(a, b):
    return lax.dot_general(a, b, (((1,), (1,)), ((), ())), preferred_element_type=F32)


def dot_tn(a, b):
    return lax.dot_general(a, b, (((0,), (0,)), ((), ())), preferred_element_type=F32)


def swap(x, axis, mask):
    return lax.ppermute(x, axis, [(i, i ^ mask) for i in range(lax.axis_size(axis))])


def shift(x, step):
    size = lax.axis_size("expert")
    return lax.ppermute(x, "expert", [(i, (i + step) % size) for i in range(size)])


def staged():
    return lax.axis_size("batch") == 4 and lax.axis_size("expert") == 8


def gather_rows(x):
    if not staged():
        return lax.all_gather(x, ALL, axis=0, tiled=True)
    mb, me = lax.axis_index("batch"), lax.axis_index("expert")
    mz, mc = me // 2, me % 2
    ring = [shift(x, 2 * k) for k in (3, 2, 1)] + [x]
    ring = jnp.stack(ring + ring[:3])
    zs = lax.dynamic_slice_in_dim(ring, 3 - mz, 4, 0)
    b = [zs] + [swap(zs, "batch", k) for k in (1, 2, 3)]
    odd, high = (mb & 1) == 1, (mb & 2) == 2
    u = [jnp.where(odd, b[i ^ 1], b[i]) for i in range(4)]
    rows = jnp.stack([jnp.where(high, u[i ^ 2], u[i]) for i in range(4)])
    other = swap(rows, "expert", 1)
    both = jnp.stack(
        [jnp.where(mc == 0, rows, other), jnp.where(mc == 0, other, rows)], axis=2
    )
    return both.reshape(32 * x.shape[0], x.shape[1])


def scatter_rows(g):
    if not staged():
        return lax.psum_scatter(g, ALL, scatter_dimension=0, tiled=True).astype(F32)
    mb, me = lax.axis_index("batch"), lax.axis_index("expert")
    mz, mc = me // 2, me % 2
    r, c = g.shape[0] // 32, g.shape[1]
    g = g.reshape(4, 4, 2, r, c)
    mine = jnp.where(mc == 0, g[:, :, 0], g[:, :, 1])
    other = swap(jnp.where(mc == 0, g[:, :, 1], g[:, :, 0]), "expert", 1)
    s = (mine.astype(F32) + other.astype(F32)).astype(BF16)
    pick = lambda t, i: lax.dynamic_index_in_dim(t, i, 0, keepdims=False)
    parts = [swap(pick(s, mb ^ k), "batch", k) for k in (1, 2, 3)]
    t = sum((p.astype(F32) for p in parts), pick(s, mb).astype(F32)).astype(BF16)
    parts = [shift(pick(t, (mz + k) % 4), 2 * k) for k in (1, 2, 3)]
    return sum((p.astype(F32) for p in parts), pick(t, mz).astype(F32))


def total(x):
    if not staged():
        return lax.psum(x, ALL)
    for axis, mask in (("expert", 1), ("batch", 1), ("batch", 2), ("expert", 2), ("expert", 4)):
        x = x + swap(x, axis, mask)
    return x


def to_owners(x):
    return lax.all_to_all(x, "expert", split_axis=1, concat_axis=1, tiled=True)


def windows(length):
    for start in range(0, length, QROWS):
        yield start, max(0, start - REACH), start + QROWS


def half_masks():
    lane = lax.broadcasted_iota(jnp.int32, (1, LANES), 1)
    first = (lane < HEAD).astype(F32)
    return first, (first.astype(BF16), (1.0 - first).astype(BF16))


def attend_kernel(q_ref, k_ref, v_ref, row_ref, col_ref, out_ref, log_ref, mask_ref):
    length = q_ref.shape[0]

    @pl.when(pl.program_id(0) == 0)
    def _():
        for n, (start, low, stop) in enumerate(windows(length)):
            shape = (QROWS, stop - low)
            i = lax.broadcasted_iota(jnp.int32, shape, 0) + start
            j = lax.broadcasted_iota(jnp.int32, shape, 1) + low
            same = col_ref[start:stop, :] == row_ref[:, low:stop]
            mask_ref[n, :, : stop - low] = jnp.where((j <= i) & same, 0.0, -1e30)

    first, halves = half_masks()
    for n, (start, low, stop) in enumerate(windows(length)):
        q = q_ref[start:stop, :] * jnp.asarray(HEAD**-0.5, BF16)
        k, v = k_ref[low:stop, :], v_ref[low:stop, :]
        outs, logs = [], []
        for half in halves:
            s = dot_nt(q * half, k) + mask_ref[n, :, : stop - low]
            top = jnp.max(s, axis=1, keepdims=True)
            e = jnp.exp(s - top)
            sums = jnp.sum(e, axis=1, keepdims=True)
            outs.append(dot(e.astype(BF16), v) / sums)
            logs.append(top + jnp.log(sums))
        out_ref[start:stop, :] = (outs[0] * first + outs[1] * (1.0 - first)).astype(BF16)
        log_ref[start:stop, :] = logs[0] * first + logs[1] * (1.0 - first)


def attend(qkv, seg_row, seg_col, width):
    length = qkv.shape[0]
    pairs = width // LANES
    spec = lambda offset: pl.BlockSpec((length, LANES), lambda p, o=offset: (0, o + p))
    whole = lambda shape: pl.BlockSpec(shape, lambda p: (0,) * len(shape))
    return pl.pallas_call(
        attend_kernel,
        grid=(pairs,),
        in_specs=[spec(0), spec(pairs), spec(2 * pairs), whole((1, length)), whole((length, 1))],
        out_specs=[spec(0), spec(0)],
        out_shape=[
            jax.ShapeDtypeStruct((length, width), BF16),
            jax.ShapeDtypeStruct((length, width), F32),
        ],
        scratch_shapes=[pltpu.VMEM((length // QROWS, QROWS, QROWS + REACH), F32)],
        compiler_params=pltpu.CompilerParams(vmem_limit_bytes=VMEM),
        cost_estimate=pl.CostEstimate(
            flops=4 * length * 512 * width, bytes_accessed=12 * length * width, transcendentals=12 * length * 512
        ),
        name="attend",
    )(qkv, qkv, qkv, seg_row, seg_col)


def attend_back_kernel(
    q_ref, k_ref, v_ref, g_ref, log_ref, row_ref, col_ref, out_ref, mask_ref, dk_ref, dv_ref
):
    length = q_ref.shape[0]

    @pl.when(pl.program_id(0) == 0)
    def _():
        for n, (start, low, stop) in enumerate(windows(length)):
            shape = (stop - low, QROWS)
            j = lax.broadcasted_iota(jnp.int32, shape, 0) + low
            i = lax.broadcasted_iota(jnp.int32, shape, 1) + start
            same = col_ref[low:stop, :] == row_ref[:, start:stop]
            mask_ref[n, : stop - low, :] = jnp.where((j <= i) & same, 0.0, -1e30)

    dk_ref[...] = jnp.zeros_like(dk_ref)
    dv_ref[...] = jnp.zeros_like(dv_ref)
    _, halves = half_masks()
    scale = HEAD**-0.5
    for n, (start, low, stop) in enumerate(windows(length)):
        q = q_ref[start:stop, :] * jnp.asarray(scale, BF16)
        g = g_ref[start:stop, :]
        k, v = k_ref[low:stop, :], v_ref[low:stop, :]
        logs = log_ref[start:stop, :].T
        dq = jnp.zeros((QROWS, LANES), F32)
        for at, half in zip((0, HEAD), halves):
            qh, gh = q * half, g * half
            s = dot_nt(k, qh) + mask_ref[n, : stop - low, :]
            p = jnp.exp(s - logs[at : at + 1, :])
            dp = dot_nt(v, gh)
            centre = jnp.sum(dp * p, axis=0, keepdims=True)
            ds = (p * (dp - centre)).astype(BF16)
            dv_ref[low:stop, :] += dot(p.astype(BF16), gh)
            dk_ref[low:stop, :] += dot(ds, qh)
            dq += dot_tn(ds, k * half)
        out_ref[0, start:stop, :] = (dq * scale).astype(BF16)
    out_ref[1] = dk_ref[...].astype(BF16)
    out_ref[2] = dv_ref[...].astype(BF16)


def attend_back(qkv, grad, logs, seg_row, seg_col, width):
    length = qkv.shape[0]
    pairs = width // LANES
    spec = lambda offset: pl.BlockSpec((length, LANES), lambda p, o=offset: (0, o + p))
    whole = lambda shape: pl.BlockSpec(shape, lambda p: (0,) * len(shape))
    return pl.pallas_call(
        attend_back_kernel,
        grid=(pairs,),
        in_specs=[spec(0), spec(pairs), spec(2 * pairs), spec(0), spec(0), whole((1, length)), whole((length, 1))],
        out_specs=pl.BlockSpec((3, length, LANES), lambda p: (0, 0, p)),
        out_shape=jax.ShapeDtypeStruct((3, length, width), BF16),
        scratch_shapes=[
            pltpu.VMEM((length // QROWS, QROWS + REACH, QROWS), F32),
            pltpu.VMEM((length, LANES), F32),
            pltpu.VMEM((length, LANES), F32),
        ],
        compiler_params=pltpu.CompilerParams(vmem_limit_bytes=VMEM),
        cost_estimate=pl.CostEstimate(
            flops=10 * length * 512 * width, bytes_accessed=18 * length * width, transcendentals=12 * length * 512
        ),
        name="attend_back",
    )(qkv, qkv, qkv, grad, logs, seg_row, seg_col)


def slot_ids(shape, axis, base, groups, owners, split, slots):
    at = lax.broadcasted_iota(jnp.int32, shape, axis) + base
    row, slot = at // slots, at % slots
    return ((row % owners) * groups + row // owners) // split * slots + slot


def dispatch_kernel(groups, owners, split, slots, id_ref, x_ref, out_ref):
    rows, tokens = out_ref.shape[0], x_ref.shape[0]
    ids = slot_ids((rows, 1), 0, pl.program_id(0) * rows, groups, owners, split, slots)
    chosen = (ids == id_ref[...]).astype(F32).astype(BF16)
    out_ref[...] = dot(chosen, x_ref[...]).astype(BF16)


def dispatch(ids, x, groups, owners, split, slots):
    tokens, width = x.shape
    count, block = groups * owners * slots, 256
    return pl.pallas_call(
        functools.partial(dispatch_kernel, groups, owners, split, slots),
        grid=(count // block,),
        in_specs=[
            pl.BlockSpec((1, tokens), lambda i: (0, 0)),
            pl.BlockSpec((tokens, width), lambda i: (0, 0)),
        ],
        out_specs=pl.BlockSpec((block, width), lambda i: (i, 0)),
        out_shape=jax.ShapeDtypeStruct((count, width), BF16),
        compiler_params=pltpu.CompilerParams(vmem_limit_bytes=VMEM),
        cost_estimate=pl.CostEstimate(
            flops=2 * count * tokens * width, bytes_accessed=4 * count * width, transcendentals=0
        ),
        name="dispatch",
    )(ids, x)


def combine_kernel(groups, owners, split, slots, id_ref, x_ref, out_ref):
    rows, count = out_ref.shape[0], x_ref.shape[0]
    out_ref[...] = jnp.zeros_like(out_ref)
    step = 512
    for base in range(0, count, step):
        ids = slot_ids((1, step), 1, base, groups, owners, split, slots)
        chosen = (id_ref[...] == ids).astype(F32).astype(BF16)
        out_ref[...] += dot(chosen, x_ref[base : base + step, :])


def combine(ids, x, groups, owners, split, slots):
    tokens, (count, width), block = ids.shape[0], x.shape, 256
    return pl.pallas_call(
        functools.partial(combine_kernel, groups, owners, split, slots),
        grid=(tokens // block,),
        in_specs=[
            pl.BlockSpec((block, 1), lambda i: (i, 0)),
            pl.BlockSpec((count, width), lambda i: (0, 0)),
        ],
        out_specs=pl.BlockSpec((block, width), lambda i: (i, 0)),
        out_shape=jax.ShapeDtypeStruct((tokens, width), F32),
        compiler_params=pltpu.CompilerParams(vmem_limit_bytes=VMEM),
        cost_estimate=pl.CostEstimate(
            flops=2 * count * tokens * width, bytes_accessed=2 * count * width + 4 * tokens * width, transcendentals=0
        ),
        name="combine",
    )(ids, x)


def gelu_parts(x):
    size = jnp.abs(x)
    t = 1.0 / (1.0 + (0.3275911 * 0.5**0.5) * size)
    bell = jnp.exp(-0.5 * x * x)
    poly = t * (
        0.5 * 0.254829592
        + t * (0.5 * -0.284496736 + t * (0.5 * 1.421413741 + t * (0.5 * -1.453152027 + t * (0.5 * 1.061405429))))
    )
    tail = poly * bell
    return jnp.where(x < 0, tail, 1.0 - tail), bell * 0.3989422804014327


def expert_kernel(
    steps, experts,
    id_ref, h0, h1, z0, z1, win_a, wout_a, win_b, wout_b, wr_ref,
    p0, p1, d0, d1, gwin_a, gwout_a, gwin_b, gwout_b, groute,
    hid_a, hid_b, dpre_a, dpre_b, dexp_s, acc_win, acc_wout,
):
    i = pl.program_id(0)
    width = wr_ref.shape[0]
    rows = h0.shape[1]
    sub = min(rows, 256)

    @pl.when(i == 0)
    def _():
        gwin_a[...] = jnp.zeros_like(gwin_a)
        gwout_a[...] = jnp.zeros_like(gwout_a)
        acc_win[...] = jnp.zeros_like(acc_win)
        acc_wout[...] = jnp.zeros_like(acc_wout)
        groute[...] = jnp.zeros_like(groute)

    def work(h_ref, z_ref, p_ref, d_ref):
        lane = lax.broadcasted_iota(jnp.int32, (1, LANES), 1)
        own = (lane == id_ref[0]).astype(F32)

        def block(n, _):
            at = pl.ds(pl.multiple_of(n * sub, sub), sub)
            h = h_ref[0, at, :]
            logits = jnp.where(lane < experts, dot(h, wr_ref[...]), -1e30)
            e = jnp.exp(logits - jnp.max(logits, axis=1, keepdims=True))
            probs = e / jnp.sum(e, axis=1, keepdims=True)
            gate = jnp.sum(probs * own, axis=1, keepdims=True)
            dz = z_ref[0, at, :].astype(F32)
            dexp = (gate * dz).astype(BF16)
            dexp_s[at, :] = dexp
            piece = back = None
            for win, wout, hid_s, dpre_s in ((win_a, wout_a, hid_a, dpre_a), (win_b, wout_b, hid_b, dpre_b)):
                pre = dot(h, win[:width, :]) + win[width : width + 1, :].astype(F32)
                phi, bell = gelu_parts(pre)
                hid = (pre * phi).astype(BF16)
                hid_s[at, :] = hid
                out = dot(hid, wout[...])
                piece = out if piece is None else piece + out
                dpre = (dot_nt(dexp, wout[...]) * (phi + pre * bell)).astype(BF16)
                dpre_s[at, :] = dpre
                out = dot_nt(dpre, win[:width, :])
                back = out if back is None else back + out
            p_ref[at, :] = piece.astype(BF16)
            dgate = jnp.sum(dz * piece, axis=1, keepdims=True)
            dlog = (dgate * probs * (own - gate)).astype(BF16)
            d_ref[at, :] = (back + dot_nt(dlog, wr_ref[...])).astype(BF16)
            groute[...] += dot_tn(h, dlog)
            return 0

        lax.fori_loop(0, rows // sub, block, 0)
        for dpre_s, hid_s, to_win, to_wout in (
            (dpre_a, hid_a, gwin_a, gwout_a),
            (dpre_b, hid_b, acc_win, acc_wout),
        ):
            dpre = dpre_s[...]
            to_win[:width, :] += dot_tn(h_ref[0], dpre)
            to_win[width : width + 8, :] += jnp.broadcast_to(
                jnp.sum(dpre.astype(F32), axis=0, keepdims=True), (8, dpre.shape[1])
            )
            to_wout[...] += dot_tn(hid_s[...], dexp_s[...])

    @pl.when(i < steps)
    def _():
        work(h0, z0, p0, d0)

    @pl.when(i >= steps)
    def _():
        work(h1, z1, p1, d1)

    @pl.when(i == 2 * steps - 1)
    def _():
        gwin_b[...] = acc_win[...].astype(BF16)
        gwout_b[...] = acc_wout[...].astype(BF16)


def expert(expert_id, own_h, other_h, own_z, other_z, at, weights, w_route, experts):
    win_a, wout_a, win_b, wout_b = weights
    rows, width = own_h.shape[1:]
    hidden = wout_a.shape[0]
    block = min(rows, 512)
    steps = rows // block
    early = lambda i: jnp.minimum(i, steps - 1)
    late = lambda i: jnp.maximum(i - steps, 0)
    once = lambda a: pl.BlockSpec(a.shape, lambda i: (0,) * a.ndim)
    first = pl.BlockSpec((1, block, width), lambda i: (at, early(i), 0))
    second = pl.BlockSpec((1, block, width), lambda i: (0, late(i), 0))
    out_first = pl.BlockSpec((block, width), lambda i: (early(i), 0))
    out_second = pl.BlockSpec((block, width), lambda i: (late(i), 0))
    shape = jax.ShapeDtypeStruct
    outs = [shape((rows, width), BF16)] * 4 + [
        shape((width + 16, hidden), F32),
        shape((hidden, width), F32),
        shape((width + 16, hidden), BF16),
        shape((hidden, width), BF16),
        shape((width, LANES), F32),
    ]
    return pl.pallas_call(
        functools.partial(expert_kernel, steps, experts),
        grid=(2 * steps,),
        in_specs=[pl.BlockSpec(memory_space=pltpu.SMEM), first, second, first, second]
        + [once(w) for w in (win_a, wout_a, win_b, wout_b, w_route)],
        out_specs=[out_first, out_second, out_first, out_second] + [once(o) for o in outs[4:]],
        out_shape=outs,
        scratch_shapes=[
            *[pltpu.VMEM((block, hidden), BF16)] * 4,
            pltpu.VMEM((block, width), BF16),
            pltpu.VMEM((width + 16, hidden), F32),
            pltpu.VMEM((hidden, width), F32),
        ],
        compiler_params=pltpu.CompilerParams(vmem_limit_bytes=VMEM),
        cost_estimate=pl.CostEstimate(
            flops=48 * rows * hidden * width, bytes_accessed=28 * width * hidden, transcendentals=4 * rows * hidden
        ),
        name="expert",
    )(expert_id, own_h, other_h, own_z, other_z, win_a, wout_a, win_b, wout_b, w_route)


def normed(x):
    centred = x - jnp.mean(x, axis=-1, keepdims=True)
    rstd = lax.rsqrt(jnp.mean(centred * centred, axis=-1, keepdims=True) + EPSILON)
    return centred * rstd, rstd


def norm_back(grad, gain, unit, rstd):
    g = grad * gain
    mean = lambda t: jnp.mean(t, axis=-1, keepdims=True)
    return rstd * (g - mean(g) - unit * mean(g * unit))


def pad_columns(x, count):
    return jnp.pad(x, ((0, 0), (0, count - x.shape[1])))


def up(count):
    return -(-count // LANES) * LANES


def local(
    tokens, cotangent, segment_ids, routes, capacity, ln1_gain, ln1_bias, w_query, b_query, w_key, w_value,
    b_value, w_output, b_output, ln2_gain, ln2_bias, w_router, w_in, b_in, w_out, b_out,
):
    row_count, width = tokens.shape
    experts = capacity.shape[0]
    slots = 2 * row_count // experts
    groups = w_in.shape[0]
    owners = lax.axis_size("expert")
    split = groups * owners // experts
    share = w_query.shape[0]
    devices = lax.axis_size("batch") * owners
    me = lax.axis_index("expert")
    layout = (groups, owners, split, slots)

    chosen = routes[:, 0]
    picked = chosen[:, None] == jnp.arange(experts, dtype=jnp.int32)[None, :]
    picked_float = picked.astype(F32)
    position = jnp.arange(row_count, dtype=jnp.int32)
    earlier = (position[None, :] < position[:, None]).astype(BF16)
    rank = dot(earlier, picked.astype(BF16))
    slot = jnp.sum(rank * picked_float, axis=1)
    limit = jnp.sum(capacity.astype(F32)[None, :] * picked_float, axis=1)
    kept = slot < limit
    kept_float = kept.astype(F32)
    ids = jnp.where(kept, chosen * slots + slot.astype(jnp.int32), -1)
    id_row, id_col = ids[None, :], ids[:, None]
    counts = jnp.sum(picked_float, axis=0)

    spread = -(-experts // share)
    small = jnp.stack([ln1_gain, ln1_bias, b_query, b_value, b_output, ln2_gain, ln2_bias], axis=1)
    tally = jnp.pad(counts, (0, spread * share - experts)).reshape(spread, share).T.astype(BF16)
    extra = pad_columns(jnp.concatenate([small, tally], axis=1), up(7 + spread))
    wide = gather_rows(jnp.concatenate([w_query, w_key, w_value, extra], axis=1))
    rest = gather_rows(jnp.concatenate([w_output, pad_columns(jnp.concatenate([w_router, b_out.T], axis=1), up(2 * experts))], axis=1))
    vectors = wide[:, 3 * width : 3 * width + 7].astype(F32).T
    gain_one, shift_one, bias_query, bias_value, bias_output, gain_two, shift_two = vectors
    tallies = wide[:, 3 * width + 7 : 3 * width + 7 + spread].astype(F32).reshape(devices, share, spread)
    all_counts = jnp.sum(tallies, axis=0).T.reshape(-1)[:experts]
    full_output = rest[:, :width]
    full_router = pad_columns(rest[:, width : width + experts], LANES)
    bias_expert = rest[:, width + experts : width + 2 * experts].T

    token_total = float(row_count * devices)
    fraction = all_counts / token_total

    weights = []
    for l in range(groups):
        mask = 1 if l % 2 == 0 else 2
        win = jnp.concatenate([w_in[l], jnp.broadcast_to(b_in[l][None, :], (16, b_in.shape[1]))], axis=0)
        weights.append((win, w_out[l], swap(win, "batch", mask), swap(w_out[l], "batch", mask)))

    chunk = min(2, groups)
    flat = (chunk, owners * slots, width)

    def send(x):
        rows = dispatch(id_row, x, *layout).reshape(groups, owners, slots, width)
        got = []
        for c in range(0, groups, chunk):
            mine = to_owners(rows[c : c + chunk]).reshape(flat)
            for l in range(chunk):
                theirs = swap(mine[l : l + 1], "batch", 2 if (c + l) % 2 == 0 else 1)
                got.append((mine, theirs, l))
        return got

    def bring(pieces):
        back = []
        for c in range(0, groups, chunk):
            rows = []
            for l in range(c, c + chunk):
                own, sent = pieces[l]
                rows.append((own.astype(F32) + swap(sent, "batch", 2 if l % 2 == 0 else 1).astype(F32)).astype(BF16))
            rows = jnp.stack(rows).reshape(chunk, owners, slots, width)
            back.append(to_owners(rows).reshape(chunk * owners * slots, width))
        return jnp.concatenate(back) if len(back) > 1 else back[0]

    grad_rows = send(cotangent)

    inputs = tokens.astype(F32)
    unit_one, rstd_one = normed(inputs)
    h_one = (unit_one * gain_one + shift_one).astype(BF16)
    nothing = jnp.zeros((width,), F32)
    bias = jnp.concatenate([bias_query, nothing, bias_value, jnp.zeros((wide.shape[1] - 3 * width,), F32)])
    qkv = (dot(h_one, wide) + bias).astype(BF16)
    seg_row = segment_ids.reshape(1, row_count)
    seg_col = segment_ids.reshape(row_count, 1)
    attended, logs = attend(qkv, seg_row, seg_col, width)
    resid = inputs + dot(attended, full_output) + bias_output
    unit_two, rstd_two = normed(resid)
    h_two = (unit_two * gain_two + shift_two).astype(BF16)

    token_rows = send(h_two)
    made = []
    for l in range(groups):
        mine_h, theirs_h, at = token_rows[l]
        mine_z, theirs_z, _ = grad_rows[l]
        number = ((me * groups + l) // split).astype(jnp.int32).reshape(1)
        made.append(expert(number, mine_h, theirs_h, mine_z, theirs_z, at, weights[l], full_router, experts))

    router_probs = jax.nn.softmax(dot(h_two, full_router)[:, :experts], axis=-1)
    mixing = kept_float * jnp.sum(router_probs * picked_float, axis=1)
    grad_out = cotangent.astype(F32)
    expert_bias = dot(picked.astype(BF16), bias_expert)
    gate_bias = kept_float * jnp.sum(grad_out * expert_bias, axis=1)
    grad_probs = picked_float * gate_bias[:, None] + BALANCE * experts * fraction[None, :] / token_total
    grad_logits = router_probs * (grad_probs - jnp.sum(grad_probs * router_probs, axis=1, keepdims=True))
    grad_logits = grad_logits.astype(BF16)
    mixed = picked_float * mixing[:, None]
    mixed_high = mixed.astype(BF16)
    mixed_low = (mixed - mixed_high.astype(F32)).astype(BF16)
    grad_bias_expert = dot_tn(cotangent, mixed_high) + dot_tn(cotangent, mixed_low)
    grad_router = dot_tn(h_two, grad_logits) + sum(m[8] for m in made)[:, :experts]
    prob_sums = total(jnp.sum(router_probs, axis=0))
    mean_probs = prob_sums / token_total
    balance_loss = experts * jnp.sum(fraction * mean_probs)
    expert_shares = jnp.stack([experts * fraction, experts * mean_probs])

    returned = bring([(m[2], m[3]) for m in made])
    grad_h_two = dot_nt(grad_logits, full_router[:, :experts]) + combine(id_col, returned, *layout)

    grad_resid = grad_out + norm_back(grad_h_two, gain_two, unit_two, rstd_two)
    grad_branch = grad_resid.astype(BF16)
    grad_att = dot_nt(grad_branch, full_output).astype(BF16)
    dqkv = attend_back(qkv, grad_att, logs, seg_row, seg_col, width)

    columns = lambda *rows: jnp.stack(rows, axis=1)
    grads_two = columns(
        jnp.sum(grad_h_two * unit_two, axis=0), jnp.sum(grad_h_two, axis=0), jnp.sum(grad_branch.astype(F32), axis=0)
    )
    packed = jnp.concatenate([grad_router, grad_bias_expert, grads_two], axis=1)
    packed = jnp.concatenate([dot_tn(attended, grad_branch), pad_columns(packed, up(packed.shape[1]))], axis=1)
    rest_sum = scatter_rows(packed.astype(BF16))

    grad_in, grad_in_bias, grad_w_out = [], [], []
    for l in range(groups):
        mask = 1 if l % 2 == 0 else 2
        got_in, got_out = swap(made[l][6], "batch", mask), swap(made[l][7], "batch", mask)
        grad_in.append(made[l][4][:width] + got_in[:width].astype(F32))
        grad_in_bias.append(made[l][4][width] + got_in[width].astype(F32))
        grad_w_out.append(made[l][5] + got_out.astype(F32))

    fetched = combine(id_col, bring([(m[0], m[1]) for m in made]), *layout)
    block_out = (resid + mixing[:, None] * (fetched + expert_bias)).astype(BF16)

    grads_w = jnp.concatenate([dot_tn(h_one, dqkv[s]) for s in range(3)], axis=1)
    grad_h_one = sum(dot_nt(dqkv[s], wide[:, s * width : (s + 1) * width]) for s in range(3))
    input_grad = grad_resid + norm_back(grad_h_one, gain_one, unit_one, rstd_one)
    grads_one = columns(
        jnp.sum(grad_h_one * unit_one, axis=0),
        jnp.sum(grad_h_one, axis=0),
        jnp.sum(dqkv[0].astype(F32), axis=0),
        jnp.sum(dqkv[2].astype(F32), axis=0),
    )
    wide_sum = scatter_rows(jnp.concatenate([grads_w, pad_columns(grads_one, LANES)], axis=1).astype(BF16))

    tail = 3 * width
    side = width + 2 * experts
    return (
        block_out,
        balance_loss,
        expert_shares,
        input_grad,
        wide_sum[:, tail],
        wide_sum[:, tail + 1],
        wide_sum[:, :width],
        wide_sum[:, tail + 2],
        wide_sum[:, width : 2 * width],
        wide_sum[:, 2 * width : 3 * width],
        wide_sum[:, tail + 3],
        rest_sum[:, :width],
        rest_sum[:, side + 2],
        rest_sum[:, side],
        rest_sum[:, side + 1],
        rest_sum[:, width : width + experts],
        jnp.stack(grad_in),
        jnp.stack(grad_in_bias),
        jnp.stack(grad_w_out),
        rest_sum[:, width + experts : side].T,
    )


def solution(mesh):
    rows, split = P(ALL, None), P(ALL)
    experts = (P("expert", None, "batch"), P("expert", "batch"), P("expert", "batch", None), P(None, ALL))
    return jax.shard_map(
        local,
        mesh=mesh,
        in_specs=(
            rows, rows, rows, rows, P(), split, split, rows, split, rows, rows, split, rows, split, split, split,
            rows, *experts,
        ),
        out_specs=(
            rows, P(), P(), rows, split, split, rows, split, rows, rows, split, rows, split, split, split, rows,
            *experts,
        ),
        check_vma=False,
    )
```

time: 1930 us -> 845 us (0.44)
  waiting for transfers between devices: 1020 us -> 299 us
  blocking collectives: 334 us -> 0 us
  matrix products: 351 us -> 49.5 us
  Pallas kernels: 0 us -> 197 us
  starting transfers between devices: 14 us -> 114 us
    reduce_scatter x6 -> x0, waiting for transfers between devices: 417 us -> none  [the longest x1 105 us: local(): lax.psum_scatter(grad_value, ('batch', 'expert'), scatter_dimension=0, ti...]
    dot_general x29 -> x17, matrix products: 351 us -> 49.5 us  [the longest x7 19.2 us: dot_tn(): lax.dot_general(a, b, (((0,), (0,)), ((), ())), preferred_element_type=F32)]
    all_gather x6 -> x0, waiting for transfers between devices: 288 us -> none  [the longest x1 111 us: local(): lax.all_gather(w_out, 'batch', axis=1, tiled=True)]
    ppermute x0 -> x65, waiting for transfers between devices: none -> 264 us  [the longest x53 259 us: swap(): lax.ppermute(x, axis, [(i, i ^ mask) for i in range(lax.axis_size(axis))])]
    pallas_call x0 -> x10, Pallas kernels: none -> 197 us  [the longest x4 117 us: expert(): pl.pallas_call(functools.partial(expert_kernel, steps, experts), grid=(2...]
    unnamed x18 -> x0, waiting for transfers between devices: 186 us -> none
    psum x2 -> x0, blocking collectives: 129 us -> none  [local(): lax.psum((jnp.sum(picked_float, axis=0), jnp.sum(router_probs, axis=0)),...]
    all_to_all x3 -> x8, waiting for transfers between devices: 127 us -> 35.3 us  [to_owners(): return lax.all_to_all(x, 'expert', split_axis=1, concat_axis=1, tiled=True)]
  transfers between devices with their start and end apart: 18 -> 73, of which waited for: 13 -> 31; matrix products, arithmetic and copies ran while one was open for 23% -> 20% of each run, Pallas kernels for 0% -> 19%
where the time goes in v1:
time: 845 us; the launch traced here: 837 us
  waiting for transfers between devices  299 us (35%)
  Pallas kernels  197 us (23%)
  starting transfers between devices  114 us (13%)
  other arithmetic  94.6 us (11%)
  local copies, waits for them, and re-layouts  78.9 us (9%)
  matrix products  49.5 us (6%)
    ppermute x53, waiting for transfers between devices, swap(): lax.ppermute(x, axis, [(i, i ^ mask) for i in range(lax.axis_size(axis))])  259 us
    pallas_call x4, Pallas kernels, expert(): pl.pallas_call(functools.partial(expert_kernel, steps, experts), grid=(2...  117 us
    ppermute x53, starting transfers between devices, swap(): lax.ppermute(x, axis, [(i, i ^ mask) for i in range(lax.axis_size(axis))])  58.1 us
    all_to_all x8, starting transfers between devices, to_owners(): return lax.all_to_all(x, 'expert', split_axis=1, concat_axis=1, tiled=True)  36.5 us
    all_to_all x8, waiting for transfers between devices, to_owners(): return lax.all_to_all(x, 'expert', split_axis=1, concat_axis=1, tiled=True)  35.3 us
    pallas_call x1, Pallas kernels, attend_back(): pl.pallas_call(attend_back_kernel, grid=(pairs,), in_specs=[spec(0), spec...  28.7 us
    pallas_call x1, Pallas kernels, attend(): pl.pallas_call(attend_kernel, grid=(pairs,), in_specs=[spec(0), spec(pair...  21.2 us
    ppermute x12, starting transfers between devices, shift(): lax.ppermute(x, 'expert', [(i, (i + step) % size) for i in range(size)])  19.7 us
  transfers between devices with their start and end apart: 73, of which 31 were waited for; matrix products, arithmetic and copies ran while one was open for 20% of the time, Pallas kernels for 19%

profile of v1, /device:TPU:0, one launch (start us, length us, event | category | flops | bytes accessed | tf_op | source)
XLA Modules:
  0.0 837.4 jit_solution(12161606089306224780)
XLA Ops:
  33.9 9.8 %collective-permute-done.5 = bf16[4,24,2432]{2,1,0:T(8,128)(2,1)S(1)} collective-permute-done((bf16[4,24,2432]{2,1,0:T(8,128)(2,1)S(1)}, bf16[4,24,2432]{2,1,0:T(8,128)(2,1)S(1)}, u32[]{:S(2)}, u32[]{:S(2)}) %collective-permute-start.5) | collective-permute-done | bytes 466976 | tf_op jit(solution)/shard_map/ppermute | solution.py:35
  43.6 8.3 collective-permute-done.3
  61.6 8.1 dispatch.3
  89.6 21.2 %attend.1 = (bf16[1024,768]{1,0:T(8,128)(2,1)}, f32[1024,768]{1,0:T(8,128)}) custom-call(bf16[1024,2432]{1,0:T(8,128)(2,1)} %add_convert_fusion.q_ref.k_ref.v_ref, bf16[1024,2432]{1,0:T(8,128)(2,1)} %add_convert_fusion.q_ref.k_ref.v_ref, bf16[1024,2432]{1,0:T(8,128)(2,1)} %add_convert_fusion.q_ref.k_ref.v_ref, s32[1,1024]{1,0:T(1,128)} %row_ref.3, ...), custom_call_target="tpu_custom_call" | custom-call | flops 1610612736 | bytes 9437184 | tf_op jit(solution)/shard_map/attend/pallas_call | solution.py:139
  116.7 8.1 dispatch.2
  137.1 35.3 %all-to-all-done.3 = bf16[2,8,64,768]{3,2,0,1:T(8,128)(2,1)} async-done(((bf16[2,8,64,768]{3,2,0,1:T(8,128)(2,1)}), bf16[2,8,64,768]{3,2,0,1:T(8,128)(2,1)}, u32[]{:S(2)}, u32[]{:S(2)}) %all-to-all-start.3) | async-done | bytes 1572896 | tf_op jit(solution)/shard_map/all_to_all | solution.py:92
  206.2 30.3 %collective-permute-done.27.wout_b = bf16[768,768]{1,0:T(8,128)(2,1)} collective-permute-done((bf16[768,768]{1,0:T(8,128)(2,1)}, bf16[768,768]{1,0:T(8,128)(2,1)}, u32[]{:S(2)}, u32[]{:S(2)}) %collective-permute-start.27) | collective-permute-done | bytes 1179680 | tf_op jit(solution)/shard_map/ppermute | solution.py:35
  244.9 29.3 %expert.6 = (bf16[512,768]{1,0:T(8,128)(2,1)}, bf16[512,768]{1,0:T(8,128)(2,1)}, bf16[512,768]{1,0:T(8,128)(2,1)}, bf16[512,768]{1,0:T(8,128)(2,1)}, f32[784,768...) custom-call(s32[1]{0:T(128)} %bitcast.56.id_ref, ...), custom_call_target="tpu_custom_call" | custom-call | flops 14495514624 | bytes 16515072 | tf_op jit(solution)/shard_map/expert/pallas_call | solution.py:393
  279.9 29.3 %expert.7 = (bf16[512,768]{1,0:T(8,128)(2,1)}, bf16[512,768]{1,0:T(8,128)(2,1)}, bf16[512,768]{1,0:T(8,128)(2,1)}, bf16[512,768]{1,0:T(8,128)(2,1)}, f32[784,768...) custom-call(s32[1]{0:T(128)} %bitcast.67.id_ref, ...), custom_call_target="tpu_custom_call" | custom-call | flops 14495514624 | bytes 16515072 | tf_op jit(solution)/shard_map/expert/pallas_call | solution.py:393
  320.4 9.6 %collective-permute-done.33 = bf16[512,768]{1,0:T(8,128)(2,1)} collective-permute-done((bf16[512,768]{1,0:T(8,128)(2,1)}, bf16[512,768]{1,0:T(8,128)(2,1)}, u32[]{:S(2)}, u32[]{:S(2)}) %collective-permute-start.33) | collective-permute-done | bytes 786464 | tf_op jit(solution)/shard_map/ppermute | solution.py:35
  342.4 37.3 %collective-permute-done.35 = f32[32]{0:T(128)S(1)} collective-permute-done((f32[32]{0:T(128)S(1)}, f32[32]{0:T(128)S(1)}, u32[]{:S(2)}, u32[]{:S(2)}) %collective-permute-start.35) | collective-permute-done | bytes 160 | tf_op jit(solution)/shard_map/ppermute | solution.py:35
  392.3 8.7 %collective-permute-done.41 = bf16[512,768]{1,0:T(8,128)(2,1)} collective-permute-done((bf16[512,768]{1,0:T(8,128)(2,1)}, bf16[512,768]{1,0:T(8,128)(2,1)}, u32[]{:S(2)}, u32[]{:S(2)}) %collective-permute-start.41) | collective-permute-done | bytes 786464 | tf_op jit(solution)/shard_map/ppermute | solution.py:35
  419.4 15.4 %collective-permute-done.14.h1 = bf16[1,512,768]{2,1,0:T(8,128)(2,1)} collective-permute-done((bf16[1,512,768]{2,1,0:T(8,128)(2,1)}, bf16[1,512,768]{2,1,0:T(8,128)(2,1)}, u32[]{:S(2)}, u32[]{:S(2)}) %collective-permute-start.14) | collective-permute-done | bytes 786464 | tf_op jit(solution)/shard_map/ppermute | solution.py:35
  440.6 28.7 %expert.4 = (bf16[512,768]{1,0:T(8,128)(2,1)}, bf16[512,768]{1,0:T(8,128)(2,1)}, bf16[512,768]{1,0:T(8,128)(2,1)}, bf16[512,768]{1,0:T(8,128)(2,1)}, f32[784,768...) custom-call(s32[1]{0:T(128)} %bitcast.36.id_ref, ...), custom_call_target="tpu_custom_call" | custom-call | flops 14495514624 | bytes 16515072 | tf_op jit(solution)/shard_map/expert/pallas_call | solution.py:393
  469.4 13.9 %collective-permute-done.22.wout_b = bf16[768,768]{1,0:T(8,128)(2,1)} collective-permute-done((bf16[768,768]{1,0:T(8,128)(2,1)}, bf16[768,768]{1,0:T(8,128)(2,1)}, u32[]{:S(2)}, u32[]{:S(2)}) %collective-permute-start.22) | collective-permute-done | bytes 1179680 | tf_op jit(solution)/shard_map/ppermute | solution.py:35
  484.8 29.3 %expert.5 = (bf16[512,768]{1,0:T(8,128)(2,1)}, bf16[512,768]{1,0:T(8,128)(2,1)}, bf16[512,768]{1,0:T(8,128)(2,1)}, bf16[512,768]{1,0:T(8,128)(2,1)}, f32[784,768...) custom-call(s32[1]{0:T(128)} %bitcast.48.id_ref, ...), custom_call_target="tpu_custom_call" | custom-call | flops 14495514624 | bytes 16515072 | tf_op jit(solution)/shard_map/expert/pallas_call | solution.py:393
  525.4 9.6 %collective-permute-done.23 = bf16[512,768]{1,0:T(8,128)(2,1)} collective-permute-done((bf16[512,768]{1,0:T(8,128)(2,1)}, bf16[512,768]{1,0:T(8,128)(2,1)}, u32[]{:S(2)}, u32[]{:S(2)}) %collective-permute-start.23) | collective-permute-done | bytes 786464 | tf_op jit(solution)/shard_map/ppermute | solution.py:35
  538.1 26.0 %collective-permute-done.39 = bf16[512,768]{1,0:T(8,128)(2,1)} collective-permute-done((bf16[512,768]{1,0:T(8,128)(2,1)}, bf16[512,768]{1,0:T(8,128)(2,1)}, u32[]{:S(2)}, u32[]{:S(2)}) %collective-permute-start.39) | collective-permute-done | bytes 786464 | tf_op jit(solution)/shard_map/ppermute | solution.py:35
  582.5 32.7 %collective-permute-done.62 = bf16[768,768]{1,0:T(8,128)(2,1)} collective-permute-done((bf16[768,768]{1,0:T(8,128)(2,1)}, bf16[768,768]{1,0:T(8,128)(2,1)}, u32[]{:S(2)}, u32[]{:S(2)}) %collective-permute-start.62) | collective-permute-done | bytes 1179680 | tf_op jit(solution)/shard_map/ppermute | solution.py:35
  628.9 7.8 collective-permute-done.58
  637.4 13.2 %collective-permute-done.57 = bf16[784,768]{1,0:T(8,128)(2,1)} collective-permute-done((bf16[784,768]{1,0:T(8,128)(2,1)}, bf16[784,768]{1,0:T(8,128)(2,1)}, u32[]{:S(2)}, u32[]{:S(2)}) %collective-permute-start.57) | collective-permute-done | bytes 1204256 | tf_op jit(solution)/shard_map/ppermute | solution.py:35
  700.9 28.7 %attend_back.1 = bf16[3,1024,768]{2,1,0:T(8,128)(2,1)} custom-call(bf16[1024,2432]{1,0:T(8,128)(2,1)} %add_convert_fusion.q_ref.k_ref.v_ref, bf16[1024,2432]{1,0:T(8,128)(2,1)} %add_convert_fusion.q_ref.k_ref.v_ref, bf16[1024,2432]{1,0:T(8,128)(2,1)} %add_convert_fusion.q_ref.k_ref.v_ref, bf16[1024,768]{1,0:T(8,128)(2,1)} %convolution_convert_fusion.g_ref, ...), custom_call_target="tpu_custom_call" | custom-call | flops 4026531840 | bytes 14155776 | tf_op jit(solution)/shard_map/attend_back/pallas_call | solution.py:201
  807.5 7.7 collective-permute-done.44
  815.2 7.3 collective-permute-done.46
  (439 shorter events, 377.9 us)
Async XLA Ops:
  74.3 55.0 %all-to-all-start.4 = ((bf16[2,8,64,768]{3,2,0,1:T(8,128)(2,1)}), bf16[2,8,64,768]{3,2,0,1:T(8,128)(2,1)}, u32[]{:S(2)}, u32[]{:S(2)}) async-start(bf16[2,8,64,768]{3,2,0,1:T(8,128)(2,1)} %copy.147), calls=%async_computation.4 | async-start | bytes 3145728 | tf_op jit(solution)/shard_map/all_to_all | solution.py:92
  172.4 65.6 %all-to-all-start.1 = ((bf16[2,8,64,768]{3,2,0,1:T(8,128)(2,1)}), bf16[2,8,64,768]{3,2,0,1:T(8,128)(2,1)}, u32[]{:S(2)}, u32[]{:S(2)}) async-start(bf16[2,8,64,768]{3,2,0,1:T(8,128)(2,1)} %copy.140), calls=%async_computation.1 | async-start | bytes 3145728 | tf_op jit(solution)/shard_map/all_to_all | solution.py:92
  182.1 60.6 %collective-permute-start.26 = (bf16[784,768]{1,0:T(8,128)(2,1)}, bf16[784,768]{1,0:T(8,128)(2,1)}, u32[]{:S(2)}, u32[]{:S(2)}) collective-permute-start(bf16[784,768]{1,0:T(8,128)(2,1)} %pad_maximum_fusion.14.win_a), channel_id=1, source_target_pairs={{0,8},{8,0},{16,24},{24,16},{1,9},{9,1},{17,25},{25,17},{2,10},{10... | collective-permute-start | bytes 3612680 | tf_op jit(solution)/shard_map/ppermute | solution.py:35
  189.1 55.2 %collective-permute-start.25 = (bf16[1,512,768]{2,1,0:T(8,128)(2,1)}, bf16[1,512,768]{2,1,0:T(8,128)(2,1)}, u32[]{:S(2)}, u32[]{:S(2)}) collective-permute-start(bf16[1,512,768]{2,1,0:T(8,128)(2,1)} %bitcast.62), channel_id=1, source_target_pairs={{0,16},{8,24},{16,0},{24,8},{1,17},{9,25},{17,1},{25,9},{2,18},{10... | collective-permute-start | bytes 2359304 | tf_op jit(solution)/shard_map/ppermute | solution.py:35
  193.3 51.6 %collective-permute-start.24 = (bf16[1,512,768]{2,1,0:T(8,128)(2,1)}, bf16[1,512,768]{2,1,0:T(8,128)(2,1)}, u32[]{:S(2)}, u32[]{:S(2)}) collective-permute-start(bf16[1,512,768]{2,1,0:T(8,128)(2,1)} %bitcast.59), channel_id=1, source_target_pairs={{0,16},{8,24},{16,0},{24,8},{1,17},{9,25},{17,1},{25,9},{2,18},{10... | collective-permute-start | bytes 2359304 | tf_op jit(solution)/shard_map/ppermute | solution.py:35
  194.9 81.7 %collective-permute-start.31 = (bf16[784,768]{1,0:T(8,128)(2,1)}, bf16[784,768]{1,0:T(8,128)(2,1)}, u32[]{:S(2)}, u32[]{:S(2)}) collective-permute-start(bf16[784,768]{1,0:T(8,128)(2,1)} %pad_maximum_fusion.15.win_a), channel_id=1, source_target_pairs={{0,16},{8,24},{16,0},{24,8},{1,17},{9,25},{17,1},{25,9},{2,18},{10... | collective-permute-start | bytes 3612680 | tf_op jit(solution)/shard_map/ppermute | solution.py:35
  238.0 94.6 %all-to-all-start = ((bf16[2,8,64,768]{3,2,0,1:T(8,128)(2,1)}), bf16[2,8,64,768]{3,2,0,1:T(8,128)(2,1)}, u32[]{:S(2)}, u32[]{:S(2)}) async-start(bf16[2,8,64,768]{3,2,0,1:T(8,128)(2,1)} %copy.138), calls=%async_computation | async-start | bytes 3145728 | tf_op jit(solution)/shard_map/all_to_all | solution.py:92
  313.1 102.4 %collective-permute-start.16 = (bf16[784,768]{1,0:T(8,128)(2,1)}, bf16[784,768]{1,0:T(8,128)(2,1)}, u32[]{:S(2)}, u32[]{:S(2)}) collective-permute-start(bf16[784,768]{1,0:T(8,128)(2,1)} %pad_maximum_fusion.12.win_a), channel_id=1, source_target_pairs={{0,8},{8,0},{16,24},{24,16},{1,9},{9,1},{17,25},{25,17},{2,10},{10... | collective-permute-start | bytes 3612680 | tf_op jit(solution)/shard_map/ppermute | solution.py:35
  313.6 100.3 %collective-permute-start.17 = (bf16[768,768]{1,0:T(8,128)(2,1)}, bf16[768,768]{1,0:T(8,128)(2,1)}, u32[]{:S(2)}, u32[]{:S(2)}) collective-permute-start(bf16[768,768]{1,0:T(8,128)(2,1)} %get-tuple-element.133.wout_a), channel_id=1, source_target_pairs={{0,8},{8,0},{16,24},{24,16},{1,9},{9,1},{17,25},{25,17},{2,10},{10... | collective-permute-start | bytes 3538952 | tf_op jit(solution)/shard_map/ppermute | solution.py:35
  332.6 103.6 %all-to-all-start.5 = ((bf16[2,8,64,768]{3,2,0,1:T(8,128)(2,1)}), bf16[2,8,64,768]{3,2,0,1:T(8,128)(2,1)}, u32[]{:S(2)}, u32[]{:S(2)}) async-start(bf16[2,8,64,768]{3,2,0,1:T(8,128)(2,1)} %pad_maximum_fusion.8), calls=%async_computation.5 | async-start | bytes 3145728 | tf_op jit(solution)/shard_map/all_to_all | solution.py:92
  410.7 74.1 %collective-permute-start.21 = (bf16[784,768]{1,0:T(8,128)(2,1)}, bf16[784,768]{1,0:T(8,128)(2,1)}, u32[]{:S(2)}, u32[]{:S(2)}) collective-permute-start(bf16[784,768]{1,0:T(8,128)(2,1)} %pad_maximum_fusion.13.win_a), channel_id=1, source_target_pairs={{0,16},{8,24},{16,0},{24,8},{1,17},{9,25},{17,1},{25,9},{2,18},{10... | collective-permute-start | bytes 3612680 | tf_op jit(solution)/shard_map/ppermute | solution.py:35
  413.9 69.3 %collective-permute-start.22 = (bf16[768,768]{1,0:T(8,128)(2,1)}, bf16[768,768]{1,0:T(8,128)(2,1)}, u32[]{:S(2)}, u32[]{:S(2)}) collective-permute-start(bf16[768,768]{1,0:T(8,128)(2,1)} %get-tuple-element.134.wout_a), channel_id=1, source_target_pairs={{0,16},{8,24},{16,0},{24,8},{1,17},{9,25},{17,1},{25,9},{2,18},{10... | collective-permute-start | bytes 3538952 | tf_op jit(solution)/shard_map/ppermute | solution.py:35
  415.5 100.2 %collective-permute-start.38 = (f32[32]{0:T(128)S(1)}, f32[32]{0:T(128)S(1)}, u32[]{:S(2)}, u32[]{:S(2)}) collective-permute-start(f32[32]{0:T(128)S(1)} %add.372), channel_id=1, source_target_pairs={{0,4},{1,5},{2,6},{3,7},{4,0},{5,1},{6,2},{7,3},{8,12},{9,13},{10,... | collective-permute-start | bytes 392 | tf_op jit(solution)/shard_map/ppermute | solution.py:35
  417.9 66.9 %collective-permute-start.20 = (bf16[1,512,768]{2,1,0:T(8,128)(2,1)}, bf16[1,512,768]{2,1,0:T(8,128)(2,1)}, u32[]{:S(2)}, u32[]{:S(2)}) collective-permute-start(bf16[1,512,768]{2,1,0:T(8,128)(2,1)} %bitcast.50), channel_id=1, source_target_pairs={{0,8},{8,0},{16,24},{24,16},{1,9},{9,1},{17,25},{25,17},{2,10},{10... | collective-permute-start | bytes 2359304 | tf_op jit(solution)/shard_map/ppermute | solution.py:35
  436.2 128.4 %all-to-all-start.7 = ((bf16[2,8,64,768]{3,2,0,1:T(8,128)(2,1)}), bf16[2,8,64,768]{3,2,0,1:T(8,128)(2,1)}, u32[]{:S(2)}, u32[]{:S(2)}) async-start(bf16[2,8,64,768]{3,2,0,1:T(8,128)(2,1)} %pad_maximum_fusion.10), calls=%async_computation.7 | async-start | bytes 3145728 | tf_op jit(solution)/shard_map/all_to_all | solution.py:92
  517.5 59.9 %collective-permute-start.63 = (bf16[768,768]{1,0:T(8,128)(2,1)}, bf16[768,768]{1,0:T(8,128)(2,1)}, u32[]{:S(2)}, u32[]{:S(2)}) collective-permute-start(bf16[768,768]{1,0:T(8,128)(2,1)} %get-tuple-element.93), channel_id=1, source_target_pairs={{0,8},{8,0},{16,24},{24,16},{1,9},{9,1},{17,25},{25,17},{2,10},{10... | collective-permute-start | bytes 3538952 | tf_op jit(solution)/shard_map/ppermute | solution.py:35
  518.0 62.1 %collective-permute-start.64 = (bf16[768,768]{1,0:T(8,128)(2,1)}, bf16[768,768]{1,0:T(8,128)(2,1)}, u32[]{:S(2)}, u32[]{:S(2)}) collective-permute-start(bf16[768,768]{1,0:T(8,128)(2,1)} %get-tuple-element.95), channel_id=1, source_target_pairs={{0,16},{8,24},{16,0},{24,8},{1,17},{9,25},{17,1},{25,9},{2,18},{10... | collective-permute-start | bytes 3538952 | tf_op jit(solution)/shard_map/ppermute | solution.py:35
  522.5 50.8 %collective-permute-start.40 = (bf16[512,768]{1,0:T(8,128)(2,1)}, bf16[512,768]{1,0:T(8,128)(2,1)}, u32[]{:S(2)}, u32[]{:S(2)}) collective-permute-start(bf16[512,768]{1,0:T(8,128)(2,1)} %get-tuple-element.70), channel_id=1, source_target_pairs={{0,8},{8,0},{16,24},{24,16},{1,9},{9,1},{17,25},{25,17},{2,10},{10... | collective-permute-start | bytes 2359304 | tf_op jit(solution)/shard_map/ppermute | solution.py:35
  534.9 88.0 %collective-permute-start.60 = (bf16[784,768]{1,0:T(8,128)(2,1)}, bf16[784,768]{1,0:T(8,128)(2,1)}, u32[]{:S(2)}, u32[]{:S(2)}) collective-permute-start(bf16[784,768]{1,0:T(8,128)(2,1)} %get-tuple-element.87), channel_id=1, source_target_pairs={{0,16},{8,24},{16,0},{24,8},{1,17},{9,25},{17,1},{25,9},{2,18},{10... | collective-permute-start | bytes 3612680 | tf_op jit(solution)/shard_map/ppermute | solution.py:35
  564.1 51.1 %collective-permute-start.62 = (bf16[768,768]{1,0:T(8,128)(2,1)}, bf16[768,768]{1,0:T(8,128)(2,1)}, u32[]{:S(2)}, u32[]{:S(2)}) collective-permute-start(bf16[768,768]{1,0:T(8,128)(2,1)} %get-tuple-element.91), channel_id=1, source_target_pairs={{0,16},{8,24},{16,0},{24,8},{1,17},{9,25},{17,1},{25,9},{2,18},{10... | collective-permute-start | bytes 3538952 | tf_op jit(solution)/shard_map/ppermute | solution.py:35
  564.6 59.1 %all-to-all-start.2 = ((bf16[2,8,64,768]{3,2,0,1:T(8,128)(2,1)}), bf16[2,8,64,768]{3,2,0,1:T(8,128)(2,1)}, u32[]{:S(2)}, u32[]{:S(2)}) async-start(bf16[2,8,64,768]{3,2,0,1:T(8,128)(2,1)} %pad_maximum_fusion.7), calls=%async_computation.2 | async-start | bytes 3145728 | tf_op jit(solution)/shard_map/all_to_all | solution.py:92
  577.4 50.7 %collective-permute-start.59 = (bf16[784,768]{1,0:T(8,128)(2,1)}, bf16[784,768]{1,0:T(8,128)(2,1)}, u32[]{:S(2)}, u32[]{:S(2)}) collective-permute-start(bf16[784,768]{1,0:T(8,128)(2,1)} %get-tuple-element.85), channel_id=1, source_target_pairs={{0,8},{8,0},{16,24},{24,16},{1,9},{9,1},{17,25},{25,17},{2,10},{10... | collective-permute-start | bytes 3612680 | tf_op jit(solution)/shard_map/ppermute | solution.py:35
  580.1 56.5 %collective-permute-start.58 = (bf16[784,768]{1,0:T(8,128)(2,1)}, bf16[784,768]{1,0:T(8,128)(2,1)}, u32[]{:S(2)}, u32[]{:S(2)}) collective-permute-start(bf16[784,768]{1,0:T(8,128)(2,1)} %get-tuple-element.83), channel_id=1, source_target_pairs={{0,16},{8,24},{16,0},{24,8},{1,17},{9,25},{17,1},{25,9},{2,18},{10... | collective-permute-start | bytes 3612680 | tf_op jit(solution)/shard_map/ppermute | solution.py:35
  623.7 55.8 %all-to-all-start.6 = ((bf16[2,8,64,768]{3,2,0,1:T(8,128)(2,1)}), bf16[2,8,64,768]{3,2,0,1:T(8,128)(2,1)}, u32[]{:S(2)}, u32[]{:S(2)}) async-start(bf16[2,8,64,768]{3,2,0,1:T(8,128)(2,1)} %pad_maximum_fusion.9), calls=%async_computation.6 | async-start | bytes 3145728 | tf_op jit(solution)/shard_map/all_to_all | solution.py:92
  (110 other events, 1550.3 us)

commit v2 on v1

v2 whole, which is shorter than its diff:
```python
import functools

import jax
import jax.numpy as jnp
from jax import lax
from jax.experimental import pallas as pl
from jax.experimental.pallas import tpu as pltpu
from jax.sharding import PartitionSpec as P

HEAD = 64
LANES = 128
REACH = 384
QROWS = 256
EPSILON = 1e-05
BALANCE = 0.01
ALL = ("batch", "expert")
VMEM = 60 * 1024 * 1024
COST = pl.CostEstimate(flops=1, bytes_accessed=1, transcendentals=0)
F32 = jnp.float32
BF16 = jnp.bfloat16


def dot(a, b):
    return jnp.dot(a, b, preferred_element_type=F32)


def dot_nt(a, b):
    return lax.dot_general(a, b, (((1,), (1,)), ((), ())), preferred_element_type=F32)


def dot_tn(a, b):
    return lax.dot_general(a, b, (((0,), (0,)), ((), ())), preferred_element_type=F32)


def swap(x, axis, mask):
    return lax.ppermute(x, axis, [(i, i ^ mask) for i in range(lax.axis_size(axis))])


def shift(x, step):
    size = lax.axis_size("expert")
    return lax.ppermute(x, "expert", [(i, (i + step) % size) for i in range(size)])


def staged():
    return lax.axis_size("batch") == 4 and lax.axis_size("expert") == 8


def gather_first(x):
    mz = lax.axis_index("expert") // 2
    ring = [shift(x, 2 * k) for k in (3, 2, 1)] + [x]
    ring = jnp.stack(ring + ring[:3])
    return lax.dynamic_slice_in_dim(ring, 3 - mz, 4, 0)


def gather_second(zs, beside):
    mb = lax.axis_index("batch")
    b = after([zs] + [swap(zs, "batch", k) for k in (1, 2, 3)], beside)
    odd, high = (mb & 1) == 1, (mb & 2) == 2
    u = [jnp.where(odd, b[i ^ 1], b[i]) for i in range(4)]
    return jnp.stack([jnp.where(high, u[i ^ 2], u[i]) for i in range(4)])


def gather_third(rows, beside=()):
    mc = lax.axis_index("expert") % 2
    other = after(swap(rows, "expert", 1), beside)
    both = jnp.stack(
        [jnp.where(mc == 0, rows, other), jnp.where(mc == 0, other, rows)], axis=2
    )
    return both.reshape(-1, rows.shape[-1])


def scatter_rows(g, before, beside):
    if not staged():
        return lax.psum_scatter(g, ALL, scatter_dimension=0, tiled=True).astype(F32), beside(before)
    mb, me = lax.axis_index("batch"), lax.axis_index("expert")
    mz, mc = me // 2, me % 2
    r, c = g.shape[0] // 32, g.shape[1]
    g = g.reshape(4, 4, 2, r, c)
    mine = jnp.where(mc == 0, g[:, :, 0], g[:, :, 1])
    other = swap(jnp.where(mc == 0, g[:, :, 1], g[:, :, 0]), "expert", 1)
    s = (mine.astype(F32) + other.astype(F32)).astype(BF16)
    s, before = after((s, before), before)
    made = beside(after(before, s))
    pick = lambda t, i: lax.dynamic_index_in_dim(t, i, 0, keepdims=False)
    parts = after([swap(pick(s, mb ^ k), "batch", k) for k in (1, 2, 3)], made)
    t = sum((p.astype(F32) for p in parts), pick(s, mb).astype(F32)).astype(BF16)
    parts = [shift(pick(t, (mz + k) % 4), 2 * k) for k in (1, 2, 3)]
    return sum((p.astype(F32) for p in parts), pick(t, mz).astype(F32)), made


def to_owners(x):
    return lax.all_to_all(x, "expert", split_axis=0, concat_axis=0, tiled=True)


def after(x, *others):
    return lax.optimization_barrier((x, others))[0]


def windows(length):
    for start in range(0, length, QROWS):
        yield start, max(0, start - REACH), start + QROWS


def half_masks():
    lane = lax.broadcasted_iota(jnp.int32, (1, LANES), 1)
    first = (lane < HEAD).astype(F32)
    return first, (first.astype(BF16), (1.0 - first).astype(BF16))


def attend_kernel(q_ref, k_ref, v_ref, row_ref, col_ref, out_ref, log_ref, mask_ref):
    length = q_ref.shape[0]

    @pl.when(pl.program_id(0) == 0)
    def _():
        for n, (start, low, stop) in enumerate(windows(length)):
            shape = (QROWS, stop - low)
            i = lax.broadcasted_iota(jnp.int32, shape, 0) + start
            j = lax.broadcasted_iota(jnp.int32, shape, 1) + low
            same = col_ref[start:stop, :] == row_ref[:, low:stop]
            mask_ref[n, :, : stop - low] = jnp.where((j <= i) & same, 0.0, -1e30)

    first, halves = half_masks()
    for n, (start, low, stop) in enumerate(windows(length)):
        q = q_ref[start:stop, :] * jnp.asarray(HEAD**-0.5, BF16)
        k, v = k_ref[low:stop, :], v_ref[low:stop, :]
        outs, logs = [], []
        for half in halves:
            s = dot_nt(q * half, k) + mask_ref[n, :, : stop - low]
            top = jnp.max(s, axis=1, keepdims=True)
            e = jnp.exp(s - top)
            sums = jnp.sum(e, axis=1, keepdims=True)
            outs.append(dot(e.astype(BF16), v) / sums)
            logs.append(top + jnp.log(sums))
        out_ref[start:stop, :] = (outs[0] * first + outs[1] * (1.0 - first)).astype(BF16)
        log_ref[start:stop, :] = logs[0] * first + logs[1] * (1.0 - first)


def attend(qkv, seg_row, seg_col, width):
    length = qkv.shape[0]
    pairs = width // LANES
    spec = lambda offset: pl.BlockSpec((length, LANES), lambda p, o=offset: (0, o + p))
    whole = lambda shape: pl.BlockSpec(shape, lambda p: (0,) * len(shape))
    return pl.pallas_call(
        attend_kernel,
        grid=(pairs,),
        in_specs=[spec(0), spec(pairs), spec(2 * pairs), whole((1, length)), whole((length, 1))],
        out_specs=[spec(0), spec(0)],
        out_shape=[
            jax.ShapeDtypeStruct((length, width), BF16),
            jax.ShapeDtypeStruct((length, width), F32),
        ],
        scratch_shapes=[pltpu.VMEM((length // QROWS, QROWS, QROWS + REACH), F32)],
        compiler_params=pltpu.CompilerParams(vmem_limit_bytes=VMEM),
        cost_estimate=pl.CostEstimate(
            flops=4 * length * 512 * width, bytes_accessed=12 * length * width, transcendentals=12 * length * 512
        ),
        name="attend",
    )(qkv, qkv, qkv, seg_row, seg_col)


def attend_back_kernel(
    q_ref, k_ref, v_ref, g_ref, log_ref, row_ref, col_ref, out_ref, mask_ref, dk_ref, dv_ref
):
    length = q_ref.shape[0]

    @pl.when(pl.program_id(0) == 0)
    def _():
        for n, (start, low, stop) in enumerate(windows(length)):
            shape = (stop - low, QROWS)
            j = lax.broadcasted_iota(jnp.int32, shape, 0) + low
            i = lax.broadcasted_iota(jnp.int32, shape, 1) + start
            same = col_ref[low:stop, :] == row_ref[:, start:stop]
            mask_ref[n, : stop - low, :] = jnp.where((j <= i) & same, 0.0, -1e30)

    dk_ref[...] = jnp.zeros_like(dk_ref)
    dv_ref[...] = jnp.zeros_like(dv_ref)
    _, halves = half_masks()
    scale = HEAD**-0.5
    for n, (start, low, stop) in enumerate(windows(length)):
        q = q_ref[start:stop, :] * jnp.asarray(scale, BF16)
        g = g_ref[start:stop, :]
        k, v = k_ref[low:stop, :], v_ref[low:stop, :]
        logs = log_ref[start:stop, :].T
        dq = jnp.zeros((QROWS, LANES), F32)
        for at, half in zip((0, HEAD), halves):
            qh, gh = q * half, g * half
            s = dot_nt(k, qh) + mask_ref[n, : stop - low, :]
            p = jnp.exp(s - logs[at : at + 1, :])
            dp = dot_nt(v, gh)
            centre = jnp.sum(dp * p, axis=0, keepdims=True)
            ds = (p * (dp - centre)).astype(BF16)
            dv_ref[low:stop, :] += dot(p.astype(BF16), gh)
            dk_ref[low:stop, :] += dot(ds, qh)
            dq += dot_tn(ds, k * half)
        out_ref[0, start:stop, :] = (dq * scale).astype(BF16)
    out_ref[1] = dk_ref[...].astype(BF16)
    out_ref[2] = dv_ref[...].astype(BF16)


def attend_back(qkv, grad, logs, seg_row, seg_col, width):
    length = qkv.shape[0]
    pairs = width // LANES
    spec = lambda offset: pl.BlockSpec((length, LANES), lambda p, o=offset: (0, o + p))
    whole = lambda shape: pl.BlockSpec(shape, lambda p: (0,) * len(shape))
    return pl.pallas_call(
        attend_back_kernel,
        grid=(pairs,),
        in_specs=[spec(0), spec(pairs), spec(2 * pairs), spec(0), spec(0), whole((1, length)), whole((length, 1))],
        out_specs=pl.BlockSpec((3, length, LANES), lambda p: (0, 0, p)),
        out_shape=jax.ShapeDtypeStruct((3, length, width), BF16),
        scratch_shapes=[
            pltpu.VMEM((length // QROWS, QROWS + REACH, QROWS), F32),
            pltpu.VMEM((length, LANES), F32),
            pltpu.VMEM((length, LANES), F32),
        ],
        compiler_params=pltpu.CompilerParams(vmem_limit_bytes=VMEM),
        cost_estimate=COST,
        name="attend_back",
    )(qkv, qkv, qkv, grad, logs, seg_row, seg_col)


def slot_ids(shape, axis, base, layout, first):
    groups, chunk, split, slots = layout
    at = lax.broadcasted_iota(jnp.int32, shape, axis) + base
    row, slot = at // slots, at % slots
    return (row // chunk * groups + first + row % chunk) // split * slots + slot


def dispatch_kernel(layout, first, id_ref, x_ref, out_ref):
    rows, tokens = out_ref.shape[0], x_ref.shape[0]
    ids = slot_ids((rows, 1), 0, pl.program_id(0) * rows, layout, first)
    chosen = jnp.where(ids == id_ref[...], 1.0, 0.0).astype(BF16)
    out_ref[...] = dot(chosen, x_ref[...]).astype(BF16)


def dispatch(ids, x, count, layout, first):
    tokens, width = x.shape
    block = min(count, 512)
    return pl.pallas_call(
        functools.partial(dispatch_kernel, layout, first),
        grid=(count // block,),
        in_specs=[
            pl.BlockSpec((1, tokens), lambda i: (0, 0)),
            pl.BlockSpec((tokens, width), lambda i: (0, 0)),
        ],
        out_specs=pl.BlockSpec((block, width), lambda i: (i, 0)),
        out_shape=jax.ShapeDtypeStruct((count, width), BF16),
        compiler_params=pltpu.CompilerParams(vmem_limit_bytes=VMEM),
        cost_estimate=pl.CostEstimate(
            flops=2 * count * tokens * width, bytes_accessed=4 * count * width, transcendentals=0
        ),
        name="dispatch",
    )(ids, x)


def combine_kernel(layout, firsts, id_ref, *refs):
    *x_refs, out_ref = refs
    out_ref[...] = jnp.zeros_like(out_ref)
    for first, x_ref in zip(firsts, x_refs):
        step = min(x_ref.shape[0], 512)
        for base in range(0, x_ref.shape[0], step):
            ids = slot_ids((1, step), 1, base, layout, first)
            chosen = jnp.where(id_ref[...] == ids, 1.0, 0.0).astype(BF16)
            out_ref[...] += dot(chosen, x_ref[base : base + step, :])


def combine(ids, xs, layout, firsts):
    tokens, (count, width), block = ids.shape[0], xs[0].shape, 256
    return pl.pallas_call(
        functools.partial(combine_kernel, layout, firsts),
        grid=(tokens // block,),
        in_specs=[pl.BlockSpec((block, 1), lambda i: (i, 0))]
        + [pl.BlockSpec((count, width), lambda i: (0, 0)) for _ in xs],
        out_specs=pl.BlockSpec((block, width), lambda i: (i, 0)),
        out_shape=jax.ShapeDtypeStruct((tokens, width), F32),
        compiler_params=pltpu.CompilerParams(vmem_limit_bytes=VMEM),
        cost_estimate=pl.CostEstimate(
            flops=2 * count * len(xs) * tokens * width,
            bytes_accessed=2 * count * len(xs) * width + 4 * tokens * width,
            transcendentals=0,
        ),
        name="combine",
    )(ids, *xs)


def merge_kernel(*refs):
    *parts, out_ref = refs
    owners, chunk, slots, width = out_ref.shape
    for l in range(chunk):
        both = parts[2 * l][...].astype(F32) + parts[2 * l + 1][...].astype(F32)
        out_ref[:, l] = both.astype(BF16).reshape(owners, slots, width)


def merge(pairs, owners, slots):
    rows, width = pairs[0][0].shape
    block = min(owners, 4)
    flat = [part for pair in pairs for part in pair]
    return pl.pallas_call(
        merge_kernel,
        grid=(owners // block,),
        in_specs=[pl.BlockSpec((block * slots, width), lambda i: (i, 0)) for _ in flat],
        out_specs=pl.BlockSpec((block, len(pairs), slots, width), lambda i: (i, 0, 0, 0)),
        out_shape=jax.ShapeDtypeStruct((owners, len(pairs), slots, width), BF16),
        compiler_params=pltpu.CompilerParams(vmem_limit_bytes=VMEM),
        cost_estimate=pl.CostEstimate(
            flops=len(flat) * rows * width, bytes_accessed=3 * len(flat) * rows * width, transcendentals=0
        ),
        name="merge",
    )(*flat)


def gelu_parts(x):
    size = jnp.abs(x)
    t = 1.0 / (1.0 + (0.3275911 * 0.5**0.5) * size)
    bell = jnp.exp(-0.5 * x * x)
    poly = t * (
        0.5 * 0.254829592
        + t * (0.5 * -0.284496736 + t * (0.5 * 1.421413741 + t * (0.5 * -1.453152027 + t * (0.5 * 1.061405429))))
    )
    tail = poly * bell
    return jnp.where(x < 0, tail, 1.0 - tail), bell * 0.3989422804014327


def expert_kernel(steps, experts, n, *refs):
    id_ref, h0, h1, z0, z1 = refs[:5]
    weights = refs[5:8], refs[8:11]
    wr_ref, p0, p1, d0, d1 = refs[11:16]
    own_g, got_g = refs[16 : 16 + n], refs[16 + n : 16 + 2 * n]
    refs = refs[16 + 2 * n :]
    groute, hid_a, hid_b, dpre_a, dpre_b, dexp_s, *sums = refs
    i = pl.program_id(0)
    width = wr_ref.shape[0]
    slots = h0.shape[2]
    rows = h0.shape[0] * slots
    sub = min(h0.shape[0], 4)
    hidden = hid_a.shape[1]

    def parts(w):
        if n == 1:
            return w[0].at[0, :width], w[0].at[0, width : 2 * width], w[0].at[0, 2 * width :]
        return w[0].at[0, :width], w[1].at[0], w[0].at[0, width:]

    @pl.when(i == 0)
    def _():
        groute[...] = jnp.zeros_like(groute)
        for total_ref in sums:
            total_ref[...] = jnp.zeros_like(total_ref)

    def work(h_ref, z_ref, p_ref, d_ref):
        lane = lax.broadcasted_iota(jnp.int32, (1, LANES), 1)
        own = (lane == id_ref[0]).astype(F32)

        def block(m, _):
            part = pl.ds(m * sub, sub)
            at = pl.ds(pl.multiple_of(m * sub * slots, sub * slots), sub * slots)
            h = h_ref[part, 0].reshape(sub * slots, width)
            logits = jnp.where(lane < experts, dot(h, wr_ref[...]), -1e30)
            e = jnp.exp(logits - jnp.max(logits, axis=1, keepdims=True))
            probs = e / jnp.sum(e, axis=1, keepdims=True)
            gate = jnp.sum(probs * own, axis=1, keepdims=True)
            dz = z_ref[part, 0].reshape(sub * slots, width).astype(F32)
            dexp = (gate * dz).astype(BF16)
            dexp_s[at, :] = dexp
            piece = back = None
            for (win, wout, bias), hid_s, dpre_s in zip(weights, (hid_a, hid_b), (dpre_a, dpre_b)):
                pre = dot(h, win[...]) + bias[...].astype(F32)
                phi, bell = gelu_parts(pre)
                hid = (pre * phi).astype(BF16)
                hid_s[at, :] = hid
                out = dot(hid, wout[...])
                piece = out if piece is None else piece + out
                dpre = (dot_nt(dexp, wout[...]) * (phi + pre * bell)).astype(BF16)
                dpre_s[at, :] = dpre
                out = dot_nt(dpre, win[...])
                back = out if back is None else back + out
            p_ref[at, :] = piece.astype(BF16)
            dgate = jnp.sum(dz * piece, axis=1, keepdims=True)
            dlog = (dgate * probs * (own - gate)).astype(BF16)
            d_ref[at, :] = (back + dot_nt(dlog, wr_ref[...])).astype(BF16)
            groute[...] += dot_tn(h, dlog)
            return 0

        lax.fori_loop(0, h_ref.shape[0] // sub, block, 0)
        for k, (dpre_s, hid_s) in enumerate(((dpre_a, hid_a), (dpre_b, hid_b))):
            to_win, to_bias, to_wout = sums[3 * k : 3 * k + 3]
            dpre = dpre_s[...]
            to_win[...] += dot_tn(h_ref[...].reshape(rows, width), dpre)
            to_bias[...] += jnp.broadcast_to(jnp.sum(dpre.astype(F32), axis=0, keepdims=True), to_bias.shape)
            to_wout[...] += dot_tn(hid_s[...], dexp_s[...])

    @pl.when(i < steps)
    def _():
        work(h0, z0, p0, d0)

    @pl.when(i >= steps)
    def _():
        work(h1, z1, p1, d1)

    @pl.when(i == 2 * steps - 1)
    def _():
        for k, g in enumerate((own_g, got_g)):
            win, wout, bias = parts(g)
            win[...] = sums[3 * k][...].astype(BF16)
            bias[...] = sums[3 * k + 1][...].astype(BF16)
            wout[...] = sums[3 * k + 2][...].astype(BF16)


def expert(expert_id, own_h, other_h, own_z, other_z, places, own_w, got_w, at, w_route, experts):
    sources, _, slots, width = own_h.shape
    rows = sources * slots
    hidden = own_w[0].shape[2]
    group = min(sources, 8)
    block, steps = group * slots, sources // group
    early = lambda i: jnp.minimum(i, steps - 1)
    late = lambda i: jnp.maximum(i - steps, 0)
    once = lambda shape: pl.BlockSpec(shape, lambda i: (0,) * len(shape))
    rows_spec = lambda place, when: pl.BlockSpec((group, 1, slots, width), lambda i: (when(i), place, 0, 0))
    weight = lambda w, k: pl.BlockSpec((None, *w.shape[1:]), lambda i: (k, 0, 0))
    out_first = pl.BlockSpec((block, width), lambda i: (early(i), 0))
    out_second = pl.BlockSpec((block, width), lambda i: (late(i), 0))
    shape = jax.ShapeDtypeStruct
    if hidden == width:
        grads = [shape((1, 2 * width + 16, hidden), BF16)]
    else:
        grads = [shape((1, width + 16, hidden), BF16), shape((1, hidden, width), BF16)]
    outs = [shape((rows, width), BF16)] * 4 + grads * 2 + [shape((width, LANES), F32)]
    spots = (own_h, other_h, own_z, other_z)
    return pl.pallas_call(
        functools.partial(expert_kernel, steps, experts, len(grads)),
        grid=(2 * steps,),
        in_specs=[pl.BlockSpec(memory_space=pltpu.SMEM)]
        + [rows_spec(p, w) for p, w in zip(places, (early, late, early, late))]
        + [weight(w, k) for w, k in zip((*own_w, *got_w), at)]
        + [once(w_route.shape)],
        out_specs=[out_first, out_second, out_first, out_second] + [once(o.shape) for o in outs[4:]],
        out_shape=outs,
        scratch_shapes=[
            *[pltpu.VMEM((block, hidden), BF16)] * 4,
            pltpu.VMEM((block, width), BF16),
            *[pltpu.VMEM(s, F32) for s in ((width, hidden), (16, hidden), (hidden, width))] * 2,
        ],
        compiler_params=pltpu.CompilerParams(vmem_limit_bytes=VMEM),
        cost_estimate=pl.CostEstimate(
            flops=48 * rows * hidden * width, bytes_accessed=20 * width * hidden, transcendentals=4 * rows * hidden
        ),
        name="expert",
    )(expert_id, *spots, *own_w, *got_w, w_route)


def finish_kernel(n, *refs):
    parts, (win, wout, bias) = refs[: 6 * n], refs[-3:]
    for l in range(n):
        for k, out in enumerate((win, wout, bias)):
            out[l] = parts[6 * l + k][...].astype(F32) + parts[6 * l + 3 + k][...].astype(F32)


def finish(own, got):
    n, (_, height, hidden) = len(own), own[0].shape
    width = (height - 16) // 2
    tile = 128
    steps = width // tile
    spec = lambda r, k: pl.BlockSpec((None, r, hidden), lambda i: (0, k(i), 0))
    three = [spec(tile, lambda i: i), spec(tile, lambda i: steps + i), spec(16, lambda i: 2 * width // 16)]
    flat = [x for pair in zip(own, got) for a in pair for x in (a, a, a)]
    big = pl.BlockSpec((n, tile, hidden), lambda i: (0, i, 0))
    shape = jax.ShapeDtypeStruct
    return pl.pallas_call(
        functools.partial(finish_kernel, n),
        grid=(steps,),
        in_specs=three * (2 * n),
        out_specs=[big, big, pl.BlockSpec((n, 16, hidden), lambda i: (0, 0, 0))],
        out_shape=[shape((n, width, hidden), F32), shape((n, width, hidden), F32), shape((n, 16, hidden), F32)],
        compiler_params=pltpu.CompilerParams(vmem_limit_bytes=VMEM),
        cost_estimate=pl.CostEstimate(
            flops=2 * n * height * hidden, bytes_accessed=8 * n * height * hidden, transcendentals=0
        ),
        name="finish",
    )(*flat)


def to_send_kernel(in_ref, out_ref, *refs):
    for l in range(in_ref.shape[0]):
        refs[2 * l][0] = in_ref[l]
        refs[2 * l + 1][0] = out_ref[l]


def to_send(w_in, w_out):
    groups = w_in.shape[0]
    steps = w_in.shape[1] // 128
    spec = lambda a, k: pl.BlockSpec((k, a.shape[1] // steps, a.shape[2]), lambda i: (0, i, 0))
    flat = pl.pallas_call(
        to_send_kernel,
        grid=(steps,),
        in_specs=[spec(w_in, groups), spec(w_out, groups)],
        out_specs=[spec(w_in, 1), spec(w_out, 1)] * groups,
        out_shape=[jax.ShapeDtypeStruct((1, *a.shape[1:]), BF16) for a in (w_in, w_out)] * groups,
        compiler_params=pltpu.CompilerParams(vmem_limit_bytes=VMEM),
        name="to_send",
    )(w_in, w_out)
    return [flat[2 * l : 2 * l + 2] for l in range(groups)]


def turn_kernel(x_ref, y_ref, x_out, y_out):
    x_out[...] = x_ref[...].T
    y_out[...] = y_ref[...].T


def turn(x, y):
    whole = lambda a, b: pl.BlockSpec((a, b), lambda i: (0, 0))
    tokens, width = x.shape
    return pl.pallas_call(
        turn_kernel,
        grid=(1,),
        in_specs=[whole(tokens, width)] * 2,
        out_specs=[whole(width, tokens)] * 2,
        out_shape=[jax.ShapeDtypeStruct((width, tokens), x.dtype)] * 2,
        compiler_params=pltpu.CompilerParams(vmem_limit_bytes=VMEM),
        name="turn",
    )(x, y)


def outer_kernel(h_ref, a_ref, g_ref, b_ref, rest_ref, sums_ref, out_ref):
    width = b_ref.shape[1]
    for k in range(3):
        out_ref[:, k * width : (k + 1) * width] = dot(h_ref[...], g_ref[k]).astype(BF16)
    out_ref[:, 3 * width : 4 * width] = dot(a_ref[...], b_ref[...]).astype(BF16)
    out_ref[:, 4 * width : 4 * width + LANES] = rest_ref[...]
    out_ref[:, 4 * width + LANES :] = sums_ref[...].T.astype(BF16)


def outer(h, a, g, b, rest, sums):
    width, tokens = h.shape
    tile = 256
    whole = lambda *shape: pl.BlockSpec(shape, lambda i: (0,) * len(shape))
    rows = lambda n: pl.BlockSpec((tile, n), lambda i: (i, 0))
    columns = 4 * width + 2 * LANES
    return pl.pallas_call(
        outer_kernel,
        grid=(width // tile,),
        in_specs=[
            rows(tokens), rows(tokens), whole(3, tokens, width), whole(tokens, width), rows(LANES),
            pl.BlockSpec((LANES, tile), lambda i: (0, i)),
        ],
        out_specs=rows(columns),
        out_shape=jax.ShapeDtypeStruct((width, columns), BF16),
        compiler_params=pltpu.CompilerParams(vmem_limit_bytes=VMEM),
        cost_estimate=COST,
        name="outer",
    )(h, a, g, b, rest, sums)


def input_kernel(g_ref, w_ref, x_ref, dy_ref, gain_ref, out_ref, sums_ref):
    width = x_ref.shape[1]

    @pl.when(pl.program_id(0) == 0)
    def _():
        sums_ref[...] = jnp.zeros_like(sums_ref)

    grad = dot_nt(g_ref[0], w_ref[:, :width])
    for k in (1, 2):
        grad += dot_nt(g_ref[k], w_ref[:, k * width : (k + 1) * width])
    unit, rstd = normed(x_ref[...].astype(F32))
    out_ref[...] = dy_ref[...] + norm_back(grad, gain_ref[...], unit, rstd)
    add = lambda t: jnp.sum(t, axis=0, keepdims=True)
    sums_ref[0:1, :] += add(grad * unit)
    sums_ref[1:2, :] += add(grad)
    sums_ref[2:3, :] += add(g_ref[0].astype(F32))
    sums_ref[3:4, :] += add(g_ref[2].astype(F32))


def input_back(g, wide, tokens, dy, gain):
    count, width = tokens.shape
    tile = 256
    rows = pl.BlockSpec((tile, width), lambda i: (i, 0))
    whole = lambda *shape: pl.BlockSpec(shape, lambda i: (0,) * len(shape))
    return pl.pallas_call(
        input_kernel,
        grid=(count // tile,),
        in_specs=[
            pl.BlockSpec((3, tile, width), lambda i: (0, i, 0)), whole(*wide.shape), rows, rows, whole(1, width),
        ],
        out_specs=[rows, whole(LANES, width)],
        out_shape=[jax.ShapeDtypeStruct((count, width), F32), jax.ShapeDtypeStruct((LANES, width), F32)],
        compiler_params=pltpu.CompilerParams(vmem_limit_bytes=VMEM),
        cost_estimate=COST,
        name="input_back",
    )(g, wide, tokens, dy, gain)


def normed(x):
    centred = x - jnp.mean(x, axis=-1, keepdims=True)
    rstd = lax.rsqrt(jnp.mean(centred * centred, axis=-1, keepdims=True) + EPSILON)
    return centred * rstd, rstd


def norm_back(grad, gain, unit, rstd):
    g = grad * gain
    mean = lambda t: jnp.mean(t, axis=-1, keepdims=True)
    return rstd * (g - mean(g) - unit * mean(g * unit))


def pad_columns(x, count):
    return jnp.pad(x, ((0, 0), (0, count - x.shape[1])))


def up(count):
    return -(-count // LANES) * LANES


def local(
    tokens, cotangent, segment_ids, routes, capacity, ln1_gain, ln1_bias, w_query, b_query, w_key, w_value,
    b_value, w_output, b_output, ln2_gain, ln2_bias, w_router, w_in, b_in, w_out, b_out,
):
    row_count, width = tokens.shape
    experts = capacity.shape[0]
    slots = 2 * row_count // experts
    groups = w_in.shape[0]
    owners = lax.axis_size("expert")
    split = groups * owners // experts
    share = w_query.shape[0]
    devices = lax.axis_size("batch") * owners
    me = lax.axis_index("expert")
    chunk = min(2, groups)
    layout = (groups, chunk, split, slots)
    firsts = tuple(range(0, groups, chunk))
    pair = lambda first: range(first, first + chunk)
    heavy = lambda l: 1 if l % 2 == 0 else 2
    light = lambda l: 3 - heavy(l)

    spread = -(-experts // share)
    fold = lambda x: jnp.pad(x, (0, spread * share - experts)).reshape(spread, share).T
    unfold = lambda x: x.T.reshape(-1)[:experts]

    chosen = routes[:, 0]
    picked = chosen[:, None] == jnp.arange(experts, dtype=jnp.int32)[None, :]
    picked_float = picked.astype(F32)
    position = jnp.arange(row_count, dtype=jnp.int32)
    earlier = (position[None, :] < position[:, None]).astype(BF16)
    rank = dot(earlier, picked.astype(BF16))
    slot = jnp.sum(rank * picked_float, axis=1)
    limit = jnp.sum(capacity.astype(F32)[None, :] * picked_float, axis=1)
    kept = slot < limit
    kept_float = kept.astype(F32)
    ids = jnp.where(kept, chosen * slots + slot.astype(jnp.int32), -1)
    id_row, id_col = ids[None, :], ids[:, None]
    counts = jnp.sum(picked_float, axis=0)

    def send(x, first, count):
        rows = dispatch(id_row, x, count * owners * slots, (groups, count, split, slots), first)
        return rows.reshape(owners, count, slots, width)

    grad_send = send(cotangent, 0, groups)

    small = jnp.stack([ln1_gain, ln1_bias, b_query, b_value, b_output, ln2_gain, ln2_bias], axis=1)
    tally = fold(counts).astype(BF16)
    extra = pad_columns(jnp.concatenate([small, tally], axis=1), up(7 + spread))
    wide = jnp.concatenate([w_query, w_key, w_value, extra], axis=1)
    rest = jnp.concatenate([w_router, b_out.T], axis=1)
    rest = jnp.concatenate([w_output, pad_columns(rest, up(2 * experts))], axis=1)
    if staged():
        wide, rest = gather_first(wide), gather_first(rest)
        rest_first = rest
        sent_w = to_send(*after((w_in, w_out), grad_send))
        free = gather_second(wide, (grad_send, sent_w))
        wide = gather_third(free)
        rest = after(rest, free)
    else:
        wide = lax.all_gather(wide, ALL, axis=0, tiled=True)
        rest = lax.all_gather(rest, ALL, axis=0, tiled=True)
        free = rest_first = ()
        sent_w = to_send(w_in, w_out)

    bias_rows = b_in[:, None, :]
    got_bias = [swap(after(bias_rows, free), "batch", mask) for mask in (1, 2)]
    got_w, last = [], free
    for l in range(groups):
        if l % chunk == 0:
            last = got_w[-chunk:] or free
        got_w.append([swap(w, "batch", heavy(l)) for w in after(sent_w[l], last)])

    own_z = to_owners(after(grad_send, rest_first))
    theirs = lambda rows, l, at: swap(rows[:, at : at + 1], "batch", light(l))
    other_z = [theirs(own_z, l, l) for l in range(groups)]

    vectors = wide[:, 3 * width : 3 * width + 7].astype(F32).T
    gain_one, shift_one, bias_query, bias_value, bias_output, gain_two, shift_two = vectors
    tallies = wide[:, 3 * width + 7 : 3 * width + 7 + spread].astype(F32).reshape(devices, share, spread)
    all_counts = unfold(jnp.sum(tallies, axis=0))
    token_total = float(row_count * devices)
    fraction = all_counts / token_total

    inputs = tokens.astype(F32)
    unit_one, rstd_one = normed(inputs)
    h_one = (unit_one * gain_one + shift_one).astype(BF16)
    nothing = jnp.zeros((width,), F32)
    bias = jnp.concatenate([bias_query, nothing, bias_value, jnp.zeros((wide.shape[1] - 3 * width,), F32)])
    qkv = (dot(h_one, wide) + bias).astype(BF16)
    if staged():
        rest = gather_second(rest, qkv)
    seg_row = segment_ids.reshape(1, row_count)
    seg_col = segment_ids.reshape(row_count, 1)
    attended, logs = attend(qkv, seg_row, seg_col, width)
    attended = after(attended, [w[0] for w in got_w[:chunk]])
    if staged():
        rest = gather_third(rest, attended)
    full_output = rest[:, :width]
    full_router = pad_columns(rest[:, width : width + experts], LANES)
    bias_expert = rest[:, width + experts : width + 2 * experts].T
    resid = inputs + dot(attended, full_output) + bias_output
    unit_two, rstd_two = normed(resid)
    h_two = (unit_two * gain_two + shift_two).astype(BF16)
    h_two = after(h_two, own_z, [w[1] for w in got_w[:chunk]])

    rows = [send(h_two, first, chunk) for first in firsts]
    token_rows = []
    for at in range(len(firsts)):
        if at:
            rows[at] = after(rows[at], token_rows[-1], [w[0] for w in got_w[chunk:]])
        token_rows.append(to_owners(rows[at]))
    token_rows = [after(t, rows) for t in token_rows]
    their_h = [token_rows[l // chunk][:, l % chunk : l % chunk + 1] for l in range(groups)]
    their_h = [lax.optimization_barrier(their_h[first : first + chunk]) for first in firsts]
    other_h = [swap(their_h[l // chunk][l % chunk], "batch", light(l)) for l in range(groups)]
    h_turned, att_turned = turn(h_one, attended)

    router_probs = jax.nn.softmax(dot(h_two, full_router)[:, :experts], axis=-1)
    mixing = kept_float * jnp.sum(router_probs * picked_float, axis=1)
    grad_out = cotangent.astype(F32)
    expert_bias = dot(picked.astype(BF16), bias_expert)
    gate_bias = kept_float * jnp.sum(grad_out * expert_bias, axis=1)
    grad_probs = picked_float * gate_bias[:, None] + BALANCE * experts * fraction[None, :] / token_total
    grad_logits = router_probs * (grad_probs - jnp.sum(grad_probs * router_probs, axis=1, keepdims=True))
    grad_logits = grad_logits.astype(BF16)
    mixed = picked_float * mixing[:, None]
    mixed_high = mixed.astype(BF16)
    mixed_low = (mixed - mixed_high.astype(F32)).astype(BF16)
    grad_bias_expert = dot_tn(cotangent, mixed_high) + dot_tn(cotangent, mixed_low)
    home_router = dot_tn(h_two, grad_logits)
    home_h_two = dot_nt(grad_logits, full_router[:, :experts])
    home_h_two, home_router, grad_bias_expert, probs_sum = lax.optimization_barrier(
        (home_h_two, home_router, grad_bias_expert, jnp.sum(router_probs, axis=0))
    )
    made, returned, piece_sums, got_g = [], [], [], []
    for at, first in enumerate(firsts):
        for l in pair(first):
            number = ((me * groups + l) // split).astype(jnp.int32).reshape(1)
            if l == 0:
                number = after(number, h_turned, home_h_two)
            if l == 1:
                number = after(number, made[-1], got_w[-chunk:], their_h)
            made.append(
                expert(
                    number, token_rows[at], other_h[l], own_z, other_z[l], (l - first, 0, l, 0),
                    (w_in, w_out, bias_rows), (*got_w[l], got_bias[heavy(l) - 1]), (l, l, l, 0, 0, l),
                    full_router, experts,
                )
            )
        sums = [(made[l][2], swap(after(made[l][3], other_h), "batch", light(l))) for l in pair(first)]
        rows = merge(sums, owners, slots)
        if returned:
            rows = after(rows, returned[-1], got_g)
        returned.append(to_owners(rows).reshape(-1, width))
        n = (len(made[0]) - 5) // 2
        if first + chunk == groups:
            piece_sums = [(m[0], swap(after(m[1], sums), "batch", light(l))) for l, m in enumerate(made)]
        for l in pair(first):
            grads = after(made[l][4 + n : 4 + 2 * n], sums, other_h, piece_sums)
            got_g.append([swap(g, "batch", heavy(l)) for g in grads])
    own_g = [m[4 : 4 + n] for m in made]

    grad_router = home_router + sum(m[-1] for m in made)[:, :experts]

    grad_h_two = home_h_two + combine(after(id_col, piece_sums), returned, layout, firsts)
    grad_resid = grad_out + norm_back(grad_h_two, gain_two, unit_two, rstd_two)
    grad_branch = grad_resid.astype(BF16)
    grad_att = dot_nt(grad_branch, full_output).astype(BF16)
    columns = lambda *rows: jnp.stack(rows, axis=1)
    prob_sums = jnp.tile(fold(probs_sum), (devices, 1))
    sums = columns(
        jnp.sum(grad_h_two * unit_two, axis=0), jnp.sum(grad_h_two, axis=0), jnp.sum(grad_branch.astype(F32), axis=0)
    )
    packed = jnp.concatenate([grad_router, grad_bias_expert, sums, prob_sums], axis=1)
    packed = pad_columns(packed, LANES).astype(BF16)
    merged = merge(after(piece_sums, grad_att, packed), owners, slots)
    pieces = to_owners(merged).reshape(-1, width)
    grad_att = after(grad_att, merged, packed)
    dqkv = attend_back(qkv, grad_att, logs, seg_row, seg_col, width)

    dqkv, got_g = after((dqkv, got_g), got_g)
    input_grad, sums = input_back(dqkv, wide, tokens, grad_resid, gain_one[None])
    def close(waiting):
        own, got, _ = waiting
        if n == 1:
            win, wout, bias = finish([g[0] for g in own], [g[0] for g in got])
            return win, bias[:, 0], wout
        both = [[a[0].astype(F32) + b[0].astype(F32) for a, b in zip(*pair_g)] for pair_g in zip(own, got)]
        return (
            jnp.stack([g[0][:width] for g in both]),
            jnp.stack([g[0][width] for g in both]),
            jnp.stack([g[1] for g in both]),
        )

    wide_sum, (grad_w_in, grad_b_in, grad_w_out) = scatter_rows(
        outer(h_turned, att_turned, dqkv, grad_branch, packed, sums), (own_g, got_g, pieces), close
    )
    pieces = after(pieces, grad_b_in)
    fetched = combine(id_col, [pieces], (groups, groups, split, slots), (0,))
    block_out = (resid + mixing[:, None] * (fetched + expert_bias)).astype(BF16)
    router_sum = wide_sum[:, 4 * width : 4 * width + 2 * experts]
    side = wide_sum[:, 4 * width + 2 * experts :]
    late_side = wide_sum[:, 4 * width + LANES :]
    mean_probs = unfold(side[:, 3 : 3 + spread]) / token_total
    balance_loss = experts * jnp.sum(fraction * mean_probs)
    expert_shares = jnp.stack([experts * fraction, experts * mean_probs])

    return (
        block_out,
        balance_loss,
        expert_shares,
        input_grad,
        late_side[:, 0],
        late_side[:, 1],
        wide_sum[:, :width],
        late_side[:, 2],
        wide_sum[:, width : 2 * width],
        wide_sum[:, 2 * width : 3 * width],
        late_side[:, 3],
        wide_sum[:, 3 * width : 4 * width],
        side[:, 2],
        side[:, 0],
        side[:, 1],
        router_sum[:, :experts],
        grad_w_in,
        grad_b_in,
        grad_w_out,
        router_sum[:, experts:].T,
    )


def solution(mesh):
    rows, split = P(ALL, None), P(ALL)
    experts = (P("expert", None, "batch"), P("expert", "batch"), P("expert", "batch", None), P(None, ALL))
    return jax.shard_map(
        local,
        mesh=mesh,
        in_specs=(
            rows, rows, rows, rows, P(), split, split, rows, split, rows, rows, split, rows, split, split, split,
            rows, *experts,
        ),
        out_specs=(
            rows, P(), P(), rows, split, split, rows, split, rows, rows, split, rows, split, split, split, rows,
            *experts,
        ),
        check_vma=False,
    )
```

time: 845 us -> 595 us (0.70)
  waiting for transfers between devices: 299 us -> 135 us
  Pallas kernels: 197 us -> 253 us
  other arithmetic: 94.6 us -> 44 us
  local copies, waits for them, and re-layouts: 78.9 us -> 37.3 us
  starting transfers between devices: 114 us -> 87.6 us
  matrix products: 49.5 us -> 27.7 us
    ppermute x53 -> x42, waiting for transfers between devices: 259 us -> 102 us  [swap(): lax.ppermute(x, axis, [(i, i ^ mask) for i in range(lax.axis_size(axis))])]
    pallas_call x8 -> x17, Pallas kernels: 147 us -> 203 us  [the longest x4 114 us: expert(): pl.pallas_call(functools.partial(expert_kernel, steps, experts, len(grads...]
    another operation x24 -> x9, other arithmetic: 40 us -> 9.17 us  [the longest x4 4.27 us: gather_second(): return jnp.stack([jnp.where(high, u[i ^ 2], u[i]) for i in range(4)])]
    all_to_all x8 -> x0, local copies, waits for them, and re-layouts: 18.3 us -> none  [to_owners(): return lax.all_to_all(x, 'expert', split_axis=1, concat_axis=1, tiled=True)]
    slice x16 -> x7, local copies, waits for them, and re-layouts: 29 us -> 11.1 us  [the longest x2 5.09 us: local(): token_rows[l // chunk][:, l % chunk:l % chunk + 1]]
    dot_general x7 -> x3, matrix products: 19.2 us -> 3.32 us  [dot_tn(): lax.dot_general(a, b, (((0,), (0,)), ((), ())), preferred_element_type=F32)]
    all_to_all x8 -> x6, waiting for transfers between devices: 35.3 us -> 21 us  [to_owners(): return lax.all_to_all(x, 'expert', split_axis=0, concat_axis=0, tiled=True)]
    ppermute x53 -> x42, starting transfers between devices: 58.1 us -> 44 us  [swap(): lax.ppermute(x, axis, [(i, i ^ mask) for i in range(lax.axis_size(axis))])]
  transfers between devices with their start and end apart: 73 -> 57, of which waited for: 31 -> 22; matrix products, arithmetic and copies ran while one was open for 20% -> 16% of each run, Pallas kernels for 19% -> 42%
where the time goes in v2:
time: 595 us; the launch traced here: 588 us
  Pallas kernels  253 us (43%)
  waiting for transfers between devices  135 us (23%)
  starting transfers between devices  87.6 us (15%)
  other arithmetic  44 us (7%)
  local copies, waits for them, and re-layouts  37.3 us (6%)
  matrix products  27.7 us (5%)
    pallas_call x4, Pallas kernels, expert(): pl.pallas_call(functools.partial(expert_kernel, steps, experts, len(grads...  114 us
    ppermute x42, waiting for transfers between devices, swap(): lax.ppermute(x, axis, [(i, i ^ mask) for i in range(lax.axis_size(axis))])  102 us
    ppermute x42, starting transfers between devices, swap(): lax.ppermute(x, axis, [(i, i ^ mask) for i in range(lax.axis_size(axis))])  44 us
    pallas_call x1, Pallas kernels, attend_back(): pl.pallas_call(attend_back_kernel, grid=(pairs,), in_specs=[spec(0), spec...  28.4 us
    all_to_all x6, starting transfers between devices, to_owners(): return lax.all_to_all(x, 'expert', split_axis=0, concat_axis=0, tiled=True)  28 us
    pallas_call x1, Pallas kernels, attend(): pl.pallas_call(attend_kernel, grid=(pairs,), in_specs=[spec(0), spec(pair...  21.1 us
    all_to_all x6, waiting for transfers between devices, to_owners(): return lax.all_to_all(x, 'expert', split_axis=0, concat_axis=0, tiled=True)  21 us
    pallas_call x3, Pallas kernels, dispatch(): pl.pallas_call(functools.partial(dispatch_kernel, layout, first), grid=(c...  17.6 us
  transfers between devices with their start and end apart: 57, of which 22 were waited for; matrix products, arithmetic and copies ran while one was open for 16% of the time, Pallas kernels for 42%

profile of v2, /device:TPU:0, one launch (start us, length us, event | category | flops | bytes accessed | tf_op | source)
XLA Modules:
  0.0 588.5 jit_solution(406039495469668325)
XLA Ops:
  26.4 7.6 %dispatch.3 = bf16[2048,768]{1,0:T(8,128)(2,1)} custom-call(s32[1,1024]{1,0:T(1,128)} %reshape_select_fusion.id_ref, bf16[1024,768]{1,0:T(8,128)(2,1)} %x_ref.2), custom_call_target="tpu_custom_call" | custom-call | flops 3221225472 | bytes 6291456 | tf_op jit(solution)/shard_map/dispatch/pallas_call | solution.py:239
  34.1 8.7 %to_send.1 = (bf16[1,768,768]{2,1,0:T(8,128)(2,1)}, bf16[1,768,768]{2,1,0:T(8,128)(2,1)}, bf16[1,768,768]{2,1,0:T(8,128)(2,1)}, bf16[1,768,768]{2,1,0:T(8,128)(2...) custom-call(bf16[4,768,768]{2,1,0:T(8,128)(2,1)} %refs_5_.7, ...), custom_call_target="tpu_custom_call" | custom-call | tf_op jit(solution)/shard_map/to_send/pallas_call | solution.py:491
  67.1 8.5 %add_convert_fusion.q_ref.k_ref.v_ref = bf16[1024,2432]{1,0:T(8,128)(2,1)} fusion(bf16[1024,768]{1,0:T(8,128)(2,1)S(1)} %fusion.7.x_ref, bf16[768,2432]{1,0:T(8,128)(2,1)} %bitcast.141, f32[2432]{0:T(1024)S(1)} %pad_maximum_fusion.5), kind=kOutput, calls=%fused_computation | convolution fusion | flops 3830185984 | bytes 10298880 | tf_op jit(solution)/shard_map/dot_general | solution.py:24
  79.0 21.1 %attend.1 = (bf16[1024,768]{1,0:T(8,128)(2,1)}, f32[1024,768]{1,0:T(8,128)}) custom-call(bf16[1024,2432]{1,0:T(8,128)(2,1)} %add_convert_fusion.q_ref.k_ref.v_ref, bf16[1024,2432]{1,0:T(8,128)(2,1)} %add_convert_fusion.q_ref.k_ref.v_ref, bf16[1024,2432]{1,0:T(8,128)(2,1)} %add_convert_fusion.q_ref.k_ref.v_ref, s32[1,1024]{1,0:T(1,128)} %row_ref.3, ...), custom_call_target="tpu_custom_call" | custom-call | flops 1610612736 | bytes 9437184 | tf_op jit(solution)/shard_map/attend/pallas_call | solution.py:143
  106.5 10.5 %collective-permute-done.16.refs_9_ = bf16[1,768,768]{2,1,0:T(8,128)(2,1)} collective-permute-done((bf16[1,768,768]{2,1,0:T(8,128)(2,1)}, bf16[1,768,768]{2,1,0:T(8,128)(2,1)}, u32[]{:S(2)}, u32[]{:S(2)}) %collective-permute-start.16) | collective-permute-done | bytes 1179680 | tf_op jit(solution)/shard_map/ppermute | solution.py:36
  117.0 9.4 %all-to-all-done.refs_3_ = bf16[8,4,64,768]{3,2,1,0:T(8,128)(2,1)} async-done(((bf16[8,4,64,768]{3,2,1,0:T(8,128)(2,1)}), bf16[8,4,64,768]{3,2,1,0:T(8,128)(2,1)}, u32[]{:S(2)}, u32[]{:S(2)}) %all-to-all-start) | async-done | bytes 3145760 | tf_op jit(solution)/shard_map/all_to_all | solution.py:92
  192.0 12.4 %collective-permute-done.20.refs_2_ = bf16[8,1,64,768]{3,2,1,0:T(8,128)(2,1)} collective-permute-done((bf16[8,1,64,768]{3,2,1,0:T(8,128)(2,1)}, bf16[8,1,64,768]{3,2,1,0:T(8,128)(2,1)}, u32[]{:S(2)}, u32[]{:S(2)}) %collective-permute-start.20) | collective-permute-done | bytes 786464 | tf_op jit(solution)/shard_map/ppermute | solution.py:36
  205.8 28.4 %expert.4 = (bf16[512,768]{1,0:T(8,128)(2,1)}, bf16[512,768]{1,0:T(8,128)(2,1)}, bf16[512,768]{1,0:T(8,128)(2,1)}, bf16[512,768]{1,0:T(8,128)(2,1)}, bf16[1,1552...) custom-call(s32[1]{0:T(128)} %bitcast.38.refs_0_, ...), custom_call_target="tpu_custom_call" | custom-call | flops 14495514624 | bytes 11796480 | tf_op jit(solution)/shard_map/expert/pallas_call | solution.py:428
  238.7 28.5 %expert.7 = (bf16[512,768]{1,0:T(8,128)(2,1)}, bf16[512,768]{1,0:T(8,128)(2,1)}, bf16[512,768]{1,0:T(8,128)(2,1)}, bf16[512,768]{1,0:T(8,128)(2,1)}, bf16[1,1552...) custom-call(s32[1]{0:T(128)} %bitcast.46.refs_0_, ...), custom_call_target="tpu_custom_call" | custom-call | flops 14495514624 | bytes 11796480 | tf_op jit(solution)/shard_map/expert/pallas_call | solution.py:428
  271.3 16.7 %collective-permute-done.38.refs_1_ = bf16[512,768]{1,0:T(8,128)(2,1)} collective-permute-done((bf16[512,768]{1,0:T(8,128)(2,1)}, bf16[512,768]{1,0:T(8,128)(2,1)}, u32[]{:S(2)}, u32[]{:S(2)}) %collective-permute-start.38) | collective-permute-done | bytes 786464 | tf_op jit(solution)/shard_map/ppermute | solution.py:36
  302.9 28.7 %expert.5 = (bf16[512,768]{1,0:T(8,128)(2,1)}, bf16[512,768]{1,0:T(8,128)(2,1)}, bf16[512,768]{1,0:T(8,128)(2,1)}, bf16[512,768]{1,0:T(8,128)(2,1)}, bf16[1,1552...) custom-call(s32[1]{0:T(128)} %bitcast.44.refs_0_, ...), custom_call_target="tpu_custom_call" | custom-call | flops 14495514624 | bytes 11796480 | tf_op jit(solution)/shard_map/expert/pallas_call | solution.py:428
  331.7 28.8 %expert.6 = (bf16[512,768]{1,0:T(8,128)(2,1)}, bf16[512,768]{1,0:T(8,128)(2,1)}, bf16[512,768]{1,0:T(8,128)(2,1)}, bf16[512,768]{1,0:T(8,128)(2,1)}, bf16[1,1552...) custom-call(s32[1]{0:T(128)} %bitcast.45.refs_0_, ...), custom_call_target="tpu_custom_call" | custom-call | flops 14495514624 | bytes 11796480 | tf_op jit(solution)/shard_map/expert/pallas_call | solution.py:428
  362.9 13.7 %collective-permute-done.32.refs_3_ = bf16[512,768]{1,0:T(8,128)(2,1)S(1)} collective-permute-done((bf16[512,768]{1,0:T(8,128)(2,1)}, bf16[512,768]{1,0:T(8,128)(2,1)S(1)}, u32[]{:S(2)}, u32[]{:S(2)}) %collective-permute-start.32) | collective-permute-done | bytes 786464 | tf_op jit(solution)/shard_map/ppermute | solution.py:36
  393.2 12.6 %collective-permute-done.33.refs_1_ = bf16[512,768]{1,0:T(8,128)(2,1)} collective-permute-done((bf16[512,768]{1,0:T(8,128)(2,1)}, bf16[512,768]{1,0:T(8,128)(2,1)}, u32[]{:S(2)}, u32[]{:S(2)}) %collective-permute-start.33) | collective-permute-done | bytes 786464 | tf_op jit(solution)/shard_map/ppermute | solution.py:36
  407.0 15.3 %collective-permute-done.36.refs_5_ = bf16[512,768]{1,0:T(8,128)(2,1)} collective-permute-done((bf16[512,768]{1,0:T(8,128)(2,1)}, bf16[512,768]{1,0:T(8,128)(2,1)}, u32[]{:S(2)}, u32[]{:S(2)}) %collective-permute-start.36) | collective-permute-done | bytes 786464 | tf_op jit(solution)/shard_map/ppermute | solution.py:36
  425.1 7.1 %combine.2 = f32[1024,768]{1,0:T(8,128)} custom-call(s32[1024,1]{1,0:T(8,128)} %get-tuple-element.218.id_ref, bf16[1024,768]{1,0:T(8,128)(2,1)} %bitcast.47.refs_0_, bf16[1024,768]{1,0:T(8,128)(2,1)} %bitcast.48.refs_1_), custom_call_target="tpu_custom_call" | custom-call | flops 3221225472 | bytes 6291456 | tf_op jit(solution)/shard_map/combine/pallas_call | solution.py:269
  458.7 28.4 %attend_back.1.g_ref = bf16[3,1024,768]{2,1,0:T(8,128)(2,1)} custom-call(bf16[1024,2432]{1,0:T(8,128)(2,1)} %add_convert_fusion.q_ref.k_ref.v_ref, bf16[1024,2432]{1,0:T(8,128)(2,1)} %add_convert_fusion.q_ref.k_ref.v_ref, bf16[1024,2432]{1,0:T(8,128)(2,1)} %add_convert_fusion.q_ref.k_ref.v_ref, bf16[1024,768]{1,0:T(8,128)(2,1)} %convolution_convert_fusion.g_ref, ...), custom_call_target="tpu_custom_call" | custom-call | flops 1 | bytes 1 | tf_op jit(solution)/shard_map/attend_back/pallas_call | solution.py:205
  487.2 10.1 %input_back.1 = (f32[1024,768]{1,0:T(8,128)}, f32[128,768]{1,0:T(8,128)}) custom-call(bf16[3,1024,768]{2,1,0:T(8,128)(2,1)} %attend_back.1.g_ref, bf16[768,2432]{1,0:T(8,128)(2,1)} %bitcast.143, bf16[1024,768]{1,0:T(8,128)(2,1)} %x_ref.3, f32[1024,768]{1,0:T(8,128)} %get-tuple-element.307.dy_ref, f32[1,768]{1,0:T(1,128)} %get-tuple-element.343.gain_ref), custom_call_target="tpu_custom_call" | custom-call | flops 1 | bytes 1 | tf_op jit(solution)/shard_map/input_back/pallas_call | solution.py:576
  497.2 10.2 %outer.1 = bf16[768,3328]{1,0:T(8,128)(2,1)} custom-call(bf16[768,1024]{1,0:T(8,128)(2,1)} %get-tuple-element.179.h_ref, bf16[768,1024]{1,0:T(8,128)(2,1)} %get-tuple-element.241.a_ref, bf16[3,1024,768]{2,1,0:T(8,128)(2,1)} %attend_back.1.g_ref, bf16[1024,768]{1,0:T(8,128)(2,1)} %get-tuple-element.306.b_ref, bf16[768,128]{1,0:T(8,128)(2,1)} %pad.30.rest_ref, ...), custom_call_target="tpu_custom_call" | custom-call | flops 1 | bytes 1 | tf_op jit(solution)/shard_map/outer/pallas_call | solution.py:537
  516.9 5.7 fusion
  522.6 7.8 %all-to-all-done.5 = bf16[8,4,64,768]{3,2,1,0:T(8,128)(2,1)} async-done(((bf16[8,4,64,768]{3,2,1,0:T(8,128)(2,1)}), bf16[8,4,64,768]{3,2,1,0:T(8,128)(2,1)}, u32[]{:S(2)}, u32[]{:S(2)}) %all-to-all-start.5) | async-done | bytes 3145760 | tf_op jit(solution)/shard_map/all_to_all | solution.py:92
  536.7 14.0 %finish.1 = (f32[4,768,768]{2,1,0:T(8,128)}, f32[4,768,768]{2,1,0:T(8,128)}, f32[4,16,768]{2,1,0:T(8,128)}) custom-call(bf16[1,1552,768]{2,1,0:T(8,128)(2,1)} %get-tuple-element.266.refs_0_.refs_1_.refs_2_, bf16[1,1552,768]{2,1,0:T(8,128)(2,1)} %get-tuple-element.266.refs_0_.refs_1_.refs_2_, ...), custom_call_target="tpu_custom_call" | custom-call | flops 9535488 | bytes 38141952 | tf_op jit(solution)/shard_map/finish/pallas_call | solution.py:467
  552.2 7.0 %combine.3 = f32[1024,768]{1,0:T(8,128)} custom-call(s32[1024,1]{1,0:T(8,128)} %get-tuple-element.218.id_ref, bf16[2048,768]{1,0:T(8,128)(2,1)} %bitcast.51.refs_0_), custom_call_target="tpu_custom_call" | custom-call | flops 3221225472 | bytes 6291456 | tf_op jit(solution)/shard_map/combine/pallas_call | solution.py:269
  576.4 6.2 %collective-permute-done.49 = bf16[24,3328]{1,0:T(8,128)(2,1)S(1)} collective-permute-done((bf16[24,3328]{1,0:T(8,128)(2,1)S(1)}, bf16[24,3328]{1,0:T(8,128)(2,1)S(1)}, u32[]{:S(2)}, u32[]{:S(2)}) %collective-permute-start.49) | collective-permute-done | bytes 159776 | tf_op jit(solution)/shard_map/ppermute | solution.py:41
  (286 shorter events, 237.2 us)
Async XLA Ops:
  2.2 47.8 %collective-permute-start.11 = (bf16[24,896]{1,0:T(8,128)(2,1)S(1)}, bf16[24,896]{1,0:T(8,128)(2,1)S(1)}, u32[]{:S(2)}, u32[]{:S(2)}) collective-permute-start(bf16[24,896]{1,0:T(8,128)(2,1)S(1)} %pad_maximum_fusion.4), channel_id=1, source_target_pairs={{0,2},{1,3},{2,4},{3,5},{4,6},{5,7},{6,0},{7,1},{8,10},{9,11},{10,... | collective-permute-start | bytes 129032 | tf_op jit(solution)/shard_map/ppermute | solution.py:41
  5.2 44.7 %collective-permute-start.10 = (bf16[24,896]{1,0:T(8,128)(2,1)S(1)}, bf16[24,896]{1,0:T(8,128)(2,1)S(1)}, u32[]{:S(2)}, u32[]{:S(2)}) collective-permute-start(bf16[24,896]{1,0:T(8,128)(2,1)S(1)} %pad_maximum_fusion.4), channel_id=1, source_target_pairs={{0,4},{1,5},{2,6},{3,7},{4,0},{5,1},{6,2},{7,3},{8,12},{9,13},{10,... | collective-permute-start | bytes 129032 | tf_op jit(solution)/shard_map/ppermute | solution.py:41
  50.1 76.2 %all-to-all-start = ((bf16[8,4,64,768]{3,2,1,0:T(8,128)(2,1)}), bf16[8,4,64,768]{3,2,1,0:T(8,128)(2,1)}, u32[]{:S(2)}, u32[]{:S(2)}) async-start(bf16[8,4,64,768]{3,2,1,0:T(8,128)(2,1)} %bitcast.150), calls=%async_computation | async-start | bytes 6291456 | tf_op jit(solution)/shard_map/all_to_all | solution.py:92
  58.3 41.7 %collective-permute-start.7 = (bf16[1,768,768]{2,1,0:T(8,128)(2,1)}, bf16[1,768,768]{2,1,0:T(8,128)(2,1)}, u32[]{:S(2)}, u32[]{:S(2)}) collective-permute-start(bf16[1,768,768]{2,1,0:T(8,128)(2,1)} %get-tuple-element.166), channel_id=1, source_target_pairs={{0,8},{8,0},{16,24},{24,16},{1,9},{9,1},{17,25},{25,17},{2,10},{10... | collective-permute-start | bytes 3538952 | tf_op jit(solution)/shard_map/ppermute | solution.py:36
  59.8 40.2 %collective-permute-start.8 = (bf16[1,768,768]{2,1,0:T(8,128)(2,1)}, bf16[1,768,768]{2,1,0:T(8,128)(2,1)}, u32[]{:S(2)}, u32[]{:S(2)}) collective-permute-start(bf16[1,768,768]{2,1,0:T(8,128)(2,1)} %get-tuple-element.167), channel_id=1, source_target_pairs={{0,16},{8,24},{16,0},{24,8},{1,17},{9,25},{17,1},{25,9},{2,18},{10... | collective-permute-start | bytes 3538952 | tf_op jit(solution)/shard_map/ppermute | solution.py:36
  77.9 39.0 %collective-permute-start.16 = (bf16[1,768,768]{2,1,0:T(8,128)(2,1)}, bf16[1,768,768]{2,1,0:T(8,128)(2,1)}, u32[]{:S(2)}, u32[]{:S(2)}) collective-permute-start(bf16[1,768,768]{2,1,0:T(8,128)(2,1)} %get-tuple-element.176), channel_id=1, source_target_pairs={{0,8},{8,0},{16,24},{24,16},{1,9},{9,1},{17,25},{25,17},{2,10},{10... | collective-permute-start | bytes 3538952 | tf_op jit(solution)/shard_map/ppermute | solution.py:36
  78.5 38.5 %collective-permute-start.17 = (bf16[1,768,768]{2,1,0:T(8,128)(2,1)}, bf16[1,768,768]{2,1,0:T(8,128)(2,1)}, u32[]{:S(2)}, u32[]{:S(2)}) collective-permute-start(bf16[1,768,768]{2,1,0:T(8,128)(2,1)} %get-tuple-element.177), channel_id=1, source_target_pairs={{0,16},{8,24},{16,0},{24,8},{1,17},{9,25},{17,1},{25,9},{2,18},{10... | collective-permute-start | bytes 3538952 | tf_op jit(solution)/shard_map/ppermute | solution.py:36
  131.3 42.7 %all-to-all-start.1 = ((bf16[8,2,64,768]{3,2,1,0:T(8,128)(2,1)}), bf16[8,2,64,768]{3,2,1,0:T(8,128)(2,1)}, u32[]{:S(2)}, u32[]{:S(2)}) async-start(bf16[8,2,64,768]{3,2,1,0:T(8,128)(2,1)} %bitcast.152), calls=%async_computation.1 | async-start | bytes 3145728 | tf_op jit(solution)/shard_map/all_to_all | solution.py:92
  137.4 101.2 %collective-permute-start.31 = (bf16[4,1,768]{2,1,0:T(2,128)(2,1)}, bf16[4,1,768]{2,1,0:T(2,128)(2,1)}, u32[]{:S(2)}, u32[]{:S(2)}) collective-permute-start(bf16[4,1,768]{2,1,0:T(2,128)(2,1)} %copy.97), channel_id=1, source_target_pairs={{0,16},{8,24},{16,0},{24,8},{1,17},{9,25},{17,1},{25,9},{2,18},{10... | collective-permute-start | bytes 18440 | tf_op jit(solution)/shard_map/ppermute | solution.py:36
  138.9 51.1 %collective-permute-start.22 = (bf16[4,1,768]{2,1,0:T(2,128)(2,1)}, bf16[4,1,768]{2,1,0:T(2,128)(2,1)}, u32[]{:S(2)}, u32[]{:S(2)}) collective-permute-start(bf16[4,1,768]{2,1,0:T(2,128)(2,1)} %copy.97), channel_id=1, source_target_pairs={{0,8},{8,0},{16,24},{24,16},{1,9},{9,1},{17,25},{25,17},{2,10},{10... | collective-permute-start | bytes 18440 | tf_op jit(solution)/shard_map/ppermute | solution.py:36
  141.0 95.6 %collective-permute-start.25 = (bf16[1,768,768]{2,1,0:T(8,128)(2,1)}, bf16[1,768,768]{2,1,0:T(8,128)(2,1)}, u32[]{:S(2)}, u32[]{:S(2)}) collective-permute-start(bf16[1,768,768]{2,1,0:T(8,128)(2,1)} %get-tuple-element.192), channel_id=1, source_target_pairs={{0,8},{8,0},{16,24},{24,16},{1,9},{9,1},{17,25},{25,17},{2,10},{10... | collective-permute-start | bytes 3538952 | tf_op jit(solution)/shard_map/ppermute | solution.py:36
  174.0 60.2 %all-to-all-start.2 = ((bf16[8,2,64,768]{3,2,1,0:T(8,128)(2,1)}), bf16[8,2,64,768]{3,2,1,0:T(8,128)(2,1)}, u32[]{:S(2)}, u32[]{:S(2)}) async-start(bf16[8,2,64,768]{3,2,1,0:T(8,128)(2,1)} %bitcast.151), calls=%async_computation.2 | async-start | bytes 3145728 | tf_op jit(solution)/shard_map/all_to_all | solution.py:92
  190.0 48.1 %collective-permute-start.30 = (bf16[1,768,768]{2,1,0:T(8,128)(2,1)}, bf16[1,768,768]{2,1,0:T(8,128)(2,1)}, u32[]{:S(2)}, u32[]{:S(2)}) collective-permute-start(bf16[1,768,768]{2,1,0:T(8,128)(2,1)} %get-tuple-element.198), channel_id=1, source_target_pairs={{0,16},{8,24},{16,0},{24,8},{1,17},{9,25},{17,1},{25,9},{2,18},{10... | collective-permute-start | bytes 3538952 | tf_op jit(solution)/shard_map/ppermute | solution.py:36
  190.5 48.1 %collective-permute-start.34 = (bf16[8,1,64,768]{3,2,1,0:T(8,128)(2,1)}, bf16[8,1,64,768]{3,2,1,0:T(8,128)(2,1)}, u32[]{:S(2)}, u32[]{:S(2)}) collective-permute-start(bf16[8,1,64,768]{3,2,1,0:T(8,128)(2,1)} %get-tuple-element.311), channel_id=1, source_target_pairs={{0,8},{8,0},{16,24},{24,16},{1,9},{9,1},{17,25},{25,17},{2,10},{10... | collective-permute-start | bytes 2359304 | tf_op jit(solution)/shard_map/ppermute | solution.py:36
  270.8 60.9 %collective-permute-start.29 = (bf16[8,1,64,768]{3,2,1,0:T(8,128)(2,1)}, bf16[8,1,64,768]{3,2,1,0:T(8,128)(2,1)}, u32[]{:S(2)}, u32[]{:S(2)}) collective-permute-start(bf16[8,1,64,768]{3,2,1,0:T(8,128)(2,1)} %get-tuple-element.312), channel_id=1, source_target_pairs={{0,8},{8,0},{16,24},{24,16},{1,9},{9,1},{17,25},{25,17},{2,10},{10... | collective-permute-start | bytes 2359304 | tf_op jit(solution)/shard_map/ppermute | solution.py:36
  291.6 89.1 %all-to-all-start.3 = ((bf16[8,2,64,768]{3,2,1,0:T(8,128)(2,1)}), bf16[8,2,64,768]{3,2,1,0:T(8,128)(2,1)}, u32[]{:S(2)}, u32[]{:S(2)}) async-start(bf16[8,2,64,768]{3,2,1,0:T(8,128)(2,1)} %merge.3), calls=%async_computation.3 | async-start | bytes 3145728 | tf_op jit(solution)/shard_map/all_to_all | solution.py:92
  296.5 84.2 %collective-permute-start.40 = (bf16[1,1552,768]{2,1,0:T(8,128)(2,1)}, bf16[1,1552,768]{2,1,0:T(8,128)(2,1)}, u32[]{:S(2)}, u32[]{:S(2)}) collective-permute-start(bf16[1,1552,768]{2,1,0:T(8,128)(2,1)} %get-tuple-element.223), channel_id=1, source_target_pairs={{0,8},{8,0},{16,24},{24,16},{1,9},{9,1},{17,25},{25,17},{2,10},{10... | collective-permute-start | bytes 7151624 | tf_op jit(solution)/shard_map/ppermute | solution.py:36
  298.0 82.8 %collective-permute-start.41 = (bf16[1,1552,768]{2,1,0:T(8,128)(2,1)}, bf16[1,1552,768]{2,1,0:T(8,128)(2,1)}, u32[]{:S(2)}, u32[]{:S(2)}) collective-permute-start(bf16[1,1552,768]{2,1,0:T(8,128)(2,1)} %get-tuple-element.225), channel_id=1, source_target_pairs={{0,16},{8,24},{16,0},{24,8},{1,17},{9,25},{17,1},{25,9},{2,18},{10... | collective-permute-start | bytes 7151624 | tf_op jit(solution)/shard_map/ppermute | solution.py:36
  380.7 44.3 %all-to-all-start.4 = ((bf16[8,2,64,768]{3,2,1,0:T(8,128)(2,1)}), bf16[8,2,64,768]{3,2,1,0:T(8,128)(2,1)}, u32[]{:S(2)}, u32[]{:S(2)}) async-start(bf16[8,2,64,768]{3,2,1,0:T(8,128)(2,1)} %merge.4), calls=%async_computation.4 | async-start | bytes 3145728 | tf_op jit(solution)/shard_map/all_to_all | solution.py:92
  387.2 35.1 %collective-permute-start.36 = (bf16[512,768]{1,0:T(8,128)(2,1)}, bf16[512,768]{1,0:T(8,128)(2,1)}, u32[]{:S(2)}, u32[]{:S(2)}) collective-permute-start(bf16[512,768]{1,0:T(8,128)(2,1)} %get-tuple-element.214), channel_id=1, source_target_pairs={{0,16},{8,24},{16,0},{24,8},{1,17},{9,25},{17,1},{25,9},{2,18},{10... | collective-permute-start | bytes 2359304 | tf_op jit(solution)/shard_map/ppermute | solution.py:36
  388.2 34.7 %collective-permute-start.37 = (bf16[512,768]{1,0:T(8,128)(2,1)}, bf16[512,768]{1,0:T(8,128)(2,1)}, u32[]{:S(2)}, u32[]{:S(2)}) collective-permute-start(bf16[512,768]{1,0:T(8,128)(2,1)} %get-tuple-element.217), channel_id=1, source_target_pairs={{0,8},{8,0},{16,24},{24,16},{1,9},{9,1},{17,25},{25,17},{2,10},{10... | collective-permute-start | bytes 2359304 | tf_op jit(solution)/shard_map/ppermute | solution.py:36
  422.9 64.2 %collective-permute-start.42 = (bf16[1,1552,768]{2,1,0:T(8,128)(2,1)}, bf16[1,1552,768]{2,1,0:T(8,128)(2,1)}, u32[]{:S(2)}, u32[]{:S(2)}) collective-permute-start(bf16[1,1552,768]{2,1,0:T(8,128)(2,1)} %get-tuple-element.245), channel_id=1, source_target_pairs={{0,8},{8,0},{16,24},{24,16},{1,9},{9,1},{17,25},{25,17},{2,10},{10... | collective-permute-start | bytes 7151624 | tf_op jit(solution)/shard_map/ppermute | solution.py:36
  423.9 63.3 %collective-permute-start.43 = (bf16[1,1552,768]{2,1,0:T(8,128)(2,1)}, bf16[1,1552,768]{2,1,0:T(8,128)(2,1)}, u32[]{:S(2)}, u32[]{:S(2)}) collective-permute-start(bf16[1,1552,768]{2,1,0:T(8,128)(2,1)} %get-tuple-element.247), channel_id=1, source_target_pairs={{0,16},{8,24},{16,0},{24,8},{1,17},{9,25},{17,1},{25,9},{2,18},{10... | collective-permute-start | bytes 7151624 | tf_op jit(solution)/shard_map/ppermute | solution.py:36
  454.0 76.4 %all-to-all-start.5 = ((bf16[8,4,64,768]{3,2,1,0:T(8,128)(2,1)}), bf16[8,4,64,768]{3,2,1,0:T(8,128)(2,1)}, u32[]{:S(2)}, u32[]{:S(2)}) async-start(bf16[8,4,64,768]{3,2,1,0:T(8,128)(2,1)} %merge.5), calls=%async_computation.5 | async-start | bytes 6291456 | tf_op jit(solution)/shard_map/all_to_all | solution.py:92
  (64 other events, 872.3 us)

commit v3 on v2

--- a/solution.py
+++ b/solution.py
@@ -122,17 +122,16 @@
     first, halves = half_masks()
     for n, (start, low, stop) in enumerate(windows(length)):
         q = q_ref[start:stop, :] * jnp.asarray(HEAD**-0.5, BF16)
-        k, v = k_ref[low:stop, :], v_ref[low:stop, :]
-        outs, logs = [], []
-        for half in halves:
-            s = dot_nt(q * half, k) + mask_ref[n, :, : stop - low]
-            top = jnp.max(s, axis=1, keepdims=True)
-            e = jnp.exp(s - top)
-            sums = jnp.sum(e, axis=1, keepdims=True)
-            outs.append(dot(e.astype(BF16), v) / sums)
-            logs.append(top + jnp.log(sums))
-        out_ref[start:stop, :] = (outs[0] * first + outs[1] * (1.0 - first)).astype(BF16)
-        log_ref[start:stop, :] = logs[0] * first + logs[1] * (1.0 - first)
+        both = jnp.concatenate([q * half for half in halves])
+        mask = mask_ref[n, :, : stop - low]
+        s = dot_nt(both, k_ref[low:stop, :]) + jnp.concatenate([mask, mask])
+        top = jnp.max(s, axis=1, keepdims=True)
+        e = jnp.exp(s - top)
+        sums = jnp.sum(e, axis=1, keepdims=True)
+        out = dot(e.astype(BF16), v_ref[low:stop, :]) / sums
+        logs = top + jnp.log(sums)
+        out_ref[start:stop, :] = (out[:QROWS] * first + out[QROWS:] * (1.0 - first)).astype(BF16)
+        log_ref[start:stop, :] = logs[:QROWS] * first + logs[QROWS:] * (1.0 - first)
 
 
 def attend(qkv, seg_row, seg_col, width):
@@ -174,24 +173,25 @@
 
     dk_ref[...] = jnp.zeros_like(dk_ref)
     dv_ref[...] = jnp.zeros_like(dv_ref)
-    _, halves = half_masks()
+    first, halves = half_masks()
     scale = HEAD**-0.5
     for n, (start, low, stop) in enumerate(windows(length)):
         q = q_ref[start:stop, :] * jnp.asarray(scale, BF16)
         g = g_ref[start:stop, :]
         k, v = k_ref[low:stop, :], v_ref[low:stop, :]
-        logs = log_ref[start:stop, :].T
-        dq = jnp.zeros((QROWS, LANES), F32)
-        for at, half in zip((0, HEAD), halves):
-            qh, gh = q * half, g * half
-            s = dot_nt(k, qh) + mask_ref[n, : stop - low, :]
-            p = jnp.exp(s - logs[at : at + 1, :])
-            dp = dot_nt(v, gh)
-            centre = jnp.sum(dp * p, axis=0, keepdims=True)
-            ds = (p * (dp - centre)).astype(BF16)
-            dv_ref[low:stop, :] += dot(p.astype(BF16), gh)
-            dk_ref[low:stop, :] += dot(ds, qh)
-            dq += dot_tn(ds, k * half)
+        turned = log_ref[start:stop, :].T
+        logs = jnp.concatenate([turned[:1, :], turned[HEAD : HEAD + 1, :]], axis=1)
+        qs = jnp.concatenate([q * half for half in halves])
+        gs = jnp.concatenate([g * half for half in halves])
+        mask = mask_ref[n, : stop - low, :]
+        p = jnp.exp(dot_nt(k, qs) + jnp.concatenate([mask, mask], axis=1) - logs)
+        dp = dot_nt(v, gs)
+        centre = jnp.sum(dp * p, axis=0, keepdims=True)
+        ds = (p * (dp - centre)).astype(BF16)
+        dv_ref[low:stop, :] += dot(p.astype(BF16), gs)
+        dk_ref[low:stop, :] += dot(ds, qs)
+        dqs = dot_tn(ds, k)
+        dq = dqs[:QROWS] * first + dqs[QROWS:] * (1.0 - first)
         out_ref[0, start:stop, :] = (dq * scale).astype(BF16)
     out_ref[1] = dk_ref[...].astype(BF16)
     out_ref[2] = dv_ref[...].astype(BF16)

time: 595 us -> 595 us (level)
  Pallas kernels: 253 us -> 243 us
  waiting for transfers between devices: 135 us -> 145 us
  transfers between devices with their start and end apart: 57 -> 57, of which waited for: 22 -> 22; matrix products, arithmetic and copies ran while one was open for 16% -> 16% of each run, Pallas kernels for 42% -> 40%
where the time goes in v3:
time: 595 us; the launch traced here: 588 us
  Pallas kernels  243 us (41%)
  waiting for transfers between devices  145 us (24%)
  starting transfers between devices  87.5 us (15%)
  other arithmetic  44 us (7%)
  local copies, waits for them, and re-layouts  37.3 us (6%)
  matrix products  27.7 us (5%)
    pallas_call x4, Pallas kernels, expert(): pl.pallas_call(functools.partial(expert_kernel, steps, experts, len(grads...  114 us
    ppermute x42, waiting for transfers between devices, swap(): lax.ppermute(x, axis, [(i, i ^ mask) for i in range(lax.axis_size(axis))])  107 us
    ppermute x42, starting transfers between devices, swap(): lax.ppermute(x, axis, [(i, i ^ mask) for i in range(lax.axis_size(axis))])  44 us
    all_to_all x6, starting transfers between devices, to_owners(): return lax.all_to_all(x, 'expert', split_axis=0, concat_axis=0, tiled=True)  27.8 us
    all_to_all x6, waiting for transfers between devices, to_owners(): return lax.all_to_all(x, 'expert', split_axis=0, concat_axis=0, tiled=True)  26.6 us
    pallas_call x1, Pallas kernels, attend_back(): pl.pallas_call(attend_back_kernel, grid=(pairs,), in_specs=[spec(0), spec...  22.9 us
    pallas_call x3, Pallas kernels, dispatch(): pl.pallas_call(functools.partial(dispatch_kernel, layout, first), grid=(c...  17.6 us
    dot_general x5, matrix products, dot(): return jnp.dot(a, b, preferred_element_type=F32)  16.8 us
  transfers between devices with their start and end apart: 57, of which 22 were waited for; matrix products, arithmetic and copies ran while one was open for 16% of the time, Pallas kernels for 40%

profile of v3, /device:TPU:0, one launch (start us, length us, event | category | flops | bytes accessed | tf_op | source)
XLA Modules:
  0.0 588.2 jit_solution(2559634116775919388)
XLA Ops:
  26.4 7.6 %dispatch.3 = bf16[2048,768]{1,0:T(8,128)(2,1)} custom-call(s32[1,1024]{1,0:T(1,128)} %reshape_select_fusion.id_ref, bf16[1024,768]{1,0:T(8,128)(2,1)} %x_ref.2), custom_call_target="tpu_custom_call" | custom-call | flops 3221225472 | bytes 6291456 | tf_op jit(solution)/shard_map/dispatch/pallas_call | solution.py:239
  34.1 8.7 %to_send.1 = (bf16[1,768,768]{2,1,0:T(8,128)(2,1)}, bf16[1,768,768]{2,1,0:T(8,128)(2,1)}, bf16[1,768,768]{2,1,0:T(8,128)(2,1)}, bf16[1,768,768]{2,1,0:T(8,128)(2...) custom-call(bf16[4,768,768]{2,1,0:T(8,128)(2,1)} %refs_5_.7, ...), custom_call_target="tpu_custom_call" | custom-call | tf_op jit(solution)/shard_map/to_send/pallas_call | solution.py:491
  67.0 8.5 %add_convert_fusion.q_ref.k_ref.v_ref = bf16[1024,2432]{1,0:T(8,128)(2,1)} fusion(bf16[1024,768]{1,0:T(8,128)(2,1)S(1)} %fusion.7.x_ref, bf16[768,2432]{1,0:T(8,128)(2,1)} %bitcast.141, f32[2432]{0:T(1024)S(1)} %pad_maximum_fusion.5), kind=kOutput, calls=%fused_computation | convolution fusion | flops 3830185984 | bytes 10298880 | tf_op jit(solution)/shard_map/dot_general | solution.py:24
  78.9 16.5 %attend.1 = (bf16[1024,768]{1,0:T(8,128)(2,1)}, f32[1024,768]{1,0:T(8,128)}) custom-call(bf16[1024,2432]{1,0:T(8,128)(2,1)} %add_convert_fusion.q_ref.k_ref.v_ref, bf16[1024,2432]{1,0:T(8,128)(2,1)} %add_convert_fusion.q_ref.k_ref.v_ref, bf16[1024,2432]{1,0:T(8,128)(2,1)} %add_convert_fusion.q_ref.k_ref.v_ref, s32[1,1024]{1,0:T(1,128)} %row_ref.3, ...), custom_call_target="tpu_custom_call" | custom-call | flops 1610612736 | bytes 9437184 | tf_op jit(solution)/shard_map/attend/pallas_call | solution.py:142
  101.9 15.0 %collective-permute-done.16.refs_9_ = bf16[1,768,768]{2,1,0:T(8,128)(2,1)} collective-permute-done((bf16[1,768,768]{2,1,0:T(8,128)(2,1)}, bf16[1,768,768]{2,1,0:T(8,128)(2,1)}, u32[]{:S(2)}, u32[]{:S(2)}) %collective-permute-start.16) | collective-permute-done | bytes 1179680 | tf_op jit(solution)/shard_map/ppermute | solution.py:36
  116.9 9.4 %all-to-all-done.refs_3_ = bf16[8,4,64,768]{3,2,1,0:T(8,128)(2,1)} async-done(((bf16[8,4,64,768]{3,2,1,0:T(8,128)(2,1)}), bf16[8,4,64,768]{3,2,1,0:T(8,128)(2,1)}, u32[]{:S(2)}, u32[]{:S(2)}) %all-to-all-start) | async-done | bytes 3145760 | tf_op jit(solution)/shard_map/all_to_all | solution.py:92
  191.9 12.4 %collective-permute-done.20.refs_2_ = bf16[8,1,64,768]{3,2,1,0:T(8,128)(2,1)} collective-permute-done((bf16[8,1,64,768]{3,2,1,0:T(8,128)(2,1)}, bf16[8,1,64,768]{3,2,1,0:T(8,128)(2,1)}, u32[]{:S(2)}, u32[]{:S(2)}) %collective-permute-start.20) | collective-permute-done | bytes 786464 | tf_op jit(solution)/shard_map/ppermute | solution.py:36
  205.7 28.4 %expert.4 = (bf16[512,768]{1,0:T(8,128)(2,1)}, bf16[512,768]{1,0:T(8,128)(2,1)}, bf16[512,768]{1,0:T(8,128)(2,1)}, bf16[512,768]{1,0:T(8,128)(2,1)}, bf16[1,1552...) custom-call(s32[1]{0:T(128)} %bitcast.38.refs_0_, ...), custom_call_target="tpu_custom_call" | custom-call | flops 14495514624 | bytes 11796480 | tf_op jit(solution)/shard_map/expert/pallas_call | solution.py:428
  238.6 28.5 %expert.7 = (bf16[512,768]{1,0:T(8,128)(2,1)}, bf16[512,768]{1,0:T(8,128)(2,1)}, bf16[512,768]{1,0:T(8,128)(2,1)}, bf16[512,768]{1,0:T(8,128)(2,1)}, bf16[1,1552...) custom-call(s32[1]{0:T(128)} %bitcast.46.refs_0_, ...), custom_call_target="tpu_custom_call" | custom-call | flops 14495514624 | bytes 11796480 | tf_op jit(solution)/shard_map/expert/pallas_call | solution.py:428
  271.2 16.7 %collective-permute-done.38.refs_1_ = bf16[512,768]{1,0:T(8,128)(2,1)} collective-permute-done((bf16[512,768]{1,0:T(8,128)(2,1)}, bf16[512,768]{1,0:T(8,128)(2,1)}, u32[]{:S(2)}, u32[]{:S(2)}) %collective-permute-start.38) | collective-permute-done | bytes 786464 | tf_op jit(solution)/shard_map/ppermute | solution.py:36
  302.8 28.7 %expert.5 = (bf16[512,768]{1,0:T(8,128)(2,1)}, bf16[512,768]{1,0:T(8,128)(2,1)}, bf16[512,768]{1,0:T(8,128)(2,1)}, bf16[512,768]{1,0:T(8,128)(2,1)}, bf16[1,1552...) custom-call(s32[1]{0:T(128)} %bitcast.44.refs_0_, ...), custom_call_target="tpu_custom_call" | custom-call | flops 14495514624 | bytes 11796480 | tf_op jit(solution)/shard_map/expert/pallas_call | solution.py:428
  331.6 28.8 %expert.6 = (bf16[512,768]{1,0:T(8,128)(2,1)}, bf16[512,768]{1,0:T(8,128)(2,1)}, bf16[512,768]{1,0:T(8,128)(2,1)}, bf16[512,768]{1,0:T(8,128)(2,1)}, bf16[1,1552...) custom-call(s32[1]{0:T(128)} %bitcast.45.refs_0_, ...), custom_call_target="tpu_custom_call" | custom-call | flops 14495514624 | bytes 11796480 | tf_op jit(solution)/shard_map/expert/pallas_call | solution.py:428
  362.9 13.7 %collective-permute-done.32.refs_3_ = bf16[512,768]{1,0:T(8,128)(2,1)S(1)} collective-permute-done((bf16[512,768]{1,0:T(8,128)(2,1)}, bf16[512,768]{1,0:T(8,128)(2,1)S(1)}, u32[]{:S(2)}, u32[]{:S(2)}) %collective-permute-start.32) | collective-permute-done | bytes 786464 | tf_op jit(solution)/shard_map/ppermute | solution.py:36
  393.1 12.6 %collective-permute-done.33.refs_1_ = bf16[512,768]{1,0:T(8,128)(2,1)} collective-permute-done((bf16[512,768]{1,0:T(8,128)(2,1)}, bf16[512,768]{1,0:T(8,128)(2,1)}, u32[]{:S(2)}, u32[]{:S(2)}) %collective-permute-start.33) | collective-permute-done | bytes 786464 | tf_op jit(solution)/shard_map/ppermute | solution.py:36
  407.0 15.3 %collective-permute-done.36.refs_5_ = bf16[512,768]{1,0:T(8,128)(2,1)} collective-permute-done((bf16[512,768]{1,0:T(8,128)(2,1)}, bf16[512,768]{1,0:T(8,128)(2,1)}, u32[]{:S(2)}, u32[]{:S(2)}) %collective-permute-start.36) | collective-permute-done | bytes 786464 | tf_op jit(solution)/shard_map/ppermute | solution.py:36
  425.0 7.1 %combine.2 = f32[1024,768]{1,0:T(8,128)} custom-call(s32[1024,1]{1,0:T(8,128)} %get-tuple-element.218.id_ref, bf16[1024,768]{1,0:T(8,128)(2,1)} %bitcast.47.refs_0_, bf16[1024,768]{1,0:T(8,128)(2,1)} %bitcast.48.refs_1_), custom_call_target="tpu_custom_call" | custom-call | flops 3221225472 | bytes 6291456 | tf_op jit(solution)/shard_map/combine/pallas_call | solution.py:269
  458.6 22.9 %attend_back.1.g_ref = bf16[3,1024,768]{2,1,0:T(8,128)(2,1)} custom-call(bf16[1024,2432]{1,0:T(8,128)(2,1)} %add_convert_fusion.q_ref.k_ref.v_ref, bf16[1024,2432]{1,0:T(8,128)(2,1)} %add_convert_fusion.q_ref.k_ref.v_ref, bf16[1024,2432]{1,0:T(8,128)(2,1)} %add_convert_fusion.q_ref.k_ref.v_ref, bf16[1024,768]{1,0:T(8,128)(2,1)} %convolution_convert_fusion.g_ref, ...), custom_call_target="tpu_custom_call" | custom-call | flops 1 | bytes 1 | tf_op jit(solution)/shard_map/attend_back/pallas_call | solution.py:205
  481.6 10.1 %input_back.1 = (f32[1024,768]{1,0:T(8,128)}, f32[128,768]{1,0:T(8,128)}) custom-call(bf16[3,1024,768]{2,1,0:T(8,128)(2,1)} %attend_back.1.g_ref, bf16[768,2432]{1,0:T(8,128)(2,1)} %bitcast.143, bf16[1024,768]{1,0:T(8,128)(2,1)} %x_ref.3, f32[1024,768]{1,0:T(8,128)} %get-tuple-element.307.dy_ref, f32[1,768]{1,0:T(1,128)} %get-tuple-element.343.gain_ref), custom_call_target="tpu_custom_call" | custom-call | flops 1 | bytes 1 | tf_op jit(solution)/shard_map/input_back/pallas_call | solution.py:576
  491.6 10.2 %outer.1 = bf16[768,3328]{1,0:T(8,128)(2,1)} custom-call(bf16[768,1024]{1,0:T(8,128)(2,1)} %get-tuple-element.179.h_ref, bf16[768,1024]{1,0:T(8,128)(2,1)} %get-tuple-element.241.a_ref, bf16[3,1024,768]{2,1,0:T(8,128)(2,1)} %attend_back.1.g_ref, bf16[1024,768]{1,0:T(8,128)(2,1)} %get-tuple-element.306.b_ref, bf16[768,128]{1,0:T(8,128)(2,1)} %pad.30.rest_ref, ...), custom_call_target="tpu_custom_call" | custom-call | flops 1 | bytes 1 | tf_op jit(solution)/shard_map/outer/pallas_call | solution.py:537
  511.3 5.7 fusion
  517.0 13.3 %all-to-all-done.5 = bf16[8,4,64,768]{3,2,1,0:T(8,128)(2,1)} async-done(((bf16[8,4,64,768]{3,2,1,0:T(8,128)(2,1)}), bf16[8,4,64,768]{3,2,1,0:T(8,128)(2,1)}, u32[]{:S(2)}, u32[]{:S(2)}) %all-to-all-start.5) | async-done | bytes 3145760 | tf_op jit(solution)/shard_map/all_to_all | solution.py:92
  536.6 14.0 %finish.1 = (f32[4,768,768]{2,1,0:T(8,128)}, f32[4,768,768]{2,1,0:T(8,128)}, f32[4,16,768]{2,1,0:T(8,128)}) custom-call(bf16[1,1552,768]{2,1,0:T(8,128)(2,1)} %get-tuple-element.266.refs_0_.refs_1_.refs_2_, bf16[1,1552,768]{2,1,0:T(8,128)(2,1)} %get-tuple-element.266.refs_0_.refs_1_.refs_2_, ...), custom_call_target="tpu_custom_call" | custom-call | flops 9535488 | bytes 38141952 | tf_op jit(solution)/shard_map/finish/pallas_call | solution.py:467
  552.1 7.0 %combine.3 = f32[1024,768]{1,0:T(8,128)} custom-call(s32[1024,1]{1,0:T(8,128)} %get-tuple-element.218.id_ref, bf16[2048,768]{1,0:T(8,128)(2,1)} %bitcast.51.refs_0_), custom_call_target="tpu_custom_call" | custom-call | flops 3221225472 | bytes 6291456 | tf_op jit(solution)/shard_map/combine/pallas_call | solution.py:269
  576.3 6.2 %collective-permute-done.49 = bf16[24,3328]{1,0:T(8,128)(2,1)S(1)} collective-permute-done((bf16[24,3328]{1,0:T(8,128)(2,1)S(1)}, bf16[24,3328]{1,0:T(8,128)(2,1)S(1)}, u32[]{:S(2)}, u32[]{:S(2)}) %collective-permute-start.49) | collective-permute-done | bytes 159776 | tf_op jit(solution)/shard_map/ppermute | solution.py:41
  (286 shorter events, 237.2 us)
Async XLA Ops:
  2.2 47.7 %collective-permute-start.11 = (bf16[24,896]{1,0:T(8,128)(2,1)S(1)}, bf16[24,896]{1,0:T(8,128)(2,1)S(1)}, u32[]{:S(2)}, u32[]{:S(2)}) collective-permute-start(bf16[24,896]{1,0:T(8,128)(2,1)S(1)} %pad_maximum_fusion.4), channel_id=1, source_target_pairs={{0,2},{1,3},{2,4},{3,5},{4,6},{5,7},{6,0},{7,1},{8,10},{9,11},{10,... | collective-permute-start | bytes 129032 | tf_op jit(solution)/shard_map/ppermute | solution.py:41
  5.2 44.7 %collective-permute-start.10 = (bf16[24,896]{1,0:T(8,128)(2,1)S(1)}, bf16[24,896]{1,0:T(8,128)(2,1)S(1)}, u32[]{:S(2)}, u32[]{:S(2)}) collective-permute-start(bf16[24,896]{1,0:T(8,128)(2,1)S(1)} %pad_maximum_fusion.4), channel_id=1, source_target_pairs={{0,4},{1,5},{2,6},{3,7},{4,0},{5,1},{6,2},{7,3},{8,12},{9,13},{10,... | collective-permute-start | bytes 129032 | tf_op jit(solution)/shard_map/ppermute | solution.py:41
  50.1 76.2 %all-to-all-start = ((bf16[8,4,64,768]{3,2,1,0:T(8,128)(2,1)}), bf16[8,4,64,768]{3,2,1,0:T(8,128)(2,1)}, u32[]{:S(2)}, u32[]{:S(2)}) async-start(bf16[8,4,64,768]{3,2,1,0:T(8,128)(2,1)} %bitcast.150), calls=%async_computation | async-start | bytes 6291456 | tf_op jit(solution)/shard_map/all_to_all | solution.py:92
  58.3 37.2 %collective-permute-start.7 = (bf16[1,768,768]{2,1,0:T(8,128)(2,1)}, bf16[1,768,768]{2,1,0:T(8,128)(2,1)}, u32[]{:S(2)}, u32[]{:S(2)}) collective-permute-start(bf16[1,768,768]{2,1,0:T(8,128)(2,1)} %get-tuple-element.166), channel_id=1, source_target_pairs={{0,8},{8,0},{16,24},{24,16},{1,9},{9,1},{17,25},{25,17},{2,10},{10... | collective-permute-start | bytes 3538952 | tf_op jit(solution)/shard_map/ppermute | solution.py:36
  59.8 35.7 %collective-permute-start.8 = (bf16[1,768,768]{2,1,0:T(8,128)(2,1)}, bf16[1,768,768]{2,1,0:T(8,128)(2,1)}, u32[]{:S(2)}, u32[]{:S(2)}) collective-permute-start(bf16[1,768,768]{2,1,0:T(8,128)(2,1)} %get-tuple-element.167), channel_id=1, source_target_pairs={{0,16},{8,24},{16,0},{24,8},{1,17},{9,25},{17,1},{25,9},{2,18},{10... | collective-permute-start | bytes 3538952 | tf_op jit(solution)/shard_map/ppermute | solution.py:36
  77.9 39.0 %collective-permute-start.16 = (bf16[1,768,768]{2,1,0:T(8,128)(2,1)}, bf16[1,768,768]{2,1,0:T(8,128)(2,1)}, u32[]{:S(2)}, u32[]{:S(2)}) collective-permute-start(bf16[1,768,768]{2,1,0:T(8,128)(2,1)} %get-tuple-element.176), channel_id=1, source_target_pairs={{0,8},{8,0},{16,24},{24,16},{1,9},{9,1},{17,25},{25,17},{2,10},{10... | collective-permute-start | bytes 3538952 | tf_op jit(solution)/shard_map/ppermute | solution.py:36
  78.4 38.5 %collective-permute-start.17 = (bf16[1,768,768]{2,1,0:T(8,128)(2,1)}, bf16[1,768,768]{2,1,0:T(8,128)(2,1)}, u32[]{:S(2)}, u32[]{:S(2)}) collective-permute-start(bf16[1,768,768]{2,1,0:T(8,128)(2,1)} %get-tuple-element.177), channel_id=1, source_target_pairs={{0,16},{8,24},{16,0},{24,8},{1,17},{9,25},{17,1},{25,9},{2,18},{10... | collective-permute-start | bytes 3538952 | tf_op jit(solution)/shard_map/ppermute | solution.py:36
  131.2 42.7 %all-to-all-start.1 = ((bf16[8,2,64,768]{3,2,1,0:T(8,128)(2,1)}), bf16[8,2,64,768]{3,2,1,0:T(8,128)(2,1)}, u32[]{:S(2)}, u32[]{:S(2)}) async-start(bf16[8,2,64,768]{3,2,1,0:T(8,128)(2,1)} %bitcast.152), calls=%async_computation.1 | async-start | bytes 3145728 | tf_op jit(solution)/shard_map/all_to_all | solution.py:92
  137.3 101.2 %collective-permute-start.31 = (bf16[4,1,768]{2,1,0:T(2,128)(2,1)}, bf16[4,1,768]{2,1,0:T(2,128)(2,1)}, u32[]{:S(2)}, u32[]{:S(2)}) collective-permute-start(bf16[4,1,768]{2,1,0:T(2,128)(2,1)} %copy.97), channel_id=1, source_target_pairs={{0,16},{8,24},{16,0},{24,8},{1,17},{9,25},{17,1},{25,9},{2,18},{10... | collective-permute-start | bytes 18440 | tf_op jit(solution)/shard_map/ppermute | solution.py:36
  138.8 51.1 %collective-permute-start.22 = (bf16[4,1,768]{2,1,0:T(2,128)(2,1)}, bf16[4,1,768]{2,1,0:T(2,128)(2,1)}, u32[]{:S(2)}, u32[]{:S(2)}) collective-permute-start(bf16[4,1,768]{2,1,0:T(2,128)(2,1)} %copy.97), channel_id=1, source_target_pairs={{0,8},{8,0},{16,24},{24,16},{1,9},{9,1},{17,25},{25,17},{2,10},{10... | collective-permute-start | bytes 18440 | tf_op jit(solution)/shard_map/ppermute | solution.py:36
  140.9 95.6 %collective-permute-start.25 = (bf16[1,768,768]{2,1,0:T(8,128)(2,1)}, bf16[1,768,768]{2,1,0:T(8,128)(2,1)}, u32[]{:S(2)}, u32[]{:S(2)}) collective-permute-start(bf16[1,768,768]{2,1,0:T(8,128)(2,1)} %get-tuple-element.192), channel_id=1, source_target_pairs={{0,8},{8,0},{16,24},{24,16},{1,9},{9,1},{17,25},{25,17},{2,10},{10... | collective-permute-start | bytes 3538952 | tf_op jit(solution)/shard_map/ppermute | solution.py:36
  173.9 60.2 %all-to-all-start.2 = ((bf16[8,2,64,768]{3,2,1,0:T(8,128)(2,1)}), bf16[8,2,64,768]{3,2,1,0:T(8,128)(2,1)}, u32[]{:S(2)}, u32[]{:S(2)}) async-start(bf16[8,2,64,768]{3,2,1,0:T(8,128)(2,1)} %bitcast.151), calls=%async_computation.2 | async-start | bytes 3145728 | tf_op jit(solution)/shard_map/all_to_all | solution.py:92
  189.9 48.1 %collective-permute-start.30 = (bf16[1,768,768]{2,1,0:T(8,128)(2,1)}, bf16[1,768,768]{2,1,0:T(8,128)(2,1)}, u32[]{:S(2)}, u32[]{:S(2)}) collective-permute-start(bf16[1,768,768]{2,1,0:T(8,128)(2,1)} %get-tuple-element.198), channel_id=1, source_target_pairs={{0,16},{8,24},{16,0},{24,8},{1,17},{9,25},{17,1},{25,9},{2,18},{10... | collective-permute-start | bytes 3538952 | tf_op jit(solution)/shard_map/ppermute | solution.py:36
  190.4 48.1 %collective-permute-start.34 = (bf16[8,1,64,768]{3,2,1,0:T(8,128)(2,1)}, bf16[8,1,64,768]{3,2,1,0:T(8,128)(2,1)}, u32[]{:S(2)}, u32[]{:S(2)}) collective-permute-start(bf16[8,1,64,768]{3,2,1,0:T(8,128)(2,1)} %get-tuple-element.311), channel_id=1, source_target_pairs={{0,8},{8,0},{16,24},{24,16},{1,9},{9,1},{17,25},{25,17},{2,10},{10... | collective-permute-start | bytes 2359304 | tf_op jit(solution)/shard_map/ppermute | solution.py:36
  270.7 60.9 %collective-permute-start.29 = (bf16[8,1,64,768]{3,2,1,0:T(8,128)(2,1)}, bf16[8,1,64,768]{3,2,1,0:T(8,128)(2,1)}, u32[]{:S(2)}, u32[]{:S(2)}) collective-permute-start(bf16[8,1,64,768]{3,2,1,0:T(8,128)(2,1)} %get-tuple-element.312), channel_id=1, source_target_pairs={{0,8},{8,0},{16,24},{24,16},{1,9},{9,1},{17,25},{25,17},{2,10},{10... | collective-permute-start | bytes 2359304 | tf_op jit(solution)/shard_map/ppermute | solution.py:36
  291.5 89.1 %all-to-all-start.3 = ((bf16[8,2,64,768]{3,2,1,0:T(8,128)(2,1)}), bf16[8,2,64,768]{3,2,1,0:T(8,128)(2,1)}, u32[]{:S(2)}, u32[]{:S(2)}) async-start(bf16[8,2,64,768]{3,2,1,0:T(8,128)(2,1)} %merge.3), calls=%async_computation.3 | async-start | bytes 3145728 | tf_op jit(solution)/shard_map/all_to_all | solution.py:92
  296.4 84.3 %collective-permute-start.40 = (bf16[1,1552,768]{2,1,0:T(8,128)(2,1)}, bf16[1,1552,768]{2,1,0:T(8,128)(2,1)}, u32[]{:S(2)}, u32[]{:S(2)}) collective-permute-start(bf16[1,1552,768]{2,1,0:T(8,128)(2,1)} %get-tuple-element.223), channel_id=1, source_target_pairs={{0,8},{8,0},{16,24},{24,16},{1,9},{9,1},{17,25},{25,17},{2,10},{10... | collective-permute-start | bytes 7151624 | tf_op jit(solution)/shard_map/ppermute | solution.py:36
  297.9 82.8 %collective-permute-start.41 = (bf16[1,1552,768]{2,1,0:T(8,128)(2,1)}, bf16[1,1552,768]{2,1,0:T(8,128)(2,1)}, u32[]{:S(2)}, u32[]{:S(2)}) collective-permute-start(bf16[1,1552,768]{2,1,0:T(8,128)(2,1)} %get-tuple-element.225), channel_id=1, source_target_pairs={{0,16},{8,24},{16,0},{24,8},{1,17},{9,25},{17,1},{25,9},{2,18},{10... | collective-permute-start | bytes 7151624 | tf_op jit(solution)/shard_map/ppermute | solution.py:36
  380.7 44.3 %all-to-all-start.4 = ((bf16[8,2,64,768]{3,2,1,0:T(8,128)(2,1)}), bf16[8,2,64,768]{3,2,1,0:T(8,128)(2,1)}, u32[]{:S(2)}, u32[]{:S(2)}) async-start(bf16[8,2,64,768]{3,2,1,0:T(8,128)(2,1)} %merge.4), calls=%async_computation.4 | async-start | bytes 3145728 | tf_op jit(solution)/shard_map/all_to_all | solution.py:92
  387.2 35.1 %collective-permute-start.36 = (bf16[512,768]{1,0:T(8,128)(2,1)}, bf16[512,768]{1,0:T(8,128)(2,1)}, u32[]{:S(2)}, u32[]{:S(2)}) collective-permute-start(bf16[512,768]{1,0:T(8,128)(2,1)} %get-tuple-element.214), channel_id=1, source_target_pairs={{0,16},{8,24},{16,0},{24,8},{1,17},{9,25},{17,1},{25,9},{2,18},{10... | collective-permute-start | bytes 2359304 | tf_op jit(solution)/shard_map/ppermute | solution.py:36
  388.2 34.7 %collective-permute-start.37 = (bf16[512,768]{1,0:T(8,128)(2,1)}, bf16[512,768]{1,0:T(8,128)(2,1)}, u32[]{:S(2)}, u32[]{:S(2)}) collective-permute-start(bf16[512,768]{1,0:T(8,128)(2,1)} %get-tuple-element.217), channel_id=1, source_target_pairs={{0,8},{8,0},{16,24},{24,16},{1,9},{9,1},{17,25},{25,17},{2,10},{10... | collective-permute-start | bytes 2359304 | tf_op jit(solution)/shard_map/ppermute | solution.py:36
  422.9 58.7 %collective-permute-start.42 = (bf16[1,1552,768]{2,1,0:T(8,128)(2,1)}, bf16[1,1552,768]{2,1,0:T(8,128)(2,1)}, u32[]{:S(2)}, u32[]{:S(2)}) collective-permute-start(bf16[1,1552,768]{2,1,0:T(8,128)(2,1)} %get-tuple-element.245), channel_id=1, source_target_pairs={{0,8},{8,0},{16,24},{24,16},{1,9},{9,1},{17,25},{25,17},{2,10},{10... | collective-permute-start | bytes 7151624 | tf_op jit(solution)/shard_map/ppermute | solution.py:36
  423.8 57.7 %collective-permute-start.43 = (bf16[1,1552,768]{2,1,0:T(8,128)(2,1)}, bf16[1,1552,768]{2,1,0:T(8,128)(2,1)}, u32[]{:S(2)}, u32[]{:S(2)}) collective-permute-start(bf16[1,1552,768]{2,1,0:T(8,128)(2,1)} %get-tuple-element.247), channel_id=1, source_target_pairs={{0,16},{8,24},{16,0},{24,8},{1,17},{9,25},{17,1},{25,9},{2,18},{10... | collective-permute-start | bytes 7151624 | tf_op jit(solution)/shard_map/ppermute | solution.py:36
  453.9 76.4 %all-to-all-start.5 = ((bf16[8,4,64,768]{3,2,1,0:T(8,128)(2,1)}), bf16[8,4,64,768]{3,2,1,0:T(8,128)(2,1)}, u32[]{:S(2)}, u32[]{:S(2)}) async-start(bf16[8,4,64,768]{3,2,1,0:T(8,128)(2,1)} %merge.5), calls=%async_computation.5 | async-start | bytes 6291456 | tf_op jit(solution)/shard_map/all_to_all | solution.py:92
  (64 other events, 863.1 us)

commit v4 on v3

--- a/solution.py
+++ b/solution.py
@@ -79,10 +79,9 @@
     mine = jnp.where(mc == 0, g[:, :, 0], g[:, :, 1])
     other = swap(jnp.where(mc == 0, g[:, :, 1], g[:, :, 0]), "expert", 1)
     s = (mine.astype(F32) + other.astype(F32)).astype(BF16)
-    s, before = after((s, before), before)
     made = beside(after(before, s))
     pick = lambda t, i: lax.dynamic_index_in_dim(t, i, 0, keepdims=False)
-    parts = after([swap(pick(s, mb ^ k), "batch", k) for k in (1, 2, 3)], made)
+    parts = after([swap(pick(s, mb ^ k), "batch", k) for k in (1, 2, 3)], made, before)
     t = sum((p.astype(F32) for p in parts), pick(s, mb).astype(F32)).astype(BF16)
     parts = [shift(pick(t, (mz + k) % 4), 2 * k) for k in (1, 2, 3)]
     return sum((p.astype(F32) for p in parts), pick(t, mz).astype(F32)), made
@@ -150,9 +149,7 @@
         ],
         scratch_shapes=[pltpu.VMEM((length // QROWS, QROWS, QROWS + REACH), F32)],
         compiler_params=pltpu.CompilerParams(vmem_limit_bytes=VMEM),
-        cost_estimate=pl.CostEstimate(
-            flops=4 * length * 512 * width, bytes_accessed=12 * length * width, transcendentals=12 * length * 512
-        ),
+        cost_estimate=COST,
         name="attend",
     )(qkv, qkv, qkv, seg_row, seg_col)
 
@@ -495,6 +492,7 @@
         out_specs=[spec(w_in, 1), spec(w_out, 1)] * groups,
         out_shape=[jax.ShapeDtypeStruct((1, *a.shape[1:]), BF16) for a in (w_in, w_out)] * groups,
         compiler_params=pltpu.CompilerParams(vmem_limit_bytes=VMEM),
+        cost_estimate=COST,
         name="to_send",
     )(w_in, w_out)
     return [flat[2 * l : 2 * l + 2] for l in range(groups)]
@@ -694,13 +692,12 @@
     h_one = (unit_one * gain_one + shift_one).astype(BF16)
     nothing = jnp.zeros((width,), F32)
     bias = jnp.concatenate([bias_query, nothing, bias_value, jnp.zeros((wide.shape[1] - 3 * width,), F32)])
-    qkv = (dot(h_one, wide) + bias).astype(BF16)
+    qkv = after((dot(h_one, wide) + bias).astype(BF16), [w[0] for w in got_w[:chunk]])
     if staged():
         rest = gather_second(rest, qkv)
     seg_row = segment_ids.reshape(1, row_count)
     seg_col = segment_ids.reshape(row_count, 1)
     attended, logs = attend(qkv, seg_row, seg_col, width)
-    attended = after(attended, [w[0] for w in got_w[:chunk]])
     if staged():
         rest = gather_third(rest, attended)
     full_output = rest[:, :width]

time: 595 us -> 588 us (0.988)
  waiting for transfers between devices: 145 us -> 136 us
    all_to_all x6, waiting for transfers between devices: 26.6 us -> 14.8 us  [to_owners(): return lax.all_to_all(x, 'expert', split_axis=0, concat_axis=0, tiled=True)]
    ppermute x42, waiting for transfers between devices: 107 us -> 115 us  [swap(): lax.ppermute(x, axis, [(i, i ^ mask) for i in range(lax.axis_size(axis))])]
    ppermute x9, waiting for transfers between devices: 12.3 us -> 5.74 us  [shift(): lax.ppermute(x, 'expert', [(i, (i + step) % size) for i in range(size)])]
  transfers between devices with their start and end apart: 57 -> 57, of which waited for: 22 -> 22; matrix products, arithmetic and copies ran while one was open for 16% -> 16% of each run, Pallas kernels for 40% -> 41%
where the time goes in v4:
time: 588 us; the launch traced here: 582 us
  Pallas kernels  243 us (41%)
  waiting for transfers between devices  136 us (23%)
  starting transfers between devices  89.3 us (15%)
  other arithmetic  44.4 us (8%)
  local copies, waits for them, and re-layouts  38.1 us (6%)
  matrix products  27.7 us (5%)
    ppermute x42, waiting for transfers between devices, swap(): lax.ppermute(x, axis, [(i, i ^ mask) for i in range(lax.axis_size(axis))])  115 us
    pallas_call x4, Pallas kernels, expert(): pl.pallas_call(functools.partial(expert_kernel, steps, experts, len(grads...  114 us
    ppermute x42, starting transfers between devices, swap(): lax.ppermute(x, axis, [(i, i ^ mask) for i in range(lax.axis_size(axis))])  45.1 us
    all_to_all x6, starting transfers between devices, to_owners(): return lax.all_to_all(x, 'expert', split_axis=0, concat_axis=0, tiled=True)  27.9 us
    pallas_call x1, Pallas kernels, attend_back(): pl.pallas_call(attend_back_kernel, grid=(pairs,), in_specs=[spec(0), spec...  22.9 us
    pallas_call x3, Pallas kernels, dispatch(): pl.pallas_call(functools.partial(dispatch_kernel, layout, first), grid=(c...  17.6 us
    dot_general x5, matrix products, dot(): return jnp.dot(a, b, preferred_element_type=F32)  16.8 us
    pallas_call x1, Pallas kernels, attend(): pl.pallas_call(attend_kernel, grid=(pairs,), in_specs=[spec(0), spec(pair...  16.5 us
  transfers between devices with their start and end apart: 57, of which 22 were waited for; matrix products, arithmetic and copies ran while one was open for 16% of the time, Pallas kernels for 41%

profile of v4, /device:TPU:0, one launch (start us, length us, event | category | flops | bytes accessed | tf_op | source)
XLA Modules:
  0.0 581.6 jit_solution(18262061727374099250)
XLA Ops:
  26.4 7.6 %dispatch.3 = bf16[2048,768]{1,0:T(8,128)(2,1)} custom-call(s32[1,1024]{1,0:T(1,128)} %reshape_select_fusion.id_ref, bf16[1024,768]{1,0:T(8,128)(2,1)} %x_ref.2), custom_call_target="tpu_custom_call" | custom-call | flops 3221225472 | bytes 6291456 | tf_op jit(solution)/shard_map/dispatch/pallas_call | solution.py:236
  34.1 8.7 %to_send.1 = (bf16[1,768,768]{2,1,0:T(8,128)(2,1)}, bf16[1,768,768]{2,1,0:T(8,128)(2,1)}, bf16[1,768,768]{2,1,0:T(8,128)(2,1)}, bf16[1,768,768]{2,1,0:T(8,128)(2...) custom-call(bf16[4,768,768]{2,1,0:T(8,128)(2,1)} %refs_5_.7, ...), custom_call_target="tpu_custom_call" | custom-call | flops 1 | bytes 1 | tf_op jit(solution)/shard_map/to_send/pallas_call | solution.py:488
  67.1 8.5 %add_convert_fusion.q_ref.k_ref.v_ref = bf16[1024,2432]{1,0:T(8,128)(2,1)} fusion(bf16[1024,768]{1,0:T(8,128)(2,1)S(1)} %fusion.7.x_ref, bf16[768,2432]{1,0:T(8,128)(2,1)} %bitcast.141, f32[2432]{0:T(1024)S(1)} %pad_maximum_fusion.5), kind=kOutput, calls=%fused_computation | convolution fusion | flops 3830185984 | bytes 10298880 | tf_op jit(solution)/shard_map/dot_general | solution.py:24
  75.6 16.1 %collective-permute-done.7.refs_8_ = bf16[1,768,768]{2,1,0:T(8,128)(2,1)} collective-permute-done((bf16[1,768,768]{2,1,0:T(8,128)(2,1)}, bf16[1,768,768]{2,1,0:T(8,128)(2,1)}, u32[]{:S(2)}, u32[]{:S(2)}) %collective-permute-start.7) | collective-permute-done | bytes 1179680 | tf_op jit(solution)/shard_map/ppermute | solution.py:36
  96.2 16.5 %attend.1 = (bf16[1024,768]{1,0:T(8,128)(2,1)}, f32[1024,768]{1,0:T(8,128)}) custom-call(bf16[1024,2432]{1,0:T(8,128)(2,1)} %add_convert_fusion.q_ref.k_ref.v_ref, bf16[1024,2432]{1,0:T(8,128)(2,1)} %add_convert_fusion.q_ref.k_ref.v_ref, bf16[1024,2432]{1,0:T(8,128)(2,1)} %add_convert_fusion.q_ref.k_ref.v_ref, s32[1,1024]{1,0:T(1,128)} %row_ref.3, ...), custom_call_target="tpu_custom_call" | custom-call | flops 1 | bytes 1 | tf_op jit(solution)/shard_map/attend/pallas_call | solution.py:141
  126.3 5.0 dispatch.4
  156.9 5.0 dispatch.5
  191.9 12.5 %collective-permute-done.20.refs_2_ = bf16[8,1,64,768]{3,2,1,0:T(8,128)(2,1)} collective-permute-done((bf16[8,1,64,768]{3,2,1,0:T(8,128)(2,1)}, bf16[8,1,64,768]{3,2,1,0:T(8,128)(2,1)}, u32[]{:S(2)}, u32[]{:S(2)}) %collective-permute-start.20) | collective-permute-done | bytes 786464 | tf_op jit(solution)/shard_map/ppermute | solution.py:36
  205.7 28.4 %expert.4 = (bf16[512,768]{1,0:T(8,128)(2,1)}, bf16[512,768]{1,0:T(8,128)(2,1)}, bf16[512,768]{1,0:T(8,128)(2,1)}, bf16[512,768]{1,0:T(8,128)(2,1)}, bf16[1,1552...) custom-call(s32[1]{0:T(128)} %bitcast.38.refs_0_, ...), custom_call_target="tpu_custom_call" | custom-call | flops 14495514624 | bytes 11796480 | tf_op jit(solution)/shard_map/expert/pallas_call | solution.py:425
  238.6 28.5 %expert.7 = (bf16[512,768]{1,0:T(8,128)(2,1)}, bf16[512,768]{1,0:T(8,128)(2,1)}, bf16[512,768]{1,0:T(8,128)(2,1)}, bf16[512,768]{1,0:T(8,128)(2,1)}, bf16[1,1552...) custom-call(s32[1]{0:T(128)} %bitcast.46.refs_0_, ...), custom_call_target="tpu_custom_call" | custom-call | flops 14495514624 | bytes 11796480 | tf_op jit(solution)/shard_map/expert/pallas_call | solution.py:425
  271.3 16.7 %collective-permute-done.38.refs_1_ = bf16[512,768]{1,0:T(8,128)(2,1)} collective-permute-done((bf16[512,768]{1,0:T(8,128)(2,1)}, bf16[512,768]{1,0:T(8,128)(2,1)}, u32[]{:S(2)}, u32[]{:S(2)}) %collective-permute-start.38) | collective-permute-done | bytes 786464 | tf_op jit(solution)/shard_map/ppermute | solution.py:36
  291.6 4.9 all-to-all-start.3
  302.8 28.8 %expert.5 = (bf16[512,768]{1,0:T(8,128)(2,1)}, bf16[512,768]{1,0:T(8,128)(2,1)}, bf16[512,768]{1,0:T(8,128)(2,1)}, bf16[512,768]{1,0:T(8,128)(2,1)}, bf16[1,1552...) custom-call(s32[1]{0:T(128)} %bitcast.44.refs_0_, ...), custom_call_target="tpu_custom_call" | custom-call | flops 14495514624 | bytes 11796480 | tf_op jit(solution)/shard_map/expert/pallas_call | solution.py:425
  331.6 28.7 %expert.6 = (bf16[512,768]{1,0:T(8,128)(2,1)}, bf16[512,768]{1,0:T(8,128)(2,1)}, bf16[512,768]{1,0:T(8,128)(2,1)}, bf16[512,768]{1,0:T(8,128)(2,1)}, bf16[1,1552...) custom-call(s32[1]{0:T(128)} %bitcast.45.refs_0_, ...), custom_call_target="tpu_custom_call" | custom-call | flops 14495514624 | bytes 11796480 | tf_op jit(solution)/shard_map/expert/pallas_call | solution.py:425
  362.8 13.8 %collective-permute-done.32.refs_3_ = bf16[512,768]{1,0:T(8,128)(2,1)S(1)} collective-permute-done((bf16[512,768]{1,0:T(8,128)(2,1)}, bf16[512,768]{1,0:T(8,128)(2,1)S(1)}, u32[]{:S(2)}, u32[]{:S(2)}) %collective-permute-start.32) | collective-permute-done | bytes 786464 | tf_op jit(solution)/shard_map/ppermute | solution.py:36
  389.2 16.6 %collective-permute-done.33.refs_1_ = bf16[512,768]{1,0:T(8,128)(2,1)} collective-permute-done((bf16[512,768]{1,0:T(8,128)(2,1)}, bf16[512,768]{1,0:T(8,128)(2,1)}, u32[]{:S(2)}, u32[]{:S(2)}) %collective-permute-start.33) | collective-permute-done | bytes 786464 | tf_op jit(solution)/shard_map/ppermute | solution.py:36
  407.0 15.3 %collective-permute-done.36.refs_5_ = bf16[512,768]{1,0:T(8,128)(2,1)} collective-permute-done((bf16[512,768]{1,0:T(8,128)(2,1)}, bf16[512,768]{1,0:T(8,128)(2,1)}, u32[]{:S(2)}, u32[]{:S(2)}) %collective-permute-start.36) | collective-permute-done | bytes 786464 | tf_op jit(solution)/shard_map/ppermute | solution.py:36
  428.9 7.1 %combine.2 = f32[1024,768]{1,0:T(8,128)} custom-call(s32[1024,1]{1,0:T(8,128)} %get-tuple-element.209.id_ref, bf16[1024,768]{1,0:T(8,128)(2,1)} %bitcast.47.refs_0_, bf16[1024,768]{1,0:T(8,128)(2,1)} %bitcast.48.refs_1_), custom_call_target="tpu_custom_call" | custom-call | flops 3221225472 | bytes 6291456 | tf_op jit(solution)/shard_map/combine/pallas_call | solution.py:266
  462.6 22.9 %attend_back.1.g_ref = bf16[3,1024,768]{2,1,0:T(8,128)(2,1)} custom-call(bf16[1024,2432]{1,0:T(8,128)(2,1)} %add_convert_fusion.q_ref.k_ref.v_ref, bf16[1024,2432]{1,0:T(8,128)(2,1)} %add_convert_fusion.q_ref.k_ref.v_ref, bf16[1024,2432]{1,0:T(8,128)(2,1)} %add_convert_fusion.q_ref.k_ref.v_ref, bf16[1024,768]{1,0:T(8,128)(2,1)} %convolution_convert_fusion.g_ref, ...), custom_call_target="tpu_custom_call" | custom-call | flops 1 | bytes 1 | tf_op jit(solution)/shard_map/attend_back/pallas_call | solution.py:202
  485.5 10.1 %input_back.1 = (f32[1024,768]{1,0:T(8,128)}, f32[128,768]{1,0:T(8,128)}) custom-call(bf16[3,1024,768]{2,1,0:T(8,128)(2,1)} %attend_back.1.g_ref, bf16[768,2432]{1,0:T(8,128)(2,1)} %bitcast.143, bf16[1024,768]{1,0:T(8,128)(2,1)} %x_ref.3, f32[1024,768]{1,0:T(8,128)} %get-tuple-element.289.dy_ref, f32[1,768]{1,0:T(1,128)} %get-tuple-element.325.gain_ref), custom_call_target="tpu_custom_call" | custom-call | flops 1 | bytes 1 | tf_op jit(solution)/shard_map/input_back/pallas_call | solution.py:574
  495.6 10.1 %outer.1 = bf16[768,3328]{1,0:T(8,128)(2,1)} custom-call(bf16[768,1024]{1,0:T(8,128)(2,1)} %get-tuple-element.170.h_ref, bf16[768,1024]{1,0:T(8,128)(2,1)} %get-tuple-element.245.a_ref, bf16[3,1024,768]{2,1,0:T(8,128)(2,1)} %attend_back.1.g_ref, bf16[1024,768]{1,0:T(8,128)(2,1)} %get-tuple-element.288.b_ref, bf16[768,128]{1,0:T(8,128)(2,1)} %pad.30.rest_ref, ...), custom_call_target="tpu_custom_call" | custom-call | flops 1 | bytes 1 | tf_op jit(solution)/shard_map/outer/pallas_call | solution.py:535
  525.7 8.5 %all-to-all-done.5 = bf16[8,4,64,768]{3,2,1,0:T(8,128)(2,1)} async-done(((bf16[8,4,64,768]{3,2,1,0:T(8,128)(2,1)}), bf16[8,4,64,768]{3,2,1,0:T(8,128)(2,1)}, u32[]{:S(2)}, u32[]{:S(2)}) %all-to-all-start.5) | async-done | bytes 3145760 | tf_op jit(solution)/shard_map/all_to_all | solution.py:91
  534.2 14.0 %finish.1 = (f32[4,768,768]{2,1,0:T(8,128)}, f32[4,768,768]{2,1,0:T(8,128)}, f32[4,16,768]{2,1,0:T(8,128)}) custom-call(bf16[1,1552,768]{2,1,0:T(8,128)(2,1)} %get-tuple-element.248.refs_0_.refs_1_.refs_2_, bf16[1,1552,768]{2,1,0:T(8,128)(2,1)} %get-tuple-element.248.refs_0_.refs_1_.refs_2_, ...), custom_call_target="tpu_custom_call" | custom-call | flops 9535488 | bytes 38141952 | tf_op jit(solution)/shard_map/finish/pallas_call | solution.py:464
  561.1 7.0 %combine.3 = f32[1024,768]{1,0:T(8,128)} custom-call(s32[1024,1]{1,0:T(8,128)} %get-tuple-element.209.id_ref, bf16[2048,768]{1,0:T(8,128)(2,1)} %bitcast.51.refs_0_), custom_call_target="tpu_custom_call" | custom-call | flops 3221225472 | bytes 6291456 | tf_op jit(solution)/shard_map/combine/pallas_call | solution.py:266
  (284 shorter events, 236.9 us)
Async XLA Ops:
  2.2 47.8 %collective-permute-start.11 = (bf16[24,896]{1,0:T(8,128)(2,1)S(1)}, bf16[24,896]{1,0:T(8,128)(2,1)S(1)}, u32[]{:S(2)}, u32[]{:S(2)}) collective-permute-start(bf16[24,896]{1,0:T(8,128)(2,1)S(1)} %pad_maximum_fusion.4), channel_id=1, source_target_pairs={{0,2},{1,3},{2,4},{3,5},{4,6},{5,7},{6,0},{7,1},{8,10},{9,11},{10,... | collective-permute-start | bytes 129032 | tf_op jit(solution)/shard_map/ppermute | solution.py:41
  5.2 44.7 %collective-permute-start.10 = (bf16[24,896]{1,0:T(8,128)(2,1)S(1)}, bf16[24,896]{1,0:T(8,128)(2,1)S(1)}, u32[]{:S(2)}, u32[]{:S(2)}) collective-permute-start(bf16[24,896]{1,0:T(8,128)(2,1)S(1)} %pad_maximum_fusion.4), channel_id=1, source_target_pairs={{0,4},{1,5},{2,6},{3,7},{4,0},{5,1},{6,2},{7,3},{8,12},{9,13},{10,... | collective-permute-start | bytes 129032 | tf_op jit(solution)/shard_map/ppermute | solution.py:41
  50.1 76.2 %all-to-all-start = ((bf16[8,4,64,768]{3,2,1,0:T(8,128)(2,1)}), bf16[8,4,64,768]{3,2,1,0:T(8,128)(2,1)}, u32[]{:S(2)}, u32[]{:S(2)}) async-start(bf16[8,4,64,768]{3,2,1,0:T(8,128)(2,1)} %bitcast.150), calls=%async_computation | async-start | bytes 6291456 | tf_op jit(solution)/shard_map/all_to_all | solution.py:91
  54.8 36.9 %collective-permute-start.14 = (bf16[4,24,896]{2,1,0:T(8,128)(2,1)S(1)}, bf16[4,24,896]{2,1,0:T(8,128)(2,1)S(1)}, u32[]{:S(2)}, u32[]{:S(2)}) collective-permute-start(bf16[4,24,896]{2,1,0:T(8,128)(2,1)S(1)} %constant_dynamic-slice_fusion), channel_id=1, source_target_pairs={{0,24},{8,16},{16,8},{24,0},{1,25},{9,17},{17,9},{25,1},{2,26},{10... | collective-permute-start | bytes 516104 | tf_op jit(solution)/shard_map/ppermute | solution.py:36
  57.3 34.4 %collective-permute-start.13 = (bf16[4,24,896]{2,1,0:T(8,128)(2,1)S(1)}, bf16[4,24,896]{2,1,0:T(8,128)(2,1)}, u32[]{:S(2)}, u32[]{:S(2)}) collective-permute-start(bf16[4,24,896]{2,1,0:T(8,128)(2,1)S(1)} %constant_dynamic-slice_fusion), channel_id=1, source_target_pairs={{0,16},{8,24},{16,0},{24,8},{1,17},{9,25},{17,1},{25,9},{2,18},{10... | collective-permute-start | bytes 516104 | tf_op jit(solution)/shard_map/ppermute | solution.py:36
  57.8 33.9 %collective-permute-start.12 = (bf16[4,24,896]{2,1,0:T(8,128)(2,1)S(1)}, bf16[4,24,896]{2,1,0:T(8,128)(2,1)}, u32[]{:S(2)}, u32[]{:S(2)}) collective-permute-start(bf16[4,24,896]{2,1,0:T(8,128)(2,1)S(1)} %constant_dynamic-slice_fusion), channel_id=1, source_target_pairs={{0,8},{8,0},{16,24},{24,16},{1,9},{9,1},{17,25},{25,17},{2,10},{10... | collective-permute-start | bytes 516104 | tf_op jit(solution)/shard_map/ppermute | solution.py:36
  131.3 42.7 %all-to-all-start.1 = ((bf16[8,2,64,768]{3,2,1,0:T(8,128)(2,1)}), bf16[8,2,64,768]{3,2,1,0:T(8,128)(2,1)}, u32[]{:S(2)}, u32[]{:S(2)}) async-start(bf16[8,2,64,768]{3,2,1,0:T(8,128)(2,1)} %bitcast.152), calls=%async_computation.1 | async-start | bytes 3145728 | tf_op jit(solution)/shard_map/all_to_all | solution.py:91
  137.4 101.2 %collective-permute-start.31 = (bf16[4,1,768]{2,1,0:T(2,128)(2,1)}, bf16[4,1,768]{2,1,0:T(2,128)(2,1)}, u32[]{:S(2)}, u32[]{:S(2)}) collective-permute-start(bf16[4,1,768]{2,1,0:T(2,128)(2,1)} %copy.97), channel_id=1, source_target_pairs={{0,16},{8,24},{16,0},{24,8},{1,17},{9,25},{17,1},{25,9},{2,18},{10... | collective-permute-start | bytes 18440 | tf_op jit(solution)/shard_map/ppermute | solution.py:36
  138.9 51.0 %collective-permute-start.22 = (bf16[4,1,768]{2,1,0:T(2,128)(2,1)}, bf16[4,1,768]{2,1,0:T(2,128)(2,1)}, u32[]{:S(2)}, u32[]{:S(2)}) collective-permute-start(bf16[4,1,768]{2,1,0:T(2,128)(2,1)} %copy.97), channel_id=1, source_target_pairs={{0,8},{8,0},{16,24},{24,16},{1,9},{9,1},{17,25},{25,17},{2,10},{10... | collective-permute-start | bytes 18440 | tf_op jit(solution)/shard_map/ppermute | solution.py:36
  140.9 95.6 %collective-permute-start.25 = (bf16[1,768,768]{2,1,0:T(8,128)(2,1)}, bf16[1,768,768]{2,1,0:T(8,128)(2,1)}, u32[]{:S(2)}, u32[]{:S(2)}) collective-permute-start(bf16[1,768,768]{2,1,0:T(8,128)(2,1)} %get-tuple-element.183), channel_id=1, source_target_pairs={{0,8},{8,0},{16,24},{24,16},{1,9},{9,1},{17,25},{25,17},{2,10},{10... | collective-permute-start | bytes 3538952 | tf_op jit(solution)/shard_map/ppermute | solution.py:36
  173.9 60.1 %all-to-all-start.2 = ((bf16[8,2,64,768]{3,2,1,0:T(8,128)(2,1)}), bf16[8,2,64,768]{3,2,1,0:T(8,128)(2,1)}, u32[]{:S(2)}, u32[]{:S(2)}) async-start(bf16[8,2,64,768]{3,2,1,0:T(8,128)(2,1)} %bitcast.151), calls=%async_computation.2 | async-start | bytes 3145728 | tf_op jit(solution)/shard_map/all_to_all | solution.py:91
  189.9 48.1 %collective-permute-start.30 = (bf16[1,768,768]{2,1,0:T(8,128)(2,1)}, bf16[1,768,768]{2,1,0:T(8,128)(2,1)}, u32[]{:S(2)}, u32[]{:S(2)}) collective-permute-start(bf16[1,768,768]{2,1,0:T(8,128)(2,1)} %get-tuple-element.189), channel_id=1, source_target_pairs={{0,16},{8,24},{16,0},{24,8},{1,17},{9,25},{17,1},{25,9},{2,18},{10... | collective-permute-start | bytes 3538952 | tf_op jit(solution)/shard_map/ppermute | solution.py:36
  190.4 48.2 %collective-permute-start.34 = (bf16[8,1,64,768]{3,2,1,0:T(8,128)(2,1)}, bf16[8,1,64,768]{3,2,1,0:T(8,128)(2,1)}, u32[]{:S(2)}, u32[]{:S(2)}) collective-permute-start(bf16[8,1,64,768]{3,2,1,0:T(8,128)(2,1)} %get-tuple-element.293), channel_id=1, source_target_pairs={{0,8},{8,0},{16,24},{24,16},{1,9},{9,1},{17,25},{25,17},{2,10},{10... | collective-permute-start | bytes 2359304 | tf_op jit(solution)/shard_map/ppermute | solution.py:36
  204.4 34.2 %collective-permute-start.26 = (bf16[8,1,64,768]{3,2,1,0:T(8,128)(2,1)}, bf16[8,1,64,768]{3,2,1,0:T(8,128)(2,1)}, u32[]{:S(2)}, u32[]{:S(2)}) collective-permute-start(bf16[8,1,64,768]{3,2,1,0:T(8,128)(2,1)} %get-tuple-element.186), channel_id=1, source_target_pairs={{0,8},{8,0},{16,24},{24,16},{1,9},{9,1},{17,25},{25,17},{2,10},{10... | collective-permute-start | bytes 2359304 | tf_op jit(solution)/shard_map/ppermute | solution.py:36
  270.8 60.9 %collective-permute-start.29 = (bf16[8,1,64,768]{3,2,1,0:T(8,128)(2,1)}, bf16[8,1,64,768]{3,2,1,0:T(8,128)(2,1)}, u32[]{:S(2)}, u32[]{:S(2)}) collective-permute-start(bf16[8,1,64,768]{3,2,1,0:T(8,128)(2,1)} %get-tuple-element.294), channel_id=1, source_target_pairs={{0,8},{8,0},{16,24},{24,16},{1,9},{9,1},{17,25},{25,17},{2,10},{10... | collective-permute-start | bytes 2359304 | tf_op jit(solution)/shard_map/ppermute | solution.py:36
  291.6 89.1 %all-to-all-start.3 = ((bf16[8,2,64,768]{3,2,1,0:T(8,128)(2,1)}), bf16[8,2,64,768]{3,2,1,0:T(8,128)(2,1)}, u32[]{:S(2)}, u32[]{:S(2)}) async-start(bf16[8,2,64,768]{3,2,1,0:T(8,128)(2,1)} %merge.3), calls=%async_computation.3 | async-start | bytes 3145728 | tf_op jit(solution)/shard_map/all_to_all | solution.py:91
  296.5 84.2 %collective-permute-start.40 = (bf16[1,1552,768]{2,1,0:T(8,128)(2,1)}, bf16[1,1552,768]{2,1,0:T(8,128)(2,1)}, u32[]{:S(2)}, u32[]{:S(2)}) collective-permute-start(bf16[1,1552,768]{2,1,0:T(8,128)(2,1)} %get-tuple-element.214), channel_id=1, source_target_pairs={{0,8},{8,0},{16,24},{24,16},{1,9},{9,1},{17,25},{25,17},{2,10},{10... | collective-permute-start | bytes 7151624 | tf_op jit(solution)/shard_map/ppermute | solution.py:36
  297.9 82.7 %collective-permute-start.41 = (bf16[1,1552,768]{2,1,0:T(8,128)(2,1)}, bf16[1,1552,768]{2,1,0:T(8,128)(2,1)}, u32[]{:S(2)}, u32[]{:S(2)}) collective-permute-start(bf16[1,1552,768]{2,1,0:T(8,128)(2,1)} %get-tuple-element.216), channel_id=1, source_target_pairs={{0,16},{8,24},{16,0},{24,8},{1,17},{9,25},{17,1},{25,9},{2,18},{10... | collective-permute-start | bytes 7151624 | tf_op jit(solution)/shard_map/ppermute | solution.py:36
  380.6 48.3 %all-to-all-start.4 = ((bf16[8,2,64,768]{3,2,1,0:T(8,128)(2,1)}), bf16[8,2,64,768]{3,2,1,0:T(8,128)(2,1)}, u32[]{:S(2)}, u32[]{:S(2)}) async-start(bf16[8,2,64,768]{3,2,1,0:T(8,128)(2,1)} %merge.4), calls=%async_computation.4 | async-start | bytes 3145728 | tf_op jit(solution)/shard_map/all_to_all | solution.py:91
  387.2 35.1 %collective-permute-start.36 = (bf16[512,768]{1,0:T(8,128)(2,1)}, bf16[512,768]{1,0:T(8,128)(2,1)}, u32[]{:S(2)}, u32[]{:S(2)}) collective-permute-start(bf16[512,768]{1,0:T(8,128)(2,1)} %get-tuple-element.205), channel_id=1, source_target_pairs={{0,16},{8,24},{16,0},{24,8},{1,17},{9,25},{17,1},{25,9},{2,18},{10... | collective-permute-start | bytes 2359304 | tf_op jit(solution)/shard_map/ppermute | solution.py:36
  388.2 34.7 %collective-permute-start.37 = (bf16[512,768]{1,0:T(8,128)(2,1)}, bf16[512,768]{1,0:T(8,128)(2,1)}, u32[]{:S(2)}, u32[]{:S(2)}) collective-permute-start(bf16[512,768]{1,0:T(8,128)(2,1)} %get-tuple-element.208), channel_id=1, source_target_pairs={{0,8},{8,0},{16,24},{24,16},{1,9},{9,1},{17,25},{25,17},{2,10},{10... | collective-permute-start | bytes 2359304 | tf_op jit(solution)/shard_map/ppermute | solution.py:36
  422.9 62.6 %collective-permute-start.42 = (bf16[1,1552,768]{2,1,0:T(8,128)(2,1)}, bf16[1,1552,768]{2,1,0:T(8,128)(2,1)}, u32[]{:S(2)}, u32[]{:S(2)}) collective-permute-start(bf16[1,1552,768]{2,1,0:T(8,128)(2,1)} %get-tuple-element.238), channel_id=1, source_target_pairs={{0,8},{8,0},{16,24},{24,16},{1,9},{9,1},{17,25},{25,17},{2,10},{10... | collective-permute-start | bytes 7151624 | tf_op jit(solution)/shard_map/ppermute | solution.py:36
  423.8 61.6 %collective-permute-start.43 = (bf16[1,1552,768]{2,1,0:T(8,128)(2,1)}, bf16[1,1552,768]{2,1,0:T(8,128)(2,1)}, u32[]{:S(2)}, u32[]{:S(2)}) collective-permute-start(bf16[1,1552,768]{2,1,0:T(8,128)(2,1)} %get-tuple-element.240), channel_id=1, source_target_pairs={{0,16},{8,24},{16,0},{24,8},{1,17},{9,25},{17,1},{25,9},{2,18},{10... | collective-permute-start | bytes 7151624 | tf_op jit(solution)/shard_map/ppermute | solution.py:36
  457.8 76.4 %all-to-all-start.5 = ((bf16[8,4,64,768]{3,2,1,0:T(8,128)(2,1)}), bf16[8,4,64,768]{3,2,1,0:T(8,128)(2,1)}, u32[]{:S(2)}, u32[]{:S(2)}) async-start(bf16[8,4,64,768]{3,2,1,0:T(8,128)(2,1)} %merge.5), calls=%async_computation.5 | async-start | bytes 6291456 | tf_op jit(solution)/shard_map/all_to_all | solution.py:91
  (63 other events, 918.2 us)

commit v5 on v4

--- a/solution.py
+++ b/solution.py
@@ -692,12 +692,13 @@
     h_one = (unit_one * gain_one + shift_one).astype(BF16)
     nothing = jnp.zeros((width,), F32)
     bias = jnp.concatenate([bias_query, nothing, bias_value, jnp.zeros((wide.shape[1] - 3 * width,), F32)])
-    qkv = after((dot(h_one, wide) + bias).astype(BF16), [w[0] for w in got_w[:chunk]])
+    qkv = (dot(h_one, wide) + bias).astype(BF16)
     if staged():
         rest = gather_second(rest, qkv)
     seg_row = segment_ids.reshape(1, row_count)
     seg_col = segment_ids.reshape(row_count, 1)
     attended, logs = attend(qkv, seg_row, seg_col, width)
+    attended = after(attended, [w[0] for w in got_w[:chunk]])
     if staged():
         rest = gather_third(rest, attended)
     full_output = rest[:, :width]

time: 588 us -> 588 us (level)
    all_to_all x6, waiting for transfers between devices: 14.8 us -> 21.8 us  [to_owners(): return lax.all_to_all(x, 'expert', split_axis=0, concat_axis=0, tiled=True)]
  transfers between devices with their start and end apart: 57 -> 57, of which waited for: 22 -> 20; matrix products, arithmetic and copies ran while one was open for 16% -> 16% of each run, Pallas kernels for 41% -> 41%
where the time goes in v5:
time: 588 us; the launch traced here: 582 us
  Pallas kernels  243 us (41%)
  waiting for transfers between devices  137 us (23%)
  starting transfers between devices  88.3 us (15%)
  other arithmetic  44.4 us (8%)
  local copies, waits for them, and re-layouts  38.1 us (6%)
  matrix products  27.7 us (5%)
    pallas_call x4, Pallas kernels, expert(): pl.pallas_call(functools.partial(expert_kernel, steps, experts, len(grads...  114 us
    ppermute x42, waiting for transfers between devices, swap(): lax.ppermute(x, axis, [(i, i ^ mask) for i in range(lax.axis_size(axis))])  110 us
    ppermute x42, starting transfers between devices, swap(): lax.ppermute(x, axis, [(i, i ^ mask) for i in range(lax.axis_size(axis))])  44 us
    all_to_all x6, starting transfers between devices, to_owners(): return lax.all_to_all(x, 'expert', split_axis=0, concat_axis=0, tiled=True)  27.9 us
    pallas_call x1, Pallas kernels, attend_back(): pl.pallas_call(attend_back_kernel, grid=(pairs,), in_specs=[spec(0), spec...  22.9 us
    all_to_all x6, waiting for transfers between devices, to_owners(): return lax.all_to_all(x, 'expert', split_axis=0, concat_axis=0, tiled=True)  21.8 us
    pallas_call x3, Pallas kernels, dispatch(): pl.pallas_call(functools.partial(dispatch_kernel, layout, first), grid=(c...  17.6 us
    dot_general x5, matrix products, dot(): return jnp.dot(a, b, preferred_element_type=F32)  16.8 us
  transfers between devices with their start and end apart: 57, of which 20 were waited for; matrix products, arithmetic and copies ran while one was open for 16% of the time, Pallas kernels for 41%

profile of v5, /device:TPU:0, one launch (start us, length us, event | category | flops | bytes accessed | tf_op | source)
XLA Modules:
  0.0 581.7 jit_solution(13059444356679249657)
XLA Ops:
  26.4 7.6 %dispatch.3 = bf16[2048,768]{1,0:T(8,128)(2,1)} custom-call(s32[1,1024]{1,0:T(1,128)} %reshape_select_fusion.id_ref, bf16[1024,768]{1,0:T(8,128)(2,1)} %x_ref.2), custom_call_target="tpu_custom_call" | custom-call | flops 3221225472 | bytes 6291456 | tf_op jit(solution)/shard_map/dispatch/pallas_call | solution.py:236
  34.1 8.7 %to_send.1 = (bf16[1,768,768]{2,1,0:T(8,128)(2,1)}, bf16[1,768,768]{2,1,0:T(8,128)(2,1)}, bf16[1,768,768]{2,1,0:T(8,128)(2,1)}, bf16[1,768,768]{2,1,0:T(8,128)(2...) custom-call(bf16[4,768,768]{2,1,0:T(8,128)(2,1)} %refs_5_.7, ...), custom_call_target="tpu_custom_call" | custom-call | flops 1 | bytes 1 | tf_op jit(solution)/shard_map/to_send/pallas_call | solution.py:488
  67.1 8.5 %add_convert_fusion.q_ref.k_ref.v_ref = bf16[1024,2432]{1,0:T(8,128)(2,1)} fusion(bf16[1024,768]{1,0:T(8,128)(2,1)S(1)} %fusion.7.x_ref, bf16[768,2432]{1,0:T(8,128)(2,1)} %bitcast.141, f32[2432]{0:T(1024)S(1)} %pad_maximum_fusion.5), kind=kOutput, calls=%fused_computation | convolution fusion | flops 3830185984 | bytes 10298880 | tf_op jit(solution)/shard_map/dot_general | solution.py:24
  79.0 16.5 %attend.1 = (bf16[1024,768]{1,0:T(8,128)(2,1)}, f32[1024,768]{1,0:T(8,128)}) custom-call(bf16[1024,2432]{1,0:T(8,128)(2,1)} %add_convert_fusion.q_ref.k_ref.v_ref, bf16[1024,2432]{1,0:T(8,128)(2,1)} %add_convert_fusion.q_ref.k_ref.v_ref, bf16[1024,2432]{1,0:T(8,128)(2,1)} %add_convert_fusion.q_ref.k_ref.v_ref, s32[1,1024]{1,0:T(1,128)} %row_ref.3, ...), custom_call_target="tpu_custom_call" | custom-call | flops 1 | bytes 1 | tf_op jit(solution)/shard_map/attend/pallas_call | solution.py:141
  102.0 15.0 %collective-permute-done.16.refs_9_ = bf16[1,768,768]{2,1,0:T(8,128)(2,1)} collective-permute-done((bf16[1,768,768]{2,1,0:T(8,128)(2,1)}, bf16[1,768,768]{2,1,0:T(8,128)(2,1)}, u32[]{:S(2)}, u32[]{:S(2)}) %collective-permute-start.16) | collective-permute-done | bytes 1179680 | tf_op jit(solution)/shard_map/ppermute | solution.py:36
  117.0 9.4 %all-to-all-done.refs_3_ = bf16[8,4,64,768]{3,2,1,0:T(8,128)(2,1)} async-done(((bf16[8,4,64,768]{3,2,1,0:T(8,128)(2,1)}), bf16[8,4,64,768]{3,2,1,0:T(8,128)(2,1)}, u32[]{:S(2)}, u32[]{:S(2)}) %all-to-all-start) | async-done | bytes 3145760 | tf_op jit(solution)/shard_map/all_to_all | solution.py:91
  126.4 5.0 dispatch.4
  157.0 5.0 dispatch.5
  192.0 12.5 %collective-permute-done.20.refs_2_ = bf16[8,1,64,768]{3,2,1,0:T(8,128)(2,1)} collective-permute-done((bf16[8,1,64,768]{3,2,1,0:T(8,128)(2,1)}, bf16[8,1,64,768]{3,2,1,0:T(8,128)(2,1)}, u32[]{:S(2)}, u32[]{:S(2)}) %collective-permute-start.20) | collective-permute-done | bytes 786464 | tf_op jit(solution)/shard_map/ppermute | solution.py:36
  205.8 28.4 %expert.4 = (bf16[512,768]{1,0:T(8,128)(2,1)}, bf16[512,768]{1,0:T(8,128)(2,1)}, bf16[512,768]{1,0:T(8,128)(2,1)}, bf16[512,768]{1,0:T(8,128)(2,1)}, bf16[1,1552...) custom-call(s32[1]{0:T(128)} %bitcast.38.refs_0_, ...), custom_call_target="tpu_custom_call" | custom-call | flops 14495514624 | bytes 11796480 | tf_op jit(solution)/shard_map/expert/pallas_call | solution.py:425
  238.7 28.5 %expert.7 = (bf16[512,768]{1,0:T(8,128)(2,1)}, bf16[512,768]{1,0:T(8,128)(2,1)}, bf16[512,768]{1,0:T(8,128)(2,1)}, bf16[512,768]{1,0:T(8,128)(2,1)}, bf16[1,1552...) custom-call(s32[1]{0:T(128)} %bitcast.46.refs_0_, ...), custom_call_target="tpu_custom_call" | custom-call | flops 14495514624 | bytes 11796480 | tf_op jit(solution)/shard_map/expert/pallas_call | solution.py:425
  271.3 16.7 %collective-permute-done.38.refs_1_ = bf16[512,768]{1,0:T(8,128)(2,1)} collective-permute-done((bf16[512,768]{1,0:T(8,128)(2,1)}, bf16[512,768]{1,0:T(8,128)(2,1)}, u32[]{:S(2)}, u32[]{:S(2)}) %collective-permute-start.38) | collective-permute-done | bytes 786464 | tf_op jit(solution)/shard_map/ppermute | solution.py:36
  302.9 28.8 %expert.5 = (bf16[512,768]{1,0:T(8,128)(2,1)}, bf16[512,768]{1,0:T(8,128)(2,1)}, bf16[512,768]{1,0:T(8,128)(2,1)}, bf16[512,768]{1,0:T(8,128)(2,1)}, bf16[1,1552...) custom-call(s32[1]{0:T(128)} %bitcast.44.refs_0_, ...), custom_call_target="tpu_custom_call" | custom-call | flops 14495514624 | bytes 11796480 | tf_op jit(solution)/shard_map/expert/pallas_call | solution.py:425
  331.7 28.7 %expert.6 = (bf16[512,768]{1,0:T(8,128)(2,1)}, bf16[512,768]{1,0:T(8,128)(2,1)}, bf16[512,768]{1,0:T(8,128)(2,1)}, bf16[512,768]{1,0:T(8,128)(2,1)}, bf16[1,1552...) custom-call(s32[1]{0:T(128)} %bitcast.45.refs_0_, ...), custom_call_target="tpu_custom_call" | custom-call | flops 14495514624 | bytes 11796480 | tf_op jit(solution)/shard_map/expert/pallas_call | solution.py:425
  362.9 13.8 %collective-permute-done.32.refs_3_ = bf16[512,768]{1,0:T(8,128)(2,1)S(1)} collective-permute-done((bf16[512,768]{1,0:T(8,128)(2,1)}, bf16[512,768]{1,0:T(8,128)(2,1)S(1)}, u32[]{:S(2)}, u32[]{:S(2)}) %collective-permute-start.32) | collective-permute-done | bytes 786464 | tf_op jit(solution)/shard_map/ppermute | solution.py:36
  389.3 16.6 %collective-permute-done.33.refs_1_ = bf16[512,768]{1,0:T(8,128)(2,1)} collective-permute-done((bf16[512,768]{1,0:T(8,128)(2,1)}, bf16[512,768]{1,0:T(8,128)(2,1)}, u32[]{:S(2)}, u32[]{:S(2)}) %collective-permute-start.33) | collective-permute-done | bytes 786464 | tf_op jit(solution)/shard_map/ppermute | solution.py:36
  407.0 15.4 %collective-permute-done.36.refs_5_ = bf16[512,768]{1,0:T(8,128)(2,1)} collective-permute-done((bf16[512,768]{1,0:T(8,128)(2,1)}, bf16[512,768]{1,0:T(8,128)(2,1)}, u32[]{:S(2)}, u32[]{:S(2)}) %collective-permute-start.36) | collective-permute-done | bytes 786464 | tf_op jit(solution)/shard_map/ppermute | solution.py:36
  429.0 7.1 %combine.2 = f32[1024,768]{1,0:T(8,128)} custom-call(s32[1024,1]{1,0:T(8,128)} %get-tuple-element.209.id_ref, bf16[1024,768]{1,0:T(8,128)(2,1)} %bitcast.47.refs_0_, bf16[1024,768]{1,0:T(8,128)(2,1)} %bitcast.48.refs_1_), custom_call_target="tpu_custom_call" | custom-call | flops 3221225472 | bytes 6291456 | tf_op jit(solution)/shard_map/combine/pallas_call | solution.py:266
  462.6 22.9 %attend_back.1.g_ref = bf16[3,1024,768]{2,1,0:T(8,128)(2,1)} custom-call(bf16[1024,2432]{1,0:T(8,128)(2,1)} %add_convert_fusion.q_ref.k_ref.v_ref, bf16[1024,2432]{1,0:T(8,128)(2,1)} %add_convert_fusion.q_ref.k_ref.v_ref, bf16[1024,2432]{1,0:T(8,128)(2,1)} %add_convert_fusion.q_ref.k_ref.v_ref, bf16[1024,768]{1,0:T(8,128)(2,1)} %convolution_convert_fusion.g_ref, ...), custom_call_target="tpu_custom_call" | custom-call | flops 1 | bytes 1 | tf_op jit(solution)/shard_map/attend_back/pallas_call | solution.py:202
  485.5 10.1 %input_back.1 = (f32[1024,768]{1,0:T(8,128)}, f32[128,768]{1,0:T(8,128)}) custom-call(bf16[3,1024,768]{2,1,0:T(8,128)(2,1)} %attend_back.1.g_ref, bf16[768,2432]{1,0:T(8,128)(2,1)} %bitcast.143, bf16[1024,768]{1,0:T(8,128)(2,1)} %x_ref.3, f32[1024,768]{1,0:T(8,128)} %get-tuple-element.289.dy_ref, f32[1,768]{1,0:T(1,128)} %get-tuple-element.325.gain_ref), custom_call_target="tpu_custom_call" | custom-call | flops 1 | bytes 1 | tf_op jit(solution)/shard_map/input_back/pallas_call | solution.py:574
  495.6 10.1 %outer.1 = bf16[768,3328]{1,0:T(8,128)(2,1)} custom-call(bf16[768,1024]{1,0:T(8,128)(2,1)} %get-tuple-element.170.h_ref, bf16[768,1024]{1,0:T(8,128)(2,1)} %get-tuple-element.245.a_ref, bf16[3,1024,768]{2,1,0:T(8,128)(2,1)} %attend_back.1.g_ref, bf16[1024,768]{1,0:T(8,128)(2,1)} %get-tuple-element.288.b_ref, bf16[768,128]{1,0:T(8,128)(2,1)} %pad.30.rest_ref, ...), custom_call_target="tpu_custom_call" | custom-call | flops 1 | bytes 1 | tf_op jit(solution)/shard_map/outer/pallas_call | solution.py:535
  525.8 8.5 %all-to-all-done.5 = bf16[8,4,64,768]{3,2,1,0:T(8,128)(2,1)} async-done(((bf16[8,4,64,768]{3,2,1,0:T(8,128)(2,1)}), bf16[8,4,64,768]{3,2,1,0:T(8,128)(2,1)}, u32[]{:S(2)}, u32[]{:S(2)}) %all-to-all-start.5) | async-done | bytes 3145760 | tf_op jit(solution)/shard_map/all_to_all | solution.py:91
  534.3 14.0 %finish.1 = (f32[4,768,768]{2,1,0:T(8,128)}, f32[4,768,768]{2,1,0:T(8,128)}, f32[4,16,768]{2,1,0:T(8,128)}) custom-call(bf16[1,1552,768]{2,1,0:T(8,128)(2,1)} %get-tuple-element.248.refs_0_.refs_1_.refs_2_, bf16[1,1552,768]{2,1,0:T(8,128)(2,1)} %get-tuple-element.248.refs_0_.refs_1_.refs_2_, ...), custom_call_target="tpu_custom_call" | custom-call | flops 9535488 | bytes 38141952 | tf_op jit(solution)/shard_map/finish/pallas_call | solution.py:464
  561.2 7.0 %combine.3 = f32[1024,768]{1,0:T(8,128)} custom-call(s32[1024,1]{1,0:T(8,128)} %get-tuple-element.209.id_ref, bf16[2048,768]{1,0:T(8,128)(2,1)} %bitcast.51.refs_0_), custom_call_target="tpu_custom_call" | custom-call | flops 3221225472 | bytes 6291456 | tf_op jit(solution)/shard_map/combine/pallas_call | solution.py:266
  (284 shorter events, 233.5 us)
Async XLA Ops:
  2.2 47.8 %collective-permute-start.11 = (bf16[24,896]{1,0:T(8,128)(2,1)S(1)}, bf16[24,896]{1,0:T(8,128)(2,1)S(1)}, u32[]{:S(2)}, u32[]{:S(2)}) collective-permute-start(bf16[24,896]{1,0:T(8,128)(2,1)S(1)} %pad_maximum_fusion.4), channel_id=1, source_target_pairs={{0,2},{1,3},{2,4},{3,5},{4,6},{5,7},{6,0},{7,1},{8,10},{9,11},{10,... | collective-permute-start | bytes 129032 | tf_op jit(solution)/shard_map/ppermute | solution.py:41
  5.2 44.8 %collective-permute-start.10 = (bf16[24,896]{1,0:T(8,128)(2,1)S(1)}, bf16[24,896]{1,0:T(8,128)(2,1)S(1)}, u32[]{:S(2)}, u32[]{:S(2)}) collective-permute-start(bf16[24,896]{1,0:T(8,128)(2,1)S(1)} %pad_maximum_fusion.4), channel_id=1, source_target_pairs={{0,4},{1,5},{2,6},{3,7},{4,0},{5,1},{6,2},{7,3},{8,12},{9,13},{10,... | collective-permute-start | bytes 129032 | tf_op jit(solution)/shard_map/ppermute | solution.py:41
  50.2 76.2 %all-to-all-start = ((bf16[8,4,64,768]{3,2,1,0:T(8,128)(2,1)}), bf16[8,4,64,768]{3,2,1,0:T(8,128)(2,1)}, u32[]{:S(2)}, u32[]{:S(2)}) async-start(bf16[8,4,64,768]{3,2,1,0:T(8,128)(2,1)} %bitcast.150), calls=%async_computation | async-start | bytes 6291456 | tf_op jit(solution)/shard_map/all_to_all | solution.py:91
  58.4 37.2 %collective-permute-start.7 = (bf16[1,768,768]{2,1,0:T(8,128)(2,1)}, bf16[1,768,768]{2,1,0:T(8,128)(2,1)}, u32[]{:S(2)}, u32[]{:S(2)}) collective-permute-start(bf16[1,768,768]{2,1,0:T(8,128)(2,1)} %get-tuple-element.157), channel_id=1, source_target_pairs={{0,8},{8,0},{16,24},{24,16},{1,9},{9,1},{17,25},{25,17},{2,10},{10... | collective-permute-start | bytes 3538952 | tf_op jit(solution)/shard_map/ppermute | solution.py:36
  59.9 35.7 %collective-permute-start.8 = (bf16[1,768,768]{2,1,0:T(8,128)(2,1)}, bf16[1,768,768]{2,1,0:T(8,128)(2,1)}, u32[]{:S(2)}, u32[]{:S(2)}) collective-permute-start(bf16[1,768,768]{2,1,0:T(8,128)(2,1)} %get-tuple-element.158), channel_id=1, source_target_pairs={{0,16},{8,24},{16,0},{24,8},{1,17},{9,25},{17,1},{25,9},{2,18},{10... | collective-permute-start | bytes 3538952 | tf_op jit(solution)/shard_map/ppermute | solution.py:36
  78.0 39.0 %collective-permute-start.16 = (bf16[1,768,768]{2,1,0:T(8,128)(2,1)}, bf16[1,768,768]{2,1,0:T(8,128)(2,1)}, u32[]{:S(2)}, u32[]{:S(2)}) collective-permute-start(bf16[1,768,768]{2,1,0:T(8,128)(2,1)} %get-tuple-element.167), channel_id=1, source_target_pairs={{0,8},{8,0},{16,24},{24,16},{1,9},{9,1},{17,25},{25,17},{2,10},{10... | collective-permute-start | bytes 3538952 | tf_op jit(solution)/shard_map/ppermute | solution.py:36
  78.5 38.5 %collective-permute-start.17 = (bf16[1,768,768]{2,1,0:T(8,128)(2,1)}, bf16[1,768,768]{2,1,0:T(8,128)(2,1)}, u32[]{:S(2)}, u32[]{:S(2)}) collective-permute-start(bf16[1,768,768]{2,1,0:T(8,128)(2,1)} %get-tuple-element.168), channel_id=1, source_target_pairs={{0,16},{8,24},{16,0},{24,8},{1,17},{9,25},{17,1},{25,9},{2,18},{10... | collective-permute-start | bytes 3538952 | tf_op jit(solution)/shard_map/ppermute | solution.py:36
  131.3 42.7 %all-to-all-start.1 = ((bf16[8,2,64,768]{3,2,1,0:T(8,128)(2,1)}), bf16[8,2,64,768]{3,2,1,0:T(8,128)(2,1)}, u32[]{:S(2)}, u32[]{:S(2)}) async-start(bf16[8,2,64,768]{3,2,1,0:T(8,128)(2,1)} %bitcast.152), calls=%async_computation.1 | async-start | bytes 3145728 | tf_op jit(solution)/shard_map/all_to_all | solution.py:91
  137.4 101.2 %collective-permute-start.31 = (bf16[4,1,768]{2,1,0:T(2,128)(2,1)}, bf16[4,1,768]{2,1,0:T(2,128)(2,1)}, u32[]{:S(2)}, u32[]{:S(2)}) collective-permute-start(bf16[4,1,768]{2,1,0:T(2,128)(2,1)} %copy.97), channel_id=1, source_target_pairs={{0,16},{8,24},{16,0},{24,8},{1,17},{9,25},{17,1},{25,9},{2,18},{10... | collective-permute-start | bytes 18440 | tf_op jit(solution)/shard_map/ppermute | solution.py:36
  138.9 51.0 %collective-permute-start.22 = (bf16[4,1,768]{2,1,0:T(2,128)(2,1)}, bf16[4,1,768]{2,1,0:T(2,128)(2,1)}, u32[]{:S(2)}, u32[]{:S(2)}) collective-permute-start(bf16[4,1,768]{2,1,0:T(2,128)(2,1)} %copy.97), channel_id=1, source_target_pairs={{0,8},{8,0},{16,24},{24,16},{1,9},{9,1},{17,25},{25,17},{2,10},{10... | collective-permute-start | bytes 18440 | tf_op jit(solution)/shard_map/ppermute | solution.py:36
  140.9 95.7 %collective-permute-start.25 = (bf16[1,768,768]{2,1,0:T(8,128)(2,1)}, bf16[1,768,768]{2,1,0:T(8,128)(2,1)}, u32[]{:S(2)}, u32[]{:S(2)}) collective-permute-start(bf16[1,768,768]{2,1,0:T(8,128)(2,1)} %get-tuple-element.183), channel_id=1, source_target_pairs={{0,8},{8,0},{16,24},{24,16},{1,9},{9,1},{17,25},{25,17},{2,10},{10... | collective-permute-start | bytes 3538952 | tf_op jit(solution)/shard_map/ppermute | solution.py:36
  174.0 60.2 %all-to-all-start.2 = ((bf16[8,2,64,768]{3,2,1,0:T(8,128)(2,1)}), bf16[8,2,64,768]{3,2,1,0:T(8,128)(2,1)}, u32[]{:S(2)}, u32[]{:S(2)}) async-start(bf16[8,2,64,768]{3,2,1,0:T(8,128)(2,1)} %bitcast.151), calls=%async_computation.2 | async-start | bytes 3145728 | tf_op jit(solution)/shard_map/all_to_all | solution.py:91
  190.0 48.1 %collective-permute-start.30 = (bf16[1,768,768]{2,1,0:T(8,128)(2,1)}, bf16[1,768,768]{2,1,0:T(8,128)(2,1)}, u32[]{:S(2)}, u32[]{:S(2)}) collective-permute-start(bf16[1,768,768]{2,1,0:T(8,128)(2,1)} %get-tuple-element.189), channel_id=1, source_target_pairs={{0,16},{8,24},{16,0},{24,8},{1,17},{9,25},{17,1},{25,9},{2,18},{10... | collective-permute-start | bytes 3538952 | tf_op jit(solution)/shard_map/ppermute | solution.py:36
  190.5 48.2 %collective-permute-start.34 = (bf16[8,1,64,768]{3,2,1,0:T(8,128)(2,1)}, bf16[8,1,64,768]{3,2,1,0:T(8,128)(2,1)}, u32[]{:S(2)}, u32[]{:S(2)}) collective-permute-start(bf16[8,1,64,768]{3,2,1,0:T(8,128)(2,1)} %get-tuple-element.293), channel_id=1, source_target_pairs={{0,8},{8,0},{16,24},{24,16},{1,9},{9,1},{17,25},{25,17},{2,10},{10... | collective-permute-start | bytes 2359304 | tf_op jit(solution)/shard_map/ppermute | solution.py:36
  270.8 60.9 %collective-permute-start.29 = (bf16[8,1,64,768]{3,2,1,0:T(8,128)(2,1)}, bf16[8,1,64,768]{3,2,1,0:T(8,128)(2,1)}, u32[]{:S(2)}, u32[]{:S(2)}) collective-permute-start(bf16[8,1,64,768]{3,2,1,0:T(8,128)(2,1)} %get-tuple-element.294), channel_id=1, source_target_pairs={{0,8},{8,0},{16,24},{24,16},{1,9},{9,1},{17,25},{25,17},{2,10},{10... | collective-permute-start | bytes 2359304 | tf_op jit(solution)/shard_map/ppermute | solution.py:36
  291.6 89.1 %all-to-all-start.3 = ((bf16[8,2,64,768]{3,2,1,0:T(8,128)(2,1)}), bf16[8,2,64,768]{3,2,1,0:T(8,128)(2,1)}, u32[]{:S(2)}, u32[]{:S(2)}) async-start(bf16[8,2,64,768]{3,2,1,0:T(8,128)(2,1)} %merge.3), calls=%async_computation.3 | async-start | bytes 3145728 | tf_op jit(solution)/shard_map/all_to_all | solution.py:91
  296.5 84.2 %collective-permute-start.40 = (bf16[1,1552,768]{2,1,0:T(8,128)(2,1)}, bf16[1,1552,768]{2,1,0:T(8,128)(2,1)}, u32[]{:S(2)}, u32[]{:S(2)}) collective-permute-start(bf16[1,1552,768]{2,1,0:T(8,128)(2,1)} %get-tuple-element.214), channel_id=1, source_target_pairs={{0,8},{8,0},{16,24},{24,16},{1,9},{9,1},{17,25},{25,17},{2,10},{10... | collective-permute-start | bytes 7151624 | tf_op jit(solution)/shard_map/ppermute | solution.py:36
  298.0 82.7 %collective-permute-start.41 = (bf16[1,1552,768]{2,1,0:T(8,128)(2,1)}, bf16[1,1552,768]{2,1,0:T(8,128)(2,1)}, u32[]{:S(2)}, u32[]{:S(2)}) collective-permute-start(bf16[1,1552,768]{2,1,0:T(8,128)(2,1)} %get-tuple-element.216), channel_id=1, source_target_pairs={{0,16},{8,24},{16,0},{24,8},{1,17},{9,25},{17,1},{25,9},{2,18},{10... | collective-permute-start | bytes 7151624 | tf_op jit(solution)/shard_map/ppermute | solution.py:36
  380.7 48.3 %all-to-all-start.4 = ((bf16[8,2,64,768]{3,2,1,0:T(8,128)(2,1)}), bf16[8,2,64,768]{3,2,1,0:T(8,128)(2,1)}, u32[]{:S(2)}, u32[]{:S(2)}) async-start(bf16[8,2,64,768]{3,2,1,0:T(8,128)(2,1)} %merge.4), calls=%async_computation.4 | async-start | bytes 3145728 | tf_op jit(solution)/shard_map/all_to_all | solution.py:91
  387.2 35.1 %collective-permute-start.36 = (bf16[512,768]{1,0:T(8,128)(2,1)}, bf16[512,768]{1,0:T(8,128)(2,1)}, u32[]{:S(2)}, u32[]{:S(2)}) collective-permute-start(bf16[512,768]{1,0:T(8,128)(2,1)} %get-tuple-element.205), channel_id=1, source_target_pairs={{0,16},{8,24},{16,0},{24,8},{1,17},{9,25},{17,1},{25,9},{2,18},{10... | collective-permute-start | bytes 2359304 | tf_op jit(solution)/shard_map/ppermute | solution.py:36
  388.2 34.7 %collective-permute-start.37 = (bf16[512,768]{1,0:T(8,128)(2,1)}, bf16[512,768]{1,0:T(8,128)(2,1)}, u32[]{:S(2)}, u32[]{:S(2)}) collective-permute-start(bf16[512,768]{1,0:T(8,128)(2,1)} %get-tuple-element.208), channel_id=1, source_target_pairs={{0,8},{8,0},{16,24},{24,16},{1,9},{9,1},{17,25},{25,17},{2,10},{10... | collective-permute-start | bytes 2359304 | tf_op jit(solution)/shard_map/ppermute | solution.py:36
  422.9 62.6 %collective-permute-start.42 = (bf16[1,1552,768]{2,1,0:T(8,128)(2,1)}, bf16[1,1552,768]{2,1,0:T(8,128)(2,1)}, u32[]{:S(2)}, u32[]{:S(2)}) collective-permute-start(bf16[1,1552,768]{2,1,0:T(8,128)(2,1)} %get-tuple-element.238), channel_id=1, source_target_pairs={{0,8},{8,0},{16,24},{24,16},{1,9},{9,1},{17,25},{25,17},{2,10},{10... | collective-permute-start | bytes 7151624 | tf_op jit(solution)/shard_map/ppermute | solution.py:36
  423.9 61.7 %collective-permute-start.43 = (bf16[1,1552,768]{2,1,0:T(8,128)(2,1)}, bf16[1,1552,768]{2,1,0:T(8,128)(2,1)}, u32[]{:S(2)}, u32[]{:S(2)}) collective-permute-start(bf16[1,1552,768]{2,1,0:T(8,128)(2,1)} %get-tuple-element.240), channel_id=1, source_target_pairs={{0,16},{8,24},{16,0},{24,8},{1,17},{9,25},{17,1},{25,9},{2,18},{10... | collective-permute-start | bytes 7151624 | tf_op jit(solution)/shard_map/ppermute | solution.py:36
  457.9 76.4 %all-to-all-start.5 = ((bf16[8,4,64,768]{3,2,1,0:T(8,128)(2,1)}), bf16[8,4,64,768]{3,2,1,0:T(8,128)(2,1)}, u32[]{:S(2)}, u32[]{:S(2)}) async-start(bf16[8,4,64,768]{3,2,1,0:T(8,128)(2,1)} %merge.5), calls=%async_computation.5 | async-start | bytes 6291456 | tf_op jit(solution)/shard_map/all_to_all | solution.py:91
  (63 other events, 852.9 us)
